TPU v7x, 512 devices: a whole 4x8x8 slice. The times are simulated.
512 devices in a mesh: gz: 64 (over z_lo, y, x), gy: 8 (over z_hi, core).
Axes of the slice: x: 4, y: 8, z: 8 (z_hi: 4, z_lo: 2; z = z_hi * 2 + z_lo), core: 2. Of those that a mesh axis runs over, the one named last changes fastest.
Arguments:
- features: bfloat16 [16, 256, 64, 128], P(None, 'gz', 'gy'), may hold values from -16 to 16
- field: float32 [256, 64, 128], P('gz', 'gy'), may hold values from -6 to 6
- velocity: float32 [3, 256, 64, 128], P(None, 'gz', 'gy'), may hold values from -3 to 3
- weight: bfloat16 [16, 432], replicated, may hold values from -0.3125 to 0.3125
- cotangent: float32 [256, 64, 128], P('gz', 'gy'), may hold values from -12 to 12
Outputs:
- grad_field: float32 [256, 64, 128], P('gz', 'gy')
- grad_features: bfloat16 [16, 256, 64, 128], P(None, 'gz', 'gy')
- grad_weight: float32 [16, 432], replicated
- factor_patch: float32 [432, 432], replicated
- factor_grad: float32 [16, 16], replicated
All inputs are finite; a program needn't handle non-finite values.
Results may differ from a plain program's by a relative error of at most 0.0049.
Values may be sent and summed in bfloat16 or wider, within the bound.
No kernel may reach another device: no remote copies, remote signals or barrier semaphores. Data moves between devices by JAX's collectives and lax.ppermute only.
A program may use at most 64 MiB of HBM per device.

v0:
```python
import math

import jax
import jax.numpy as jnp
from jax import lax
from jax.sharding import PartitionSpec as P

STEPS = 2


step_size = 0.15
face_weights = (2.0 / 60.0, -13.0 / 60.0, 47.0 / 60.0, 27.0 / 60.0, -3.0 / 60.0)
contract_cells = (((1,), (1,)), ((), ()))


def extended(value, sides, width):
    for axis, dim in sides:
        peers, length = (lax.axis_size(axis), value.shape[dim])
        up = [(i, (i + 1) % peers) for i in range(peers)]
        down = [(j, i) for i, j in up]
        last = lax.slice_in_dim(value, length - width, length, axis=dim)
        first = lax.slice_in_dim(value, 0, width, axis=dim)
        before = lax.ppermute(last, axis, up)
        after = lax.ppermute(first, axis, down)
        value = jnp.concatenate([before, value, after], axis=dim)
    return value


def wrap_x(values):
    return jnp.concatenate([values[..., -1:], values, values[..., :1]], axis=-1)


def interior(values):
    return values[3:-3, 3:-3]


def patch_plane(source, z_center, y_start, y_cells, mirror):
    channels = source.shape[0]
    x_cells = source.shape[-1] - 2
    z_slab = lax.dynamic_slice_in_dim(source, z_center - 1, 3, 1)
    pieces = []
    for shift_z in (-1, 0, 1):
        z_layer = z_slab[:, 1 + mirror * shift_z]
        for shift_y in (-1, 0, 1):
            y_band = lax.dynamic_slice_in_dim(z_layer, y_start + mirror * shift_y, y_cells, 1)
            for shift_x in (-1, 0, 1):
                first = 1 + mirror * shift_x
                pieces.append(y_band[:, :, first : first + x_cells])
    return jnp.stack(pieces, axis=1).reshape(channels * 27, y_cells * x_cells)


def convolve(weight, source, z_first, z_count, y_start, y_cells):
    x_cells = source.shape[-1] - 2
    outputs = weight.shape[0]
    patch_size = weight.shape[1]

    def one_plane(position, state):
        coefficients, patch_gram = state
        patch_block = patch_plane(source, z_first + position, y_start, y_cells, 1)
        out_plane = jnp.dot(weight, patch_block, preferred_element_type=jnp.float32).reshape(
            outputs, 1, y_cells, x_cells
        )
        coefficients = lax.dynamic_update_slice_in_dim(coefficients, out_plane, position, 1)
        patch_gram = patch_gram + lax.dot_general(
            patch_block, patch_block, contract_cells, preferred_element_type=jnp.float32
        )
        return (coefficients, patch_gram)

    start_coef = jnp.zeros((outputs, z_count, y_cells, x_cells), jnp.float32)
    start_gram = jnp.zeros((patch_size, patch_size), jnp.float32)
    return lax.fori_loop(0, z_count, one_plane, (start_coef, start_gram))


def advance_full(field_now, coefficients, velocities):
    updated = field_now * (1.0 + step_size * coefficients[15])
    for direction in range(3):
        face_flux = jnp.zeros_like(field_now)
        for offset in range(-2, 3):
            weights_face = face_weights[offset + 2] + coefficients[direction * 5 + offset + 2]
            face_flux = face_flux + weights_face * jnp.roll(field_now, -offset, direction)
        face_flux = velocities[direction] * face_flux
        updated = updated - step_size * (face_flux - jnp.roll(face_flux, 1, direction))
    return updated


def retreat_full(adjoint_now, field_now, coefficients, velocities):
    earlier = adjoint_now * (1.0 + step_size * coefficients[15])
    grads = []
    for direction in range(3):
        face_drive = (
            -step_size
            * (adjoint_now - jnp.roll(adjoint_now, -1, direction))
            * velocities[direction]
        )
        for offset in range(-2, 3):
            weights_face = face_weights[offset + 2] + coefficients[direction * 5 + offset + 2]
            earlier = earlier + jnp.roll(face_drive * weights_face, offset, direction)
            grads.append(face_drive * jnp.roll(field_now, -offset, direction))
    grads.append(step_size * adjoint_now * field_now)
    return (earlier, grads)


def body(features, field, velocity, weight, cotangent):
    channels, z_cells, y_cells, x_cells = features.shape
    outputs = weight.shape[0]
    cell_count = float(z_cells * y_cells * x_cells * lax.axis_size("gz") * lax.axis_size("gy"))
    patch_sum = None
    factor_patch = None
    feature_pad = extended(features, (("gz", 1), ("gy", 2)), 1)
    source = wrap_x(feature_pad)
    margin = 1
    coefficients, patch_sum = convolve(weight, source, 1, z_cells, 1, y_cells)
    stacked = extended(jnp.concatenate([coefficients, velocity], axis=0), (("gz", 1), ("gy", 2)), 3)
    coef_pad = stacked[:outputs]
    vel_pad = stacked[outputs:]
    field_pads = []
    current = field
    for step_index in range(STEPS):
        padded = extended(current, (("gz", 0), ("gy", 1)), 3)
        field_pads.append(padded)
        if step_index + 1 < STEPS:
            current = interior(advance_full(padded, coef_pad, vel_pad))
    adjoint = cotangent
    grad_total = None
    for step_index in reversed(range(STEPS)):
        adjoint_pad = extended(adjoint, (("gz", 0), ("gy", 1)), 3)
        earlier, grads = retreat_full(adjoint_pad, field_pads[step_index], coef_pad, vel_pad)
        adjoint = interior(earlier)
        stacked_grads = jnp.stack([interior(values) for values in grads])
        grad_total = stacked_grads if grad_total is None else grad_total + stacked_grads
    grad_bf = grad_total.astype(jnp.bfloat16)
    grad_pad = wrap_x(extended(grad_bf, (("gz", 1), ("gy", 2)), 1))
    flipped = (
        weight.reshape(outputs, channels, 27).transpose(1, 0, 2).reshape(channels, outputs * 27)
    )
    patch_size = weight.shape[1]

    def finish_plane(position, state):
        grad_feat, grad_w, patch_gram = state
        back_block = patch_plane(grad_pad, 1 + position, 1, y_cells, -1)
        out_plane = jnp.dot(flipped, back_block, preferred_element_type=jnp.float32).astype(
            jnp.bfloat16
        )
        grad_feat = lax.dynamic_update_slice_in_dim(
            grad_feat, out_plane.reshape(channels, 1, y_cells, x_cells), position, 1
        )
        patch_block = patch_plane(source, margin + position, margin, y_cells, 1)
        local_part = lax.dynamic_index_in_dim(grad_bf, position, 1, keepdims=False).reshape(
            outputs, y_cells * x_cells
        )
        grad_w = grad_w + lax.dot_general(
            local_part, patch_block, contract_cells, preferred_element_type=jnp.float32
        )
        return (grad_feat, grad_w, patch_gram)

    start_state = (
        jnp.zeros((channels, z_cells, y_cells, x_cells), jnp.bfloat16),
        jnp.zeros((outputs, patch_size), jnp.float32),
        jnp.zeros((patch_size, patch_size), jnp.float32),
    )
    grad_features, grad_w, patch_gram = lax.fori_loop(0, z_cells, finish_plane, start_state)
    grad_flat = grad_bf.reshape(outputs, -1)
    local_grad = (
        lax.dot_general(grad_flat, grad_flat, contract_cells, preferred_element_type=jnp.float32)
        / cell_count
    )
    local_weight = grad_w / math.sqrt(cell_count)
    factor_patch, factor_grad, grad_weight = lax.psum(
        (patch_sum / cell_count, local_grad, local_weight), ("gz", "gy")
    )
    return (adjoint, grad_features, grad_weight, factor_patch, factor_grad)


def solution(mesh):
    placed = (
        P(None, "gz", "gy", None),
        P("gz", "gy", None),
        P(None, "gz", "gy", None),
        P(),
        P("gz", "gy", None),
    )
    return jax.shard_map(
        body,
        mesh=mesh,
        in_specs=placed,
        out_specs=(P("gz", "gy", None), P(None, "gz", "gy", None), P(), P(), P()),
        check_vma=False,
    )
```

profile of v0, /device:TPU:1, one launch (start us, length us, event | category | flops | bytes accessed | tf_op | source)
XLA Modules:
  0.0 401.1 jit_solution(16501712285129159659)
XLA Ops:
  8.0 3.9 collective-permute-start.4
  12.0 7.9 %collective-permute-start.5 = (bf16[16,1,8,128]{3,2,0,1:T(8,128)(2,1)S(1)}, bf16[16,1,8,128]{3,2,0,1:T(8,128)(2,1)S(1)}, u32[]{:S(2)}, u32[]{:S(2)}) collective-permute-start(bf16[16,1,8,128]{3,2,0,1:T(8,128)(2,1)S(1)} %copy.73), channel_id=1, source_target_pairs={{8,0},{16,8},{24,16},{32,24},{40,32},{48,40},{56,48},{64,56},{72,6... | collective-permute-start | bytes 98312 | tf_op jit(solution)/shard_map/ppermute | solution.py:24
  20.7 2.0 collective-permute-start.16
  23.5 1.9 collective-permute-start
  25.4 7.6 %collective-permute-start.1 = (f32[3,8,128]{2,1,0:T(8,128)S(1)}, f32[3,8,128]{2,1,0:T(8,128)S(1)}, u32[]{:S(2)}, u32[]{:S(2)}) collective-permute-start(f32[3,8,128]{2,1,0:T(8,128)S(1)} %get-tuple-element.618), channel_id=1, source_target_pairs={{8,0},{16,8},{24,16},{32,24},{40,32},{48,40},{56,48},{64,56},{72,6... | collective-permute-start | bytes 36872 | tf_op jit(solution)/shard_map/ppermute | solution.py:24
  34.1 3.4 collective-permute-start.17
  39.3 8.7 %collective-permute-start.19 = (f32[10,3,128]{2,1,0:T(4,128)S(1)}, f32[10,3,128]{2,1,0:T(4,128)S(1)}, u32[]{:S(2)}, u32[]{:S(2)}) collective-permute-start(f32[10,3,128]{2,1,0:T(4,128)S(1)} %get-tuple-element.611), channel_id=1, source_target_pairs={{1,0},{2,1},{3,2},{4,3},{5,4},{6,5},{7,6},{0,7},{9,8},{10,9},{11,1... | collective-permute-start | bytes 46088 | tf_op jit(solution)/shard_map/ppermute | solution.py:24
  48.0 1.9 collective-permute-start.18
  50.5 3.3 collective-permute-start.3
  53.9 3.1 collective-permute-start.2
  59.6 4.6 %collective-permute-start.7 = (bf16[16,6,1,128]{3,2,0,1:T(2,128)(2,1)S(1)}, bf16[16,6,1,128]{3,2,0,1:T(2,128)(2,1)S(1)}, u32[]{:S(2)}, u32[]{:S(2)}) collective-permute-start(bf16[16,6,1,128]{3,2,0,1:T(2,128)(2,1)S(1)} %get-tuple-element.559), channel_id=1, source_target_pairs={{1,0},{2,1},{3,2},{4,3},{5,4},{6,5},{7,6},{0,7},{9,8},{10,9},{11,1... | collective-permute-start | bytes 73736 | tf_op jit(solution)/shard_map/ppermute | solution.py:24
  64.2 1.9 collective-permute-start.6
  66.7 3.9 collective-permute-done.6
  71.9 15.7 %while.40 = (s32[]{:T(128)}, f32[16,4,8,128]{3,2,1,0:T(8,128)}, f32[432,432]{1,0:T(8,128)S(1)}, bf16[16,6,10,130]{3,2,0,1:T(8,128)(2,1)S(1)}, bf16[16,432]{1,0:T...) while((s32[]{:T(128)}, f32[16,4,8,128]{3,2,1,0:T(8,128)}, f32[432,432]{1,0:T(8,128)S(1)}, ...), condition=%wide.region_1.0_spmd.clone, body=%wide.region_0.0_spmd.clone.sunk | while | flops 396734976 | bytes 7392663 | solution.py:71
  87.7 1.0 constant_dynamic-update-slice_fusion.88
  89.5 7.6 %collective-permute-start.9 = (f32[19,3,8,128]{3,2,1,0:T(8,128)S(1)}, f32[19,3,8,128]{3,2,1,0:T(8,128)S(1)}, u32[]{:S(2)}, u32[]{:S(2)}) collective-permute-start(f32[19,3,8,128]{3,2,1,0:T(8,128)S(1)} %get-tuple-element.555), channel_id=1, source_target_pairs={{8,0},{16,8},{24,16},{32,24},{40,32},{48,40},{56,48},{64,56},{72,6... | collective-permute-start | bytes 700424 | tf_op jit(solution)/shard_map/ppermute | solution.py:24
  97.1 1.9 collective-permute-start.8
  100.3 9.7 %collective-permute-done.8 = f32[19,3,8,128]{3,2,1,0:T(8,128)S(1)} collective-permute-done((f32[19,3,8,128]{3,2,1,0:T(8,128)S(1)}, f32[19,3,8,128]{3,2,1,0:T(8,128)S(1)}, u32[]{:S(2)}, u32[]{:S(2)}) %collective-permute-start.8) | collective-permute-done | bytes 233504 | tf_op jit(solution)/shard_map/ppermute | solution.py:23
  110.0 1.0 fusion.194
  111.0 7.4 %collective-permute-start.11 = (f32[19,10,3,128]{3,2,1,0:T(4,128)}, f32[19,10,3,128]{3,2,1,0:T(4,128)}, u32[]{:S(2)}, u32[]{:S(2)}) collective-permute-start(f32[19,10,3,128]{3,2,1,0:T(4,128)} %get-tuple-element.549), channel_id=1, source_target_pairs={{1,0},{2,1},{3,2},{4,3},{5,4},{6,5},{7,6},{0,7},{9,8},{10,9},{11,1... | collective-permute-start | bytes 875528 | tf_op jit(solution)/shard_map/ppermute | solution.py:24
  118.4 1.9 collective-permute-start.10
  123.1 1.3 slice.2373
  125.6 1.0 broadcast_multiply_fusion
  126.7 2.3 collective-permute-done.10
  128.9 1.4 pad_maximum_fusion
  132.7 1.1 fusion.63
  133.9 2.1 collective-permute-start.13
  136.0 3.4 collective-permute-start.12
  139.7 4.9 %collective-permute-done.12 = f32[3,8,128]{2,1,0:T(8,128)S(1)} collective-permute-done((f32[3,8,128]{2,1,0:T(8,128)S(1)}, f32[3,8,128]{2,1,0:T(8,128)S(1)}, u32[]{:S(2)}, u32[]{:S(2)}) %collective-permute-start.12) | collective-permute-done | bytes 12320 | tf_op jit(solution)/shard_map/ppermute | solution.py:23
  144.7 6.4 %collective-permute-start.14 = (f32[10,3,128]{2,1,0:T(4,128)S(1)}, f32[10,3,128]{2,1,0:T(4,128)S(1)}, u32[]{:S(2)}, u32[]{:S(2)}) collective-permute-start(f32[10,3,128]{2,1,0:T(4,128)S(1)} %get-tuple-element.613), channel_id=1, source_target_pairs={{0,1},{1,2},{2,3},{3,4},{4,5},{5,6},{6,7},{7,0},{8,9},{9,10},{10,1... | collective-permute-start | bytes 46088 | tf_op jit(solution)/shard_map/ppermute | solution.py:23
  151.1 2.6 collective-permute-start.15
  154.0 3.5 collective-permute-done.15
  158.2 1.9 collective-permute-start.21
  160.1 3.4 collective-permute-start.20
  164.1 4.7 %collective-permute-done.20 = f32[3,8,128]{2,1,0:T(8,128)S(1)} collective-permute-done((f32[3,8,128]{2,1,0:T(8,128)S(1)}, f32[3,8,128]{2,1,0:T(8,128)S(1)}, u32[]{:S(2)}, u32[]{:S(2)}) %collective-permute-start.20) | collective-permute-done | bytes 12320 | tf_op jit(solution)/shard_map/ppermute | solution.py:23
  168.8 4.5 %collective-permute-start.23 = (f32[10,3,128]{2,1,0:T(4,128)S(1)}, f32[10,3,128]{2,1,0:T(4,128)S(1)}, u32[]{:S(2)}, u32[]{:S(2)}) collective-permute-start(f32[10,3,128]{2,1,0:T(4,128)S(1)} %get-tuple-element.609), channel_id=1, source_target_pairs={{1,0},{2,1},{3,2},{4,3},{5,4},{6,5},{7,6},{0,7},{9,8},{10,9},{11,1... | collective-permute-start | bytes 46088 | tf_op jit(solution)/shard_map/ppermute | solution.py:24
  173.4 1.9 collective-permute-start.22
  175.7 3.0 collective-permute-done.22
  179.8 1.9 collective-permute-start.25
  181.7 3.4 collective-permute-start.24
  185.8 4.9 %collective-permute-done.24 = bf16[16,1,8,128]{3,2,1,0:T(8,128)(2,1)S(1)} collective-permute-done((bf16[16,1,8,128]{3,2,1,0:T(8,128)(2,1)S(1)}, bf16[16,1,8,128]{3,2,1,0:T(8,128)(2,1)S(1)}, u32[]{:S(2)}, u32[]{:S(2)}) %collective-permute-start.24) | collective-permute-done | bytes 32800 | tf_op jit(solution)/shard_map/ppermute | solution.py:23
  190.8 7.6 %collective-permute-start.27 = (bf16[16,6,1,128]{3,2,1,0:T(2,128)(2,1)S(1)}, bf16[16,6,1,128]{3,2,1,0:T(2,128)(2,1)S(1)}, u32[]{:S(2)}, u32[]{:S(2)}) collective-permute-start(bf16[16,6,1,128]{3,2,1,0:T(2,128)(2,1)S(1)} %get-tuple-element.557), channel_id=1, source_target_pairs={{1,0},{2,1},{3,2},{4,3},{5,4},{6,5},{7,6},{0,7},{9,8},{10,9},{11,1... | collective-permute-start | bytes 73736 | tf_op jit(solution)/shard_map/ppermute | solution.py:24
  198.4 2.1 collective-permute-start.26
  202.0 0.9 pad_maximum_fusion.2
  202.9 20.6 %while.41 = (s32[]{:T(128)}, bf16[16,4,8,128]{3,2,1,0:T(8,128)(2,1)S(1)}, f32[16,432]{1,0:T(8,128)S(1)}, bf16[16,6,10,130]{3,2,1,0:T(8,128)(2,1)S(1)}, bf16[16,4...) while((s32[]{:T(128)}, ...), condition=%wide.region_3.4_spmd.clone, body=%wide.region_2.3_spmd.clone.sunk | while | flops 28341764 | bytes 9678003 | solution.py:161
  223.5 99.2 %all-reduce = (f32[16,432]{1,0:T(8,128)}, f32[16,16]{1,0:T(8,128)}) all-reduce(f32[16,432]{1,0:T(8,128)S(1)} %broadcast_multiply_fusion.1, f32[16,16]{1,0:T(8,128)S(1)} %fusion.11), channel_id=1, replica_groups=mesh['gz'=64,'gy'=8] {'gz','gy'}, use_global_device_ids=true, to_apply=%region_4.5 | all-reduce | flops 7168 | bytes 57344 | tf_op jit(solution)/shard_map/psum | solution.py:168
  322.7 69.5 %all-reduce.3.cloned.1.call-done = f32[432,432]{1,0:T(8,128)} async-done(((f32[432,432]{1,0:T(8,128)}), f32[432,432]{1,0:T(8,128)}) %all-reduce.3.cloned.1.call-update) | async-done | bytes 746512 | tf_op jit(solution)/shard_map/psum | solution.py:168
  392.2 2.1 copy.231
  (615 shorter events, 59.0 us)
Async XLA Ops:
  7.2 385.0 %all-reduce.3.cloned.1.call-start = ((), (), s32[]{:S(2)}) async-start(), calls=%async_computation | async-start | bytes 1769472 | tf_op jit(solution)/shard_map/psum | solution.py:168
  8.0 51.4 %collective-permute-start.4 = (bf16[16,1,8,128]{3,2,0,1:T(8,128)(2,1)S(1)}, bf16[16,1,8,128]{3,2,0,1:T(8,128)(2,1)S(1)}, u32[]{:S(2)}, u32[]{:S(2)}) collective-permute-start(bf16[16,1,8,128]{3,2,0,1:T(8,128)(2,1)S(1)} %copy.72), channel_id=1, source_target_pairs={{0,8},{8,16},{16,24},{24,32},{32,40},{40,48},{48,56},{56,64},{64,7... | collective-permute-start | bytes 98312 | tf_op jit(solution)/shard_map/ppermute | solution.py:23
  12.0 47.5 %collective-permute-start.5 = (bf16[16,1,8,128]{3,2,0,1:T(8,128)(2,1)S(1)}, bf16[16,1,8,128]{3,2,0,1:T(8,128)(2,1)S(1)}, u32[]{:S(2)}, u32[]{:S(2)}) collective-permute-start(bf16[16,1,8,128]{3,2,0,1:T(8,128)(2,1)S(1)} %copy.73), channel_id=1, source_target_pairs={{8,0},{16,8},{24,16},{32,24},{40,32},{48,40},{56,48},{64,56},{72,6... | collective-permute-start | bytes 98312 | tf_op jit(solution)/shard_map/ppermute | solution.py:24
  20.7 38.8 %copy-start.11 = (bf16[16,4,8,128]{3,2,1,0:T(8,128)(2,1)S(1)}, bf16[16,4,8,128]{3,2,1,0:T(8,128)(2,1)}, u32[]{:S(2)}) copy-start(bf16[16,4,8,128]{3,2,1,0:T(8,128)(2,1)} %param.9) | copy-start | bytes 393220
  20.7 13.4 %collective-permute-start.16 = (f32[3,8,128]{2,1,0:T(8,128)S(1)}, f32[3,8,128]{2,1,0:T(8,128)S(1)}, u32[]{:S(2)}, u32[]{:S(2)}) collective-permute-start(f32[3,8,128]{2,1,0:T(8,128)S(1)} %get-tuple-element.617), channel_id=1, source_target_pairs={{0,8},{8,16},{16,24},{24,32},{32,40},{40,48},{48,56},{56,64},{64,7... | collective-permute-start | bytes 36872 | tf_op jit(solution)/shard_map/ppermute | solution.py:23
  23.5 15.0 %collective-permute-start = (f32[3,8,128]{2,1,0:T(8,128)S(1)}, f32[3,8,128]{2,1,0:T(8,128)S(1)}, u32[]{:S(2)}, u32[]{:S(2)}) collective-permute-start(f32[3,8,128]{2,1,0:T(8,128)S(1)} %get-tuple-element.619), channel_id=1, source_target_pairs={{0,8},{8,16},{16,24},{24,32},{32,40},{40,48},{48,56},{56,64},{64,7... | collective-permute-start | bytes 36872 | tf_op jit(solution)/shard_map/ppermute | solution.py:23
  25.4 24.5 %collective-permute-start.1 = (f32[3,8,128]{2,1,0:T(8,128)S(1)}, f32[3,8,128]{2,1,0:T(8,128)S(1)}, u32[]{:S(2)}, u32[]{:S(2)}) collective-permute-start(f32[3,8,128]{2,1,0:T(8,128)S(1)} %get-tuple-element.618), channel_id=1, source_target_pairs={{8,0},{16,8},{24,16},{32,24},{40,32},{48,40},{56,48},{64,56},{72,6... | collective-permute-start | bytes 36872 | tf_op jit(solution)/shard_map/ppermute | solution.py:24
  34.1 4.4 %collective-permute-start.17 = (f32[3,8,128]{2,1,0:T(8,128)S(1)}, f32[3,8,128]{2,1,0:T(8,128)S(1)}, u32[]{:S(2)}, u32[]{:S(2)}) collective-permute-start(f32[3,8,128]{2,1,0:T(8,128)S(1)} %get-tuple-element.616), channel_id=1, source_target_pairs={{8,0},{16,8},{24,16},{32,24},{40,32},{48,40},{56,48},{64,56},{72,6... | collective-permute-start | bytes 36872 | tf_op jit(solution)/shard_map/ppermute | solution.py:24
  39.3 14.6 %collective-permute-start.19 = (f32[10,3,128]{2,1,0:T(4,128)S(1)}, f32[10,3,128]{2,1,0:T(4,128)S(1)}, u32[]{:S(2)}, u32[]{:S(2)}) collective-permute-start(f32[10,3,128]{2,1,0:T(4,128)S(1)} %get-tuple-element.611), channel_id=1, source_target_pairs={{1,0},{2,1},{3,2},{4,3},{5,4},{6,5},{7,6},{0,7},{9,8},{10,9},{11,1... | collective-permute-start | bytes 46088 | tf_op jit(solution)/shard_map/ppermute | solution.py:24
  48.0 9.1 %collective-permute-start.18 = (f32[10,3,128]{2,1,0:T(4,128)S(1)}, f32[10,3,128]{2,1,0:T(4,128)S(1)}, u32[]{:S(2)}, u32[]{:S(2)}) collective-permute-start(f32[10,3,128]{2,1,0:T(4,128)S(1)} %get-tuple-element.610), channel_id=1, source_target_pairs={{0,1},{1,2},{2,3},{3,4},{4,5},{5,6},{6,7},{7,0},{8,9},{9,10},{10,1... | collective-permute-start | bytes 46088 | tf_op jit(solution)/shard_map/ppermute | solution.py:23
  50.5 69.8 %collective-permute-start.3 = (f32[10,3,128]{2,1,0:T(4,128)}, f32[10,3,128]{2,1,0:T(4,128)}, u32[]{:S(2)}, u32[]{:S(2)}) collective-permute-start(f32[10,3,128]{2,1,0:T(4,128)} %get-tuple-element.615), channel_id=1, source_target_pairs={{1,0},{2,1},{3,2},{4,3},{5,4},{6,5},{7,6},{0,7},{9,8},{10,9},{11,1... | collective-permute-start | bytes 46088 | tf_op jit(solution)/shard_map/ppermute | solution.py:24
  53.9 66.5 %collective-permute-start.2 = (f32[10,3,128]{2,1,0:T(4,128)}, f32[10,3,128]{2,1,0:T(4,128)}, u32[]{:S(2)}, u32[]{:S(2)}) collective-permute-start(f32[10,3,128]{2,1,0:T(4,128)} %get-tuple-element.614), channel_id=1, source_target_pairs={{0,1},{1,2},{2,3},{3,4},{4,5},{5,6},{6,7},{7,0},{8,9},{9,10},{10,1... | collective-permute-start | bytes 46088 | tf_op jit(solution)/shard_map/ppermute | solution.py:23
  59.6 7.1 %collective-permute-start.7 = (bf16[16,6,1,128]{3,2,0,1:T(2,128)(2,1)S(1)}, bf16[16,6,1,128]{3,2,0,1:T(2,128)(2,1)S(1)}, u32[]{:S(2)}, u32[]{:S(2)}) collective-permute-start(bf16[16,6,1,128]{3,2,0,1:T(2,128)(2,1)S(1)} %get-tuple-element.559), channel_id=1, source_target_pairs={{1,0},{2,1},{3,2},{4,3},{5,4},{6,5},{7,6},{0,7},{9,8},{10,9},{11,1... | collective-permute-start | bytes 73736 | tf_op jit(solution)/shard_map/ppermute | solution.py:24
  64.2 6.5 %collective-permute-start.6 = (bf16[16,6,1,128]{3,2,0,1:T(2,128)(2,1)S(1)}, bf16[16,6,1,128]{3,2,0,1:T(2,128)(2,1)S(1)}, u32[]{:S(2)}, u32[]{:S(2)}) collective-permute-start(bf16[16,6,1,128]{3,2,0,1:T(2,128)(2,1)S(1)} %get-tuple-element.558), channel_id=1, source_target_pairs={{0,1},{1,2},{2,3},{3,4},{4,5},{5,6},{6,7},{7,0},{8,9},{9,10},{10,1... | collective-permute-start | bytes 73736 | tf_op jit(solution)/shard_map/ppermute | solution.py:23
  89.5 10.8 %collective-permute-start.9 = (f32[19,3,8,128]{3,2,1,0:T(8,128)S(1)}, f32[19,3,8,128]{3,2,1,0:T(8,128)S(1)}, u32[]{:S(2)}, u32[]{:S(2)}) collective-permute-start(f32[19,3,8,128]{3,2,1,0:T(8,128)S(1)} %get-tuple-element.555), channel_id=1, source_target_pairs={{8,0},{16,8},{24,16},{32,24},{40,32},{48,40},{56,48},{64,56},{72,6... | collective-permute-start | bytes 700424 | tf_op jit(solution)/shard_map/ppermute | solution.py:24
  97.1 12.9 %collective-permute-start.8 = (f32[19,3,8,128]{3,2,1,0:T(8,128)S(1)}, f32[19,3,8,128]{3,2,1,0:T(8,128)S(1)}, u32[]{:S(2)}, u32[]{:S(2)}) collective-permute-start(f32[19,3,8,128]{3,2,1,0:T(8,128)S(1)} %get-tuple-element.554), channel_id=1, source_target_pairs={{0,8},{8,16},{16,24},{24,32},{32,40},{40,48},{48,56},{56,64},{64,7... | collective-permute-start | bytes 700424 | tf_op jit(solution)/shard_map/ppermute | solution.py:23
  111.0 15.7 %collective-permute-start.11 = (f32[19,10,3,128]{3,2,1,0:T(4,128)}, f32[19,10,3,128]{3,2,1,0:T(4,128)}, u32[]{:S(2)}, u32[]{:S(2)}) collective-permute-start(f32[19,10,3,128]{3,2,1,0:T(4,128)} %get-tuple-element.549), channel_id=1, source_target_pairs={{1,0},{2,1},{3,2},{4,3},{5,4},{6,5},{7,6},{0,7},{9,8},{10,9},{11,1... | collective-permute-start | bytes 875528 | tf_op jit(solution)/shard_map/ppermute | solution.py:24
  118.4 10.5 %collective-permute-start.10 = (f32[19,10,3,128]{3,2,1,0:T(4,128)}, f32[19,10,3,128]{3,2,1,0:T(4,128)}, u32[]{:S(2)}, u32[]{:S(2)}) collective-permute-start(f32[19,10,3,128]{3,2,1,0:T(4,128)} %get-tuple-element.548), channel_id=1, source_target_pairs={{0,1},{1,2},{2,3},{3,4},{4,5},{5,6},{6,7},{7,0},{8,9},{9,10},{10,1... | collective-permute-start | bytes 875528 | tf_op jit(solution)/shard_map/ppermute | solution.py:23
  126.6 3.7 copy-start.9
  126.6 3.7 copy-start.18
  126.6 4.6 %copy-start.10 = (f32[9,14,128]{2,1,0:T(8,128)S(1)}, f32[9,14,128]{2,1,0:T(8,128)}, u32[]{:S(2)}) copy-start(f32[9,14,128]{2,1,0:T(8,128)} %slice.2356) | copy-start | bytes 193540
  126.7 4.6 %copy-start.17 = (f32[1,14,128]{2,1,0:T(8,128)S(1)}, f32[1,14,128]{2,1,0:T(8,128)}, u32[]{:S(2)}) copy-start(f32[1,14,128]{2,1,0:T(8,128)} %slice.2357) | copy-start | bytes 21508
  132.7 6.8 %copy-start = (f32[10,12,128]{2,1,0:T(8,128)S(1)}, f32[10,12,128]{2,1,0:T(8,128)}, u32[]{:S(2)}) copy-start(f32[10,12,128]{2,1,0:T(8,128)} %get-tuple-element.594) | copy-start | bytes 184324
  132.7 6.8 %copy-start.1 = (f32[10,12,128]{2,1,0:T(8,128)S(1)}, f32[10,12,128]{2,1,0:T(8,128)}, u32[]{:S(2)}) copy-start(f32[10,12,128]{2,1,0:T(8,128)} %get-tuple-element.595) | copy-start | bytes 184324
  132.7 6.8 %copy-start.2 = (f32[10,13,128]{2,1,0:T(8,128)S(1)}, f32[10,13,128]{2,1,0:T(8,128)}, u32[]{:S(2)}) copy-start(f32[10,13,128]{2,1,0:T(8,128)} %get-tuple-element.596) | copy-start | bytes 199684
  132.7 6.8 %copy-start.3 = (f32[10,13,128]{2,1,0:T(8,128)S(1)}, f32[10,13,128]{2,1,0:T(8,128)}, u32[]{:S(2)}) copy-start(f32[10,13,128]{2,1,0:T(8,128)} %get-tuple-element.597) | copy-start | bytes 199684
  132.7 6.8 %copy-start.15 = (f32[10,1,128]{2,1,0:T(1,128)S(1)}, f32[10,1,128]{2,1,0:T(1,128)}, u32[]{:S(2)}) copy-start(f32[10,1,128]{2,1,0:T(1,128)} %slice.2461) | copy-start | bytes 15364
  132.7 6.8 %copy-start.16 = (f32[10,1,128]{2,1,0:T(1,128)S(1)}, f32[10,1,128]{2,1,0:T(1,128)}, u32[]{:S(2)}) copy-start(f32[10,1,128]{2,1,0:T(1,128)} %slice.2458) | copy-start | bytes 15364
  133.8 19.9 %copy-start.4 = (f32[9,14,128]{2,1,0:T(8,128)S(1)}, f32[9,14,128]{2,1,0:T(8,128)}, u32[]{:S(2)}) copy-start(f32[9,14,128]{2,1,0:T(8,128)} %get-tuple-element.598) | copy-start | bytes 193540
  133.8 19.9 %copy-start.5 = (f32[9,14,128]{2,1,0:T(8,128)S(1)}, f32[9,14,128]{2,1,0:T(8,128)}, u32[]{:S(2)}) copy-start(f32[9,14,128]{2,1,0:T(8,128)} %get-tuple-element.599) | copy-start | bytes 193540
  133.9 19.9 %copy-start.7 = (f32[8,14,128]{2,1,0:T(8,128)S(1)}, f32[8,14,128]{2,1,0:T(8,128)}, u32[]{:S(2)}) copy-start(f32[8,14,128]{2,1,0:T(8,128)} %get-tuple-element.605) | copy-start | bytes 172036
  133.9 19.9 %copy-start.8 = (f32[8,14,128]{2,1,0:T(8,128)S(1)}, f32[8,14,128]{2,1,0:T(8,128)}, u32[]{:S(2)}) copy-start(f32[8,14,128]{2,1,0:T(8,128)} %get-tuple-element.604) | copy-start | bytes 172036
  133.9 19.9 %copy-start.12 = (f32[2,14,128]{2,1,0:T(8,128)S(1)}, f32[2,14,128]{2,1,0:T(8,128)}, u32[]{:S(2)}) copy-start(f32[2,14,128]{2,1,0:T(8,128)} %get-tuple-element.603) | copy-start | bytes 43012
  133.9 19.9 %copy-start.13 = (f32[2,14,128]{2,1,0:T(8,128)S(1)}, f32[2,14,128]{2,1,0:T(8,128)}, u32[]{:S(2)}) copy-start(f32[2,14,128]{2,1,0:T(8,128)} %get-tuple-element.602) | copy-start | bytes 43012
  133.9 19.9 %copy-start.14 = (f32[1,14,128]{2,1,0:T(8,128)S(1)}, f32[1,14,128]{2,1,0:T(8,128)}, u32[]{:S(2)}) copy-start(f32[1,14,128]{2,1,0:T(8,128)} %get-tuple-element.600) | copy-start | bytes 21508
  133.9 5.8 %collective-permute-start.13 = (f32[3,8,128]{2,1,0:T(8,128)S(1)}, f32[3,8,128]{2,1,0:T(8,128)S(1)}, u32[]{:S(2)}, u32[]{:S(2)}) collective-permute-start(f32[3,8,128]{2,1,0:T(8,128)S(1)} %get-tuple-element.607), channel_id=1, source_target_pairs={{8,0},{16,8},{24,16},{32,24},{40,32},{48,40},{56,48},{64,56},{72,6... | collective-permute-start | bytes 36872 | tf_op jit(solution)/shard_map/ppermute | solution.py:24
  136.0 8.7 %collective-permute-start.12 = (f32[3,8,128]{2,1,0:T(8,128)S(1)}, f32[3,8,128]{2,1,0:T(8,128)S(1)}, u32[]{:S(2)}, u32[]{:S(2)}) collective-permute-start(f32[3,8,128]{2,1,0:T(8,128)S(1)} %get-tuple-element.606), channel_id=1, source_target_pairs={{0,8},{8,16},{16,24},{24,32},{32,40},{40,48},{48,56},{56,64},{64,7... | collective-permute-start | bytes 36872 | tf_op jit(solution)/shard_map/ppermute | solution.py:23
  144.7 9.3 %collective-permute-start.14 = (f32[10,3,128]{2,1,0:T(4,128)S(1)}, f32[10,3,128]{2,1,0:T(4,128)S(1)}, u32[]{:S(2)}, u32[]{:S(2)}) collective-permute-start(f32[10,3,128]{2,1,0:T(4,128)S(1)} %get-tuple-element.613), channel_id=1, source_target_pairs={{0,1},{1,2},{2,3},{3,4},{4,5},{5,6},{6,7},{7,0},{8,9},{9,10},{10,1... | collective-permute-start | bytes 46088 | tf_op jit(solution)/shard_map/ppermute | solution.py:23
  151.1 6.4 %collective-permute-start.15 = (f32[10,3,128]{2,1,0:T(4,128)S(1)}, f32[10,3,128]{2,1,0:T(4,128)S(1)}, u32[]{:S(2)}, u32[]{:S(2)}) collective-permute-start(f32[10,3,128]{2,1,0:T(4,128)S(1)} %get-tuple-element.612), channel_id=1, source_target_pairs={{1,0},{2,1},{3,2},{4,3},{5,4},{6,5},{7,6},{0,7},{9,8},{10,9},{11,1... | collective-permute-start | bytes 46088 | tf_op jit(solution)/shard_map/ppermute | solution.py:24
  158.2 5.9 %collective-permute-start.21 = (f32[3,8,128]{2,1,0:T(8,128)S(1)}, f32[3,8,128]{2,1,0:T(8,128)S(1)}, u32[]{:S(2)}, u32[]{:S(2)}) collective-permute-start(f32[3,8,128]{2,1,0:T(8,128)S(1)} %get-tuple-element.585), channel_id=1, source_target_pairs={{8,0},{16,8},{24,16},{32,24},{40,32},{48,40},{56,48},{64,56},{72,6... | collective-permute-start | bytes 36872 | tf_op jit(solution)/shard_map/ppermute | solution.py:24
  160.1 8.7 %collective-permute-start.20 = (f32[3,8,128]{2,1,0:T(8,128)S(1)}, f32[3,8,128]{2,1,0:T(8,128)S(1)}, u32[]{:S(2)}, u32[]{:S(2)}) collective-permute-start(f32[3,8,128]{2,1,0:T(8,128)S(1)} %get-tuple-element.584), channel_id=1, source_target_pairs={{0,8},{8,16},{16,24},{24,32},{32,40},{40,48},{48,56},{56,64},{64,7... | collective-permute-start | bytes 36872 | tf_op jit(solution)/shard_map/ppermute | solution.py:23
  168.8 6.9 %collective-permute-start.23 = (f32[10,3,128]{2,1,0:T(4,128)S(1)}, f32[10,3,128]{2,1,0:T(4,128)S(1)}, u32[]{:S(2)}, u32[]{:S(2)}) collective-permute-start(f32[10,3,128]{2,1,0:T(4,128)S(1)} %get-tuple-element.609), channel_id=1, source_target_pairs={{1,0},{2,1},{3,2},{4,3},{5,4},{6,5},{7,6},{0,7},{9,8},{10,9},{11,1... | collective-permute-start | bytes 46088 | tf_op jit(solution)/shard_map/ppermute | solution.py:24
  173.4 5.3 %collective-permute-start.22 = (f32[10,3,128]{2,1,0:T(4,128)S(1)}, f32[10,3,128]{2,1,0:T(4,128)S(1)}, u32[]{:S(2)}, u32[]{:S(2)}) collective-permute-start(f32[10,3,128]{2,1,0:T(4,128)S(1)} %get-tuple-element.608), channel_id=1, source_target_pairs={{0,1},{1,2},{2,3},{3,4},{4,5},{5,6},{6,7},{7,0},{8,9},{9,10},{10,1... | collective-permute-start | bytes 46088 | tf_op jit(solution)/shard_map/ppermute | solution.py:23
  179.8 6.0 %collective-permute-start.25 = (bf16[16,1,8,128]{3,2,1,0:T(8,128)(2,1)S(1)}, bf16[16,1,8,128]{3,2,1,0:T(8,128)(2,1)S(1)}, u32[]{:S(2)}, u32[]{:S(2)}) collective-permute-start(bf16[16,1,8,128]{3,2,1,0:T(8,128)(2,1)S(1)} %get-tuple-element.561), channel_id=1, source_target_pairs={{8,0},{16,8},{24,16},{32,24},{40,32},{48,40},{56,48},{64,56},{72,6... | collective-permute-start | bytes 98312 | tf_op jit(solution)/shard_map/ppermute | solution.py:24
  181.7 9.0 %collective-permute-start.24 = (bf16[16,1,8,128]{3,2,1,0:T(8,128)(2,1)S(1)}, bf16[16,1,8,128]{3,2,1,0:T(8,128)(2,1)S(1)}, u32[]{:S(2)}, u32[]{:S(2)}) collective-permute-start(bf16[16,1,8,128]{3,2,1,0:T(8,128)(2,1)S(1)} %get-tuple-element.560), channel_id=1, source_target_pairs={{0,8},{8,16},{16,24},{24,32},{32,40},{40,48},{48,56},{56,64},{64,7... | collective-permute-start | bytes 98312 | tf_op jit(solution)/shard_map/ppermute | solution.py:23
  190.8 9.9 %collective-permute-start.27 = (bf16[16,6,1,128]{3,2,1,0:T(2,128)(2,1)S(1)}, bf16[16,6,1,128]{3,2,1,0:T(2,128)(2,1)S(1)}, u32[]{:S(2)}, u32[]{:S(2)}) collective-permute-start(bf16[16,6,1,128]{3,2,1,0:T(2,128)(2,1)S(1)} %get-tuple-element.557), channel_id=1, source_target_pairs={{1,0},{2,1},{3,2},{4,3},{5,4},{6,5},{7,6},{0,7},{9,8},{10,9},{11,1... | collective-permute-start | bytes 73736 | tf_op jit(solution)/shard_map/ppermute | solution.py:24
  198.4 3.1 collective-permute-start.26
  223.5 170.8 %copy-start.20 = (bf16[16,4,8,128]{3,2,1,0:T(8,128)(2,1)}, bf16[16,4,8,128]{3,2,1,0:T(8,128)(2,1)S(1)}, u32[]{:S(2)}) copy-start(bf16[16,4,8,128]{3,2,1,0:T(8,128)(2,1)S(1)} %get-tuple-element.777) | copy-start | bytes 393220
  (2 other events, 2.2 us)
Sparse Core Ops, SparseCore 0:
  126.7 265.3 all-reduce.2
where the time goes:
time: 403 us; the launch traced here: 401 us
  starting transfers between devices  110 us (27%)
  waiting for transfers between devices  108 us (27%)
  blocking collectives  99.2 us (25%)
  local copies, waits for them, and re-layouts  50.3 us (12%)
  between operations  15.6 us (4%)
  other arithmetic  10.9 us (3%)
  matrix products  6.39 us (2%)
    psum x1, blocking collectives, body(): lax.psum((patch_sum / cell_count, local_grad, local_weight), ('gz', 'gy'))  99.2 us
    ppermute x14, starting transfers between devices, extended(): after = lax.ppermute(first, axis, down)  71 us
    psum x1, waiting for transfers between devices, body(): lax.psum((patch_sum / cell_count, local_grad, local_weight), ('gz', 'gy'))  69.5 us
    ppermute x14, starting transfers between devices, extended(): before = lax.ppermute(last, axis, up)  39.2 us
    ppermute x14, waiting for transfers between devices, extended(): before = lax.ppermute(last, axis, up)  34.2 us
    while x320, local copies, waits for them, and re-layouts  23.3 us
  transfers between devices with their start and end apart: 29, of which 11 were waited for; matrix products, arithmetic and copies ran while one was open for 16% of the time, Pallas kernels for 0%

commit v1 on v0

v1 whole, which is shorter than its diff:
```python
import math

import jax
import jax.numpy as jnp
import numpy as np
from jax import lax
from jax.experimental import pallas as pl
from jax.experimental.pallas import tpu as pltpu
from jax.sharding import PartitionSpec as P

H = 0.15
BASE = (2.0 / 60.0, -13.0 / 60.0, 47.0 / 60.0, 27.0 / 60.0, -3.0 / 60.0)
F32 = jnp.float32
BF16 = jnp.bfloat16
NT = (((1,), (1,)), ((), ()))

ROWS_IN = 19
ROWS_OUT = 17
PREV = 5
NEXT = 6

_VM = pl.BlockSpec(memory_space=pltpu.VMEM)


def call(kernel, outs, scratch, args):
    return pl.pallas_call(
        kernel,
        out_shape=[jax.ShapeDtypeStruct(s, t) for s, t in outs],
        in_specs=[_VM] * len(args),
        out_specs=[_VM] * len(outs),
        scratch_shapes=scratch,
        compiler_params=pltpu.CompilerParams(vmem_limit_bytes=48 * 1024 * 1024),
    )(*args)


def roll(value, shift, axis):
    shift %= value.shape[axis]
    return value if shift == 0 else pltpu.roll(value, shift, axis)


def split(plane):
    lead = plane.astype(BF16).astype(F32)
    return jnp.concatenate([lead, plane - lead], axis=0).astype(BF16)


def join(tile):
    both = tile.astype(F32)
    return both[:8] + both[8:]


def pack_y(feat, field, vel, cot, own_feat, own_fields, to_next, to_prev, turn):
    for c in range(16):
        turn[pl.ds(c, 32, stride=16), :] = feat[c].astype(F32)
    for zy in range(32):
        tile = turn[zy * 16 : (zy + 1) * 16, :].astype(BF16)
        own_feat[zy] = tile
        z, y = divmod(zy, 8)
        if y >= 8 - PREV:
            to_next[z * PREV + y - (8 - PREV)] = tile
        if y < NEXT:
            to_prev[z * NEXT + y] = tile
    for i in range(20):
        z = i % 4
        source = field if i < 4 else cot if i < 8 else vel
        plane = source[z] if i < 8 else source[i // 4 - 2, z]
        tile = split(plane)
        own_fields[i] = tile
        to_next[4 * PREV + i] = tile
        to_prev[4 * NEXT + i] = tile


UP_FIELDS = [1, 2, 3, 7, 11, 15, 19]
DOWN_FIELDS = [0, 1, 2, 4, 5, 8, 12, 16]


def pack_z(own_feat, own_fields, before, after, to_up, to_down):
    for out, z, fields in ((to_up, 3, UP_FIELDS), (to_down, 0, DOWN_FIELDS)):
        out[0:PREV] = before[z * PREV : (z + 1) * PREV]
        out[PREV : PREV + 8] = own_feat[z * 8 : (z + 1) * 8]
        out[PREV + 8 : ROWS_IN] = after[z * NEXT : (z + 1) * NEXT]
        at = ROWS_IN
        for i in fields:
            out[at] = before[4 * PREV + i]
            out[at + 1] = own_fields[i]
            out[at + 2] = after[4 * NEXT + i]
            at += 3


def fill_columns(columns, shifted, z, rows):
    for a in range(3):
        for b in range(3):
            at = pl.multiple_of(z * 144 + (a * 3 + b) * 16, 16)
            for y in range(rows):
                columns[pl.ds(at, 16), y * 128 : (y + 1) * 128] = shifted[
                    b, z, (y + a) * 16 : (y + a + 1) * 16, :
                ]


def stage_one(
    own_feat, before, after, below, above, field, vel, cot, w_rows, shift,
    send_up, send_down, gram, columns_own, coef, u0, lam2, velx, u1_part, lam_part, face3,
    shifted, columns,
):
    shift_value = shift[...]
    for z in range(6):
        if z == 0:
            tiles = below[0:ROWS_IN].reshape(ROWS_IN * 16, 128)
        elif z == 5:
            tiles = above[0:ROWS_IN].reshape(ROWS_IN * 16, 128)
        else:
            p = z - 1
            tiles = jnp.concatenate(
                [
                    before[p * PREV : (p + 1) * PREV].reshape(PREV * 16, 128),
                    own_feat[p * 8 : (p + 1) * 8].reshape(128, 128),
                    after[p * NEXT : (p + 1) * NEXT].reshape(NEXT * 16, 128),
                ],
                axis=0,
            )
        shifted[1, z] = tiles
        both = jnp.dot(tiles, shift_value, preferred_element_type=F32).astype(BF16)
        shifted[0, z] = both[:, :128]
        shifted[2, z] = both[:, 128:]

    def extended(i, own):
        return jnp.concatenate(
            [join(before[4 * PREV + i]), own, join(after[4 * NEXT + i])], axis=0
        )

    def received(source, slot):
        at = ROWS_IN + 3 * slot
        return jnp.concatenate([join(source[at + j]) for j in range(3)], axis=0)

    for j in range(3):
        u0[j] = received(below, j)
        u0[7 + j] = received(above, j)
        velx[j, 0] = received(below, 4 + j)
        velx[j, 5] = received(above, 5 + j)
    lam2[0] = received(below, 3)
    lam2[5] = received(above, 3)
    lam2[6] = received(above, 4)
    for z in range(4):
        u0[3 + z] = extended(z, field[z])
        lam2[1 + z] = extended(4 + z, cot[z])
        for d in range(3):
            velx[d, 1 + z] = extended(8 + 4 * d + z, vel[d, z])

    def fill(z, carry):
        fill_columns(columns, shifted, z, ROWS_OUT)
        return carry

    lax.fori_loop(0, 6, fill, 0)

    w_value = w_rows[...]
    for p in range(4):
        plane = jnp.dot(
            w_value, columns[p * 144 : p * 144 + 432, :], preferred_element_type=F32
        )
        for y in range(ROWS_OUT):
            coef[p, (4 + y) * 16 : (5 + y) * 16, :] = plane[:, y * 128 : (y + 1) * 128]

    total = None
    for p in range(4):
        part = lax.dot_general(
            columns[p * 144 : (p + 1) * 144, 512:1536],
            columns[p * 144 + 48 : p * 144 + 432, 512:1536],
            NT,
            preferred_element_type=F32,
        )
        total = part if total is None else total + part
    for t in range(3):
        gram[t * 144 : (t + 1) * 144, :] = total[:, t * 128 : (t + 1) * 128]
    gram[432:, :] = jnp.zeros((gram.shape[0] - 432, 128), F32)
    columns_own[...] = columns[:, 512:1536]

    def a(p, k):
        value = coef[p, pl.ds(k, 24, stride=16), :]
        return value + BASE[k % 5]

    pushed = [None] * 8

    def push(slot, value):
        pushed[slot] = value if pushed[slot] is None else pushed[slot] + value

    faces_z = []
    states = []
    for p in range(4):
        rate = 1.0 + H * coef[p, pl.ds(15, 24, stride=16), :]
        u = u0[3 + p]
        lam = lam2[1 + p]
        state = u * rate
        push(p + 2, lam * rate)
        for d in range(3):
            beyond = lam2[2 + p] if d == 0 else roll(lam, -1, d - 1)
            drive = (-H) * (lam - beyond) * velx[d, 1 + p]
            face = None
            for s in range(-2, 3):
                weight = a(p, 5 * d + s + 2)
                term = weight * (u0[3 + p + s] if d == 0 else roll(u, -s, d - 1))
                face = term if face is None else face + term
                back = drive * weight
                if d == 0:
                    push(p + 2 + s, back)
                else:
                    push(p + 2, roll(back, s, d - 1))
            face = (H * velx[d, 1 + p]) * face
            if d == 0:
                faces_z.append(face)
                state = state - (face if p == 0 else face - faces_z[p - 1])
            else:
                state = state - (face - roll(face, 1, d - 1))
        states.append(state)
    for p in range(4):
        u1_part[p] = states[p]
    for j in range(8):
        lam_part[j] = pushed[j]
    face3[...] = faces_z[3]
    ups = [states[1], states[2], states[3], faces_z[3], pushed[5], pushed[6], pushed[7]]
    downs = [states[0], states[1], states[2], pushed[2], pushed[3], pushed[0], pushed[1]]
    for j in range(7):
        send_up[j] = ups[j][4:20]
        send_down[j] = downs[j][4:20]


def stage_two(
    below, above, u1_part, lam_part, face3, u0, lam2, velx, coef, columns_own, w_back, shift,
    grad_w, grad_feat, lam0, push_up, push_down,
    u1, lam1, turn, shifted, columns, row, turn_out,
):
    def padded(value):
        zero = jnp.zeros((4, 128), F32)
        return jnp.concatenate([zero, value, zero], axis=0)

    low = [padded(below[j]) for j in range(7)]
    high = [padded(above[j]) for j in range(7)]
    for j in range(3):
        u1[j] = low[j]
        u1[7 + j] = high[j] + (face3[...] if j == 0 else 0.0)
        u1[4 + j] = u1_part[1 + j]
    u1[3] = u1_part[0] + low[3]
    lam1[0] = low[4] + lam_part[1]
    lam1[1] = lam_part[2] + low[5]
    lam1[2] = lam_part[3] + low[6]
    lam1[3] = lam_part[4] + high[5]
    lam1[4] = lam_part[5] + high[6]
    lam1[5] = high[3] + lam_part[6]
    lam1[6] = high[4] + lam_part[7]

    pushed = [None] * 8

    def push(slot, value):
        pushed[slot] = value if pushed[slot] is None else pushed[slot] + value

    for z in range(6):
        later, first = lam2[z], lam1[z]
        v, u = u1[z + 2], u0[z + 2]
        own = 1 <= z <= 4
        p = z - 1
        if own:
            push(z + 1, first * (1.0 + H * coef[p, pl.ds(15, 24, stride=16), :]))
        for d in range(3):
            speed = velx[d, z]
            beyond_later = lam2[z + 1] if d == 0 else roll(later, -1, d - 1)
            beyond_first = lam1[z + 1] if d == 0 else roll(first, -1, d - 1)
            drive_later = (-H) * (later - beyond_later) * speed
            drive_first = (-H) * (first - beyond_first) * speed
            for s in range(-2, 3):
                k = 5 * d + s + 2
                there_later = u1[z + 2 + s] if d == 0 else roll(v, -s, d - 1)
                there_first = u0[z + 2 + s] if d == 0 else roll(u, -s, d - 1)
                turn[z, pl.ds(k, 24, stride=16), :] = (
                    drive_later * there_later + drive_first * there_first
                )
                if own:
                    back = drive_first * (coef[p, pl.ds(k, 24, stride=16), :] + BASE[s + 2])
                    if d == 0:
                        push(z + 1 + s, back)
                    else:
                        push(z + 1, roll(back, s, d - 1))
        turn[z, pl.ds(15, 24, stride=16), :] = H * later * v + H * first * u
    for p in range(4):
        lam0[p] = pushed[2 + p][8:16]
    for j in range(2):
        push_up[j] = pushed[6 + j][8:16]
        push_down[j] = pushed[j][8:16]

    shift_value = shift[...]
    for z in range(6):
        tiles = turn[z, 7 * 16 : 17 * 16, :].astype(BF16)
        shifted[1, z] = tiles
        both = jnp.dot(tiles, shift_value, preferred_element_type=F32).astype(BF16)
        shifted[0, z] = both[:, :128]
        shifted[2, z] = both[:, 128:]

    def fill(z, carry):
        fill_columns(columns, shifted, z, 8)
        return carry

    lax.fori_loop(0, 6, fill, 0)

    sum_w = None
    sum_g = None
    for p in range(4):
        at = (p + 1) * 144 + 64
        mine = columns[at : at + 16, :]
        part_w = lax.dot_general(
            mine, columns_own[p * 144 : p * 144 + 432, :], NT, preferred_element_type=F32
        )
        part_g = lax.dot_general(mine, mine, NT, preferred_element_type=F32)
        sum_w = part_w if sum_w is None else sum_w + part_w
        sum_g = part_g if sum_g is None else sum_g + part_g
    row[...] = jnp.zeros((16, 512), F32)
    row[:, 0:432] = sum_w
    row[:, 432:448] = sum_g
    for t in range(4):
        grad_w[t * 16 : (t + 1) * 16, :] = row[:, t * 128 : (t + 1) * 128]

    w_value = w_back[...]
    for p in range(4):
        plane = jnp.dot(
            w_value, columns[p * 144 : p * 144 + 432, :], preferred_element_type=F32
        )
        for y in range(8):
            turn_out[pl.ds(p * 8 + y, 16, stride=32), :] = plane[:, y * 128 : (y + 1) * 128]
    for c in range(16):
        grad_feat[c] = turn_out[c * 32 : (c + 1) * 32, :].astype(BF16)


def pieces(value):
    one = value.astype(BF16)
    rest = value - one.astype(F32)
    two = rest.astype(BF16)
    three = (rest - two.astype(F32)).astype(BF16)
    return one, two, three


def to_channel_major(value):
    i = lax.broadcasted_iota(jnp.int32, (432, 432), 0)
    j = lax.broadcasted_iota(jnp.int32, (432, 432), 1)
    place = jnp.where((i % 16) * 27 + i // 16 == j, 1.0, 0.0).astype(BF16)
    parts = [jnp.dot(v, place, preferred_element_type=F32) for v in pieces(value)]
    return parts[2] + parts[1] + parts[0]


def finish_gram(scale, chunks, out, square, block, turn):
    for t in range(3):
        square[0:144, 48 + t * 128 : 48 + (t + 1) * 128] = chunks[t * 144 : (t + 1) * 144, :] * scale
    square[0:48, 0:48] = square[48:96, 48:96]
    block[...] = jnp.zeros((256, 256), F32)
    block[0:48, 0:96] = square[0:48, 48:144]
    square[48:144, 0:48] = jnp.transpose(block[...])[0:96, 0:48]
    square[144:288, 144:432] = square[0:144, 0:288]
    square[288:432, 288:432] = square[0:144, 0:144]
    block[0:144, 0:144] = square[0:144, 144:288]
    turned = jnp.transpose(block[...])[0:144, 0:144]
    square[144:288, 0:144] = turned
    square[288:432, 144:288] = turned
    block[0:144, 0:144] = square[0:144, 288:432]
    square[288:432, 0:144] = jnp.transpose(block[...])[0:144, 0:144]
    ready = to_channel_major(square[...])
    for t in range(4):
        wide = min(128, 432 - t * 128)
        for o in range(27):
            turn[t, pl.ds(o, 16, stride=27), 0:wide] = ready[
                o * 16 : (o + 1) * 16, t * 128 : t * 128 + wide
            ]
        out[:, t * 128 : t * 128 + wide] = turn[t, :, 0:wide]


def finish_weight(scale_w, scale_g, chunks, out_w, out_g, row):
    for t in range(4):
        row[:, t * 128 : (t + 1) * 128] = chunks[t * 16 : (t + 1) * 16, :]
    out_w[...] = to_channel_major(row[:, 0:432] * scale_w)
    out_g[...] = row[:, 432:448] * scale_g


def neighbours(to_next, to_prev, axis):
    size = lax.axis_size(axis)
    up = [(i, (i + 1) % size) for i in range(size)]
    down = [(j, i) for i, j in up]
    return lax.ppermute(to_next, axis, up), lax.ppermute(to_prev, axis, down)


def body(features, field, velocity, weight, cotangent):
    nz, ny = lax.axis_size("gz"), lax.axis_size("gy")
    cells = float(4096 * nz * ny)
    by_offset = weight.reshape(16, 16, 27)
    w_rows = by_offset.transpose(0, 2, 1).reshape(16, 432)
    w_back = by_offset.transpose(1, 2, 0)[:, ::-1, :].reshape(16, 432)
    eye = np.eye(128)
    shift = jnp.asarray(
        np.concatenate([np.roll(eye, 1, axis=1), np.roll(eye, -1, axis=1)], axis=1), BF16
    )
    tile = (16, 128)
    own_feat, own_fields, to_next, to_prev = call(
        pack_y,
        [((32,) + tile, BF16), ((20,) + tile, BF16), ((4 * PREV + 20,) + tile, BF16),
         ((4 * NEXT + 20,) + tile, BF16)],
        [pltpu.VMEM((512, 128), F32)],
        (features.reshape(16, 32, 128), field, velocity, cotangent),
    )
    before, after = neighbours(to_next, to_prev, "gy")
    to_up, to_down = call(
        pack_z,
        [((ROWS_IN + 3 * len(UP_FIELDS),) + tile, BF16), ((ROWS_IN + 3 * len(DOWN_FIELDS),) + tile, BF16)],
        [],
        (own_feat, own_fields, before, after),
    )
    below, above = neighbours(to_up, to_down, "gz")
    send_up, send_down, gram, columns_own, coef, u0, lam2, velx, u1_part, lam_part, face3 = call(
        stage_one,
        [((7, 16, 128), F32), ((7, 16, 128), F32), ((512, 128), F32), ((864, 1024), BF16),
         ((4, 384, 128), F32), ((10, 24, 128), F32), ((7, 24, 128), F32), ((3, 6, 24, 128), F32),
         ((4, 24, 128), F32), ((8, 24, 128), F32), ((24, 128), F32)],
        [pltpu.VMEM((3, 6, ROWS_IN * 16, 128), BF16), pltpu.VMEM((864, ROWS_OUT * 128), BF16)],
        (own_feat, before, after, below, above, field, velocity, cotangent, w_rows, shift),
    )
    below1, above1 = neighbours(send_up, send_down, "gz")
    gram_parts = lax.all_to_all(gram.reshape(nz, 512 // nz, 128), "gz", 0, 0)
    gram_sum = jnp.sum(gram_parts, axis=0)
    grad_w, grad_feat, lam0, push_up, push_down = call(
        stage_two,
        [((64, 128), F32), ((16, 32, 128), BF16), ((4, 8, 128), F32), ((2, 8, 128), F32),
         ((2, 8, 128), F32)],
        [pltpu.VMEM((10, 24, 128), F32), pltpu.VMEM((7, 24, 128), F32),
         pltpu.VMEM((6, 384, 128), F32), pltpu.VMEM((3, 6, 160, 128), BF16),
         pltpu.VMEM((864, 1024), BF16), pltpu.VMEM((16, 512), F32), pltpu.VMEM((512, 128), F32)],
        (below1, above1, u1_part, lam_part, face3, u0, lam2, velx, coef, columns_own, w_back, shift),
    )
    wr, gr = 64 // ny, 512 // nz
    mixed = jnp.concatenate(
        [grad_w.reshape(ny, wr, 128), jnp.broadcast_to(gram_sum[None], (ny, gr, 128))], axis=1
    )
    mixed = jnp.sum(lax.all_to_all(mixed, "gy", 0, 0), axis=0)
    everyone = lax.all_to_all(jnp.broadcast_to(mixed[None], (nz, wr + gr, 128)), "gz", 0, 0)
    weight_sum = jnp.sum(everyone[:, :wr], axis=0)
    weight_all = lax.all_to_all(jnp.broadcast_to(weight_sum[None], (ny, wr, 128)), "gy", 0, 0)
    low, high = neighbours(push_up, push_down, "gz")
    grad_field = lam0 + jnp.concatenate([low, high], axis=0)
    (factor_patch,) = call(
        lambda *refs: finish_gram(1.0 / cells, *refs),
        [((432, 432), F32)],
        [pltpu.VMEM((432, 432), F32), pltpu.VMEM((256, 256), F32), pltpu.VMEM((4, 432, 128), F32)],
        (everyone[:, wr:].reshape(512, 128),),
    )
    grad_weight, factor_grad = call(
        lambda *refs: finish_weight(1.0 / math.sqrt(cells), 1.0 / cells, *refs),
        [((16, 432), F32), ((16, 16), F32)],
        [pltpu.VMEM((16, 512), F32)],
        (weight_all.reshape(64, 128),),
    )
    return (grad_field, grad_feat.reshape(16, 4, 8, 128), grad_weight, factor_patch, factor_grad)


def solution(mesh):
    placed = (
        P(None, "gz", "gy", None),
        P("gz", "gy", None),
        P(None, "gz", "gy", None),
        P(),
        P("gz", "gy", None),
    )
    return jax.shard_map(
        body,
        mesh=mesh,
        in_specs=placed,
        out_specs=(P("gz", "gy", None), P(None, "gz", "gy", None), P(), P(), P()),
        check_vma=False,
    )
```

time: 403 us -> 135 us (0.33)
  waiting for transfers between devices: 108 us -> 22.5 us
  blocking collectives: 99.2 us -> 19.1 us
  starting transfers between devices: 110 us -> 60.5 us
  local copies, waits for them, and re-layouts: 50.3 us -> 19.1 us
  between operations: 15.6 us -> 0.82 us
  Pallas kernels: 0 us -> 10.8 us
  other arithmetic: 10.9 us -> 0.76 us
  matrix products: 6.39 us -> 0 us
    psum x1 -> x0, blocking collectives: 99.2 us -> none  [body(): lax.psum((patch_sum / cell_count, local_grad, local_weight), ('gz', 'gy'))]
    ppermute x28 -> x8, starting transfers between devices: 110 us -> 39.8 us  [neighbours(): return (lax.ppermute(to_next, axis, up), lax.ppermute(to_prev, axis, down))]
    psum x1 -> x0, waiting for transfers between devices: 69.5 us -> none  [body(): lax.psum((patch_sum / cell_count, local_grad, local_weight), ('gz', 'gy'))]
    ppermute x28 -> x8, waiting for transfers between devices: 38.1 us -> 12 us  [neighbours(): return (lax.ppermute(to_next, axis, up), lax.ppermute(to_prev, axis, down))]
    while x320 -> x0, local copies, waits for them, and re-layouts: 23.3 us -> none
    all_to_all x0 -> x3, starting transfers between devices: none -> 20.7 us  [the longest x1 10.2 us: body(): lax.all_to_all(jnp.broadcast_to(mixed[None], (nz, wr + gr, 128)), 'gz', 0...]
    all_to_all x0 -> x1, blocking collectives: none -> 19.1 us  [body(): mixed = jnp.sum(lax.all_to_all(mixed, 'gy', 0, 0), axis=0)]
    slice x95 -> x0, local copies, waits for them, and re-layouts: 14.6 us -> none  [the longest x14 5.43 us: advance_full(): jnp.roll(field_now, -offset, direction)]
  transfers between devices with their start and end apart: 29 -> 11, of which waited for: 11 -> 5; matrix products, arithmetic and copies ran while one was open for 16% -> 3% of each run, Pallas kernels for 0% -> 4%
where the time goes in v1:
time: 135 us; the launch traced here: 134 us
  starting transfers between devices  60.5 us (45%)
  waiting for transfers between devices  22.5 us (17%)
  local copies, waits for them, and re-layouts  19.1 us (14%)
  blocking collectives  19.1 us (14%)
  Pallas kernels  10.8 us (8%)
    ppermute x8, starting transfers between devices, neighbours(): return (lax.ppermute(to_next, axis, up), lax.ppermute(to_prev, axis, down))  39.8 us
    all_to_all x1, blocking collectives, body(): mixed = jnp.sum(lax.all_to_all(mixed, 'gy', 0, 0), axis=0)  19.1 us
    unnamed x44, local copies, waits for them, and re-layouts  15.1 us
    ppermute x8, waiting for transfers between devices, neighbours(): return (lax.ppermute(to_next, axis, up), lax.ppermute(to_prev, axis, down))  12 us
    pallas_call x6, Pallas kernels, call(): pl.pallas_call(kernel, out_shape=[jax.ShapeDtypeStruct(s, t) for s, t in...  10.8 us
    all_to_all x1, starting transfers between devices, body(): lax.all_to_all(jnp.broadcast_to(mixed[None], (nz, wr + gr, 128)), 'gz', 0...  10.2 us
    all_to_all x1, waiting for transfers between devices, body(): lax.all_to_all(jnp.broadcast_to(mixed[None], (nz, wr + gr, 128)), 'gz', 0...  6.37 us
    all_to_all x1, starting transfers between devices, body(): lax.all_to_all(jnp.broadcast_to(weight_sum[None], (ny, wr, 128)), 'gy', 0...  5.86 us
  transfers between devices with their start and end apart: 11, of which 5 were waited for; matrix products, arithmetic and copies ran while one was open for 3% of the time, Pallas kernels for 4%

profile of v1, /device:TPU:1, one launch (start us, length us, event | category | flops | bytes accessed | tf_op | source)
XLA Modules:
  0.0 133.5 jit_solution(1524265720094886748)
XLA Ops:
  0.7 0.8 copy-done.2
  1.5 0.9 copy-done.6
  2.4 0.7 copy-done.13
  3.1 0.7 copy-done.15
  4.0 8.8 %collective-permute-start.1 = (bf16[44,16,128]{2,1,0:T(8,128)(2,1)S(1)}, bf16[44,16,128]{2,1,0:T(8,128)(2,1)S(1)}, u32[]{:S(2)}, u32[]{:S(2)}) collective-permute-start(bf16[44,16,128]{2,1,0:T(8,128)(2,1)S(1)} %get-tuple-element.31), channel_id=1, source_target_pairs={{1,0},{2,1},{3,2},{4,3},{5,4},{6,5},{7,6},{0,7},{9,8},{10,9},{11,1... | collective-permute-start | bytes 540680 | tf_op jit(solution)/shard_map/ppermute | solution.py:381
  12.8 1.9 %collective-permute-start = (bf16[40,16,128]{2,1,0:T(8,128)(2,1)S(1)}, bf16[40,16,128]{2,1,0:T(8,128)(2,1)S(1)}, u32[]{:S(2)}, u32[]{:S(2)}) collective-permute-start(bf16[40,16,128]{2,1,0:T(8,128)(2,1)S(1)} %get-tuple-element.30), channel_id=1, source_target_pairs={{0,1},{1,2},{2,3},{3,4},{4,5},{5,6},{6,7},{7,0},{8,9},{9,10},{10,1... | collective-permute-start | bytes 491528 | tf_op jit(solution)/shard_map/ppermute | solution.py:381
  14.7 4.0 %collective-permute-done.before = bf16[40,16,128]{2,1,0:T(8,128)(2,1)S(1)} collective-permute-done((bf16[40,16,128]{2,1,0:T(8,128)(2,1)S(1)}, bf16[40,16,128]{2,1,0:T(8,128)(2,1)S(1)}, u32[]{:S(2)}, u32[]{:S(2)}) %collective-permute-start) | collective-permute-done | bytes 163872 | tf_op jit(solution)/shard_map/ppermute | solution.py:381
  18.7 8.2 %collective-permute-start.3 = (bf16[43,16,128]{2,1,0:T(8,128)(2,1)S(1)}, bf16[43,16,128]{2,1,0:T(8,128)(2,1)S(1)}, u32[]{:S(2)}, u32[]{:S(2)}) collective-permute-start(bf16[43,16,128]{2,1,0:T(8,128)(2,1)S(1)} %get-tuple-element.34), channel_id=1, source_target_pairs={{8,0},{16,8},{24,16},{32,24},{40,32},{48,40},{56,48},{64,56},{72,6... | collective-permute-start | bytes 528392 | tf_op jit(solution)/shard_map/ppermute | solution.py:381
  26.9 1.9 %collective-permute-start.2 = (bf16[40,16,128]{2,1,0:T(8,128)(2,1)S(1)}, bf16[40,16,128]{2,1,0:T(8,128)(2,1)S(1)}, u32[]{:S(2)}, u32[]{:S(2)}) collective-permute-start(bf16[40,16,128]{2,1,0:T(8,128)(2,1)S(1)} %get-tuple-element.33), channel_id=1, source_target_pairs={{0,8},{8,16},{16,24},{24,32},{32,40},{40,48},{48,56},{56,64},{64,7... | collective-permute-start | bytes 491528 | tf_op jit(solution)/shard_map/ppermute | solution.py:381
  28.8 0.8 reshape.41
  29.7 0.2 copy.13
  29.9 0.2 reshape.42.w_rows
  30.0 7.1 %collective-permute-done.2.below = bf16[40,16,128]{2,1,0:T(8,128)(2,1)S(1)} collective-permute-done((bf16[40,16,128]{2,1,0:T(8,128)(2,1)S(1)}, bf16[40,16,128]{2,1,0:T(8,128)(2,1)S(1)}, u32[]{:S(2)}, u32[]{:S(2)}) %collective-permute-start.2) | collective-permute-done | bytes 163872 | tf_op jit(solution)/shard_map/ppermute | solution.py:381
  37.2 0.7 copy-done.4
  37.9 0.8 copy-done
  38.7 0.8 copy-done.3
  39.5 0.9 copy-done.5
  40.4 0.7 copy-done.14
  41.1 0.7 copy-done.16
  41.8 4.1 %shard_map.103 = (f32[7,16,128]{2,1,0:T(8,128)S(1)}, f32[7,16,128]{2,1,0:T(8,128)S(1)}, f32[512,128]{1,0:T(8,128)}, bf16[864,1024]{1,0:T(8,128)(2,1)S(1)}, f32[4...) custom-call(bf16[32,16,128]{2,1,0:T(8,128)(2,1)S(1)} %get-tuple-elem, ...), custom_call_target="tpu_custom_call" | custom-call | tf_op jit(solution)/shard_map/pallas_call | solution.py:26
  45.9 0.6 copy-done.7
  46.6 0.6 copy-done.9
  47.2 0.6 copy-done.11
  47.9 0.6 copy-done.17
  48.5 0.6 copy-done.19
  49.1 0.6 copy-done.20
  49.7 4.6 %all-to-all-start = ((f32[64,8,128]{2,1,0:T(8,128)}), f32[64,8,128]{2,1,0:T(8,128)S(1)}, u32[]{:S(2)}, u32[]{:S(2)}) async-start(f32[64,8,128]{2,1,0:T(8,128)} %bitcast.5), calls=%async_computation | async-start | bytes 524288 | tf_op jit(solution)/shard_map/all_to_all | solution.py:419
  54.4 2.8 %collective-permute-start.4 = (f32[7,16,128]{2,1,0:T(8,128)}, f32[7,16,128]{2,1,0:T(8,128)S(1)}, u32[]{:S(2)}, u32[]{:S(2)}) collective-permute-start(f32[7,16,128]{2,1,0:T(8,128)} %copy-done.20), channel_id=1, source_target_pairs={{0,8},{8,16},{16,24},{24,32},{32,40},{40,48},{48,56},{56,64},{64,7... | collective-permute-start | bytes 172040 | tf_op jit(solution)/shard_map/ppermute | solution.py:381
  57.2 6.7 %collective-permute-start.5 = (f32[7,16,128]{2,1,0:T(8,128)}, f32[7,16,128]{2,1,0:T(8,128)S(1)}, u32[]{:S(2)}, u32[]{:S(2)}) collective-permute-start(f32[7,16,128]{2,1,0:T(8,128)} %copy-done.19), channel_id=1, source_target_pairs={{8,0},{16,8},{24,16},{32,24},{40,32},{48,40},{56,48},{64,56},{72,6... | collective-permute-start | bytes 172040 | tf_op jit(solution)/shard_map/ppermute | solution.py:381
  63.9 1.0 copy.14
  65.2 0.9 collective-permute-done.5.above
  66.1 0.9 copy-done.8
  67.0 0.9 copy-done.10
  67.9 0.9 copy-done.12
  68.8 0.8 copy-done.18
  69.6 3.1 %shard_map.104 = (f32[64,128]{1,0:T(8,128)S(1)}, bf16[16,32,128]{2,1,0:T(8,128)(2,1)}, f32[4,8,128]{2,1,0:T(8,128)S(1)}, f32[2,8,128]{2,1,0:T(8,128)S(1)}, f32[2,8,128]{2,1,0:T(8,128)S(1)}) custom-call(f32[7,16,128]{2,1,0:T(8,128)S(1)} %collective-permute-done.4.below, f32[7,16,128]{2,1,0:T(8,128)S(1)} %collective-permute-done.5.above, ...), custom_call_target="tpu_custom_call" | custom-call | tf_op jit(solution)/shard_map/pallas_call | solution.py:26
  72.8 19.1 %all_to_all.20 = f32[8,16,128]{2,1,0:T(8,128)S(1)} all-to-all(f32[8,16,128]{2,1,0:T(8,128)S(1)} %pad_maximum_fusion), channel_id=1, replica_groups=mesh['gz'=64,'gy'=8] {'gy'}, dimensions={0} | all-to-all | bytes 131072 | tf_op jit(solution)/shard_map/all_to_all | solution.py:434
  91.9 0.8 broadcast_in_dim.7
  92.7 10.2 %all-to-all-start.2 = ((f32[64,16,128]{2,1,0:T(8,128)}), f32[64,16,128]{2,1,0:T(8,128)S(1)}, u32[]{:S(2)}, u32[]{:S(2)}) async-start(f32[64,16,128]{2,1,0:T(8,128)} %broadcast_in_dim.7), calls=%async_computation.2 | async-start | bytes 1048576 | tf_op jit(solution)/shard_map/all_to_all | solution.py:435
  102.9 2.9 %collective-permute-start.6 = (f32[2,8,128]{2,1,0:T(8,128)S(1)}, f32[2,8,128]{2,1,0:T(8,128)S(1)}, u32[]{:S(2)}, u32[]{:S(2)}) collective-permute-start(f32[2,8,128]{2,1,0:T(8,128)S(1)} %get-tuple-element.46), channel_id=1, source_target_pairs={{0,8},{8,16},{16,24},{24,32},{32,40},{40,48},{48,56},{56,64},{64,7... | collective-permute-start | bytes 24584 | tf_op jit(solution)/shard_map/ppermute | solution.py:381
  105.8 6.6 %collective-permute-start.7 = (f32[2,8,128]{2,1,0:T(8,128)S(1)}, f32[2,8,128]{2,1,0:T(8,128)S(1)}, u32[]{:S(2)}, u32[]{:S(2)}) collective-permute-start(f32[2,8,128]{2,1,0:T(8,128)S(1)} %get-tuple-element.47), channel_id=1, source_target_pairs={{8,0},{16,8},{24,16},{32,24},{40,32},{48,40},{56,48},{64,56},{72,6... | collective-permute-start | bytes 24584 | tf_op jit(solution)/shard_map/ppermute | solution.py:381
  112.4 6.4 %all-to-all-done.2 = f32[64,16,128]{2,1,0:T(8,128)S(1)} async-done(((f32[64,16,128]{2,1,0:T(8,128)}), f32[64,16,128]{2,1,0:T(8,128)S(1)}, u32[]{:S(2)}, u32[]{:S(2)}) %all-to-all-start.2) | async-done | bytes 524320 | tf_op jit(solution)/shard_map/all_to_all | solution.py:435
  118.9 0.6 broadcast_in_dim.8
  119.5 5.9 %all-to-all-start.3 = ((f32[8,8,128]{2,1,0:T(8,128)}), f32[8,8,128]{2,1,0:T(8,128)S(1)}, u32[]{:S(2)}, u32[]{:S(2)}) async-start(f32[8,8,128]{2,1,0:T(8,128)} %broadcast_in_dim.8), calls=%async_computation.3 | async-start | bytes 65536 | tf_op jit(solution)/shard_map/all_to_all | solution.py:437
  125.4 0.6 maximum_add_fusion
  126.0 2.5 %shard_map.106 = f32[432,432]{1,0:T(8,128)} custom-call(f32[512,128]{1,0:T(8,128)S(1)} %get-tuple-element.53.refs_0_), custom_call_target="tpu_custom_call" | custom-call | tf_op jit(solution)/shard_map/pallas_call | solution.py:26
  128.4 4.2 %all-to-all-done.3 = f32[8,8,128]{2,1,0:T(8,128)S(1)} async-done(((f32[8,8,128]{2,1,0:T(8,128)}), f32[8,8,128]{2,1,0:T(8,128)S(1)}, u32[]{:S(2)}, u32[]{:S(2)}) %all-to-all-start.3) | async-done | bytes 32800 | tf_op jit(solution)/shard_map/all_to_all | solution.py:437
  132.6 1.0 shard_map.105
  (39 shorter events, 0.7 us)
Async XLA Ops:
  0.6 65.4 %copy-start.1 = (bf16[128,256]{1,0:T(8,128)(2,1)S(1)}, bf16[128,256]{1,0:T(8,128)(2,1)}, u32[]{:S(2)}) copy-start(bf16[128,256]{1,0:T(8,128)(2,1)} %constant.4.clone.shift) | copy-start | bytes 196612
  0.6 0.8 copy-start.2
  1.5 0.9 copy-start.6
  2.4 0.7 copy-start.13
  3.1 0.7 copy-start.15
  4.0 14.7 %collective-permute-start.1 = (bf16[44,16,128]{2,1,0:T(8,128)(2,1)S(1)}, bf16[44,16,128]{2,1,0:T(8,128)(2,1)S(1)}, u32[]{:S(2)}, u32[]{:S(2)}) collective-permute-start(bf16[44,16,128]{2,1,0:T(8,128)(2,1)S(1)} %get-tuple-element.31), channel_id=1, source_target_pairs={{1,0},{2,1},{3,2},{4,3},{5,4},{6,5},{7,6},{0,7},{9,8},{10,9},{11,1... | collective-permute-start | bytes 540680 | tf_op jit(solution)/shard_map/ppermute | solution.py:381
  12.8 5.9 %collective-permute-start = (bf16[40,16,128]{2,1,0:T(8,128)(2,1)S(1)}, bf16[40,16,128]{2,1,0:T(8,128)(2,1)S(1)}, u32[]{:S(2)}, u32[]{:S(2)}) collective-permute-start(bf16[40,16,128]{2,1,0:T(8,128)(2,1)S(1)} %get-tuple-element.30), channel_id=1, source_target_pairs={{0,1},{1,2},{2,3},{3,4},{4,5},{5,6},{6,7},{7,0},{8,9},{9,10},{10,1... | collective-permute-start | bytes 491528 | tf_op jit(solution)/shard_map/ppermute | solution.py:381
  18.7 19.2 %collective-permute-start.3 = (bf16[43,16,128]{2,1,0:T(8,128)(2,1)S(1)}, bf16[43,16,128]{2,1,0:T(8,128)(2,1)S(1)}, u32[]{:S(2)}, u32[]{:S(2)}) collective-permute-start(bf16[43,16,128]{2,1,0:T(8,128)(2,1)S(1)} %get-tuple-element.34), channel_id=1, source_target_pairs={{8,0},{16,8},{24,16},{32,24},{40,32},{48,40},{56,48},{64,56},{72,6... | collective-permute-start | bytes 528392 | tf_op jit(solution)/shard_map/ppermute | solution.py:381
  26.9 10.3 %collective-permute-start.2 = (bf16[40,16,128]{2,1,0:T(8,128)(2,1)S(1)}, bf16[40,16,128]{2,1,0:T(8,128)(2,1)S(1)}, u32[]{:S(2)}, u32[]{:S(2)}) collective-permute-start(bf16[40,16,128]{2,1,0:T(8,128)(2,1)S(1)} %get-tuple-element.33), channel_id=1, source_target_pairs={{0,8},{8,16},{16,24},{24,32},{32,40},{40,48},{48,56},{56,64},{64,7... | collective-permute-start | bytes 491528 | tf_op jit(solution)/shard_map/ppermute | solution.py:381
  29.7 7.5 %copy-start.21 = (bf16[16,16,27]{2,1,0:T(8,128)(2,1)}, bf16[16,16,27]{2,1,0:T(8,128)(2,1)S(1)}, u32[]{:S(2)}) copy-start(bf16[16,16,27]{2,1,0:T(8,128)(2,1)S(1)} %reshape.41) | copy-start | bytes 41476
  37.2 0.7 copy-start.4
  37.9 0.8 copy-start
  38.7 0.8 copy-start.3
  39.5 0.9 copy-start.5
  40.4 0.7 copy-start.14
  41.1 0.7 copy-start.16
  45.9 0.6 copy-start.7
  46.6 0.6 copy-start.9
  47.2 0.6 copy-start.11
  47.9 0.6 copy-start.17
  48.5 0.6 copy-start.19
  49.1 0.6 copy-start.20
  49.7 22.9 %all-to-all-start = ((f32[64,8,128]{2,1,0:T(8,128)}), f32[64,8,128]{2,1,0:T(8,128)S(1)}, u32[]{:S(2)}, u32[]{:S(2)}) async-start(f32[64,8,128]{2,1,0:T(8,128)} %bitcast.5), calls=%async_computation | async-start | bytes 524288 | tf_op jit(solution)/shard_map/all_to_all | solution.py:419
  54.4 10.8 %collective-permute-start.4 = (f32[7,16,128]{2,1,0:T(8,128)}, f32[7,16,128]{2,1,0:T(8,128)S(1)}, u32[]{:S(2)}, u32[]{:S(2)}) collective-permute-start(f32[7,16,128]{2,1,0:T(8,128)} %copy-done.20), channel_id=1, source_target_pairs={{0,8},{8,16},{16,24},{24,32},{32,40},{40,48},{48,56},{56,64},{64,7... | collective-permute-start | bytes 172040 | tf_op jit(solution)/shard_map/ppermute | solution.py:381
  57.2 8.9 %collective-permute-start.5 = (f32[7,16,128]{2,1,0:T(8,128)}, f32[7,16,128]{2,1,0:T(8,128)S(1)}, u32[]{:S(2)}, u32[]{:S(2)}) collective-permute-start(f32[7,16,128]{2,1,0:T(8,128)} %copy-done.19), channel_id=1, source_target_pairs={{8,0},{16,8},{24,16},{32,24},{40,32},{48,40},{56,48},{64,56},{72,6... | collective-permute-start | bytes 172040 | tf_op jit(solution)/shard_map/ppermute | solution.py:381
  66.1 0.9 copy-start.8
  67.0 0.9 copy-start.10
  67.9 0.9 copy-start.12
  68.8 0.8 copy-start.18
  92.7 26.1 %all-to-all-start.2 = ((f32[64,16,128]{2,1,0:T(8,128)}), f32[64,16,128]{2,1,0:T(8,128)S(1)}, u32[]{:S(2)}, u32[]{:S(2)}) async-start(f32[64,16,128]{2,1,0:T(8,128)} %broadcast_in_dim.7), calls=%async_computation.2 | async-start | bytes 1048576 | tf_op jit(solution)/shard_map/all_to_all | solution.py:435
  102.9 22.4 %collective-permute-start.6 = (f32[2,8,128]{2,1,0:T(8,128)S(1)}, f32[2,8,128]{2,1,0:T(8,128)S(1)}, u32[]{:S(2)}, u32[]{:S(2)}) collective-permute-start(f32[2,8,128]{2,1,0:T(8,128)S(1)} %get-tuple-element.46), channel_id=1, source_target_pairs={{0,8},{8,16},{16,24},{24,32},{32,40},{40,48},{48,56},{56,64},{64,7... | collective-permute-start | bytes 24584 | tf_op jit(solution)/shard_map/ppermute | solution.py:381
  105.8 19.5 %collective-permute-start.7 = (f32[2,8,128]{2,1,0:T(8,128)S(1)}, f32[2,8,128]{2,1,0:T(8,128)S(1)}, u32[]{:S(2)}, u32[]{:S(2)}) collective-permute-start(f32[2,8,128]{2,1,0:T(8,128)S(1)} %get-tuple-element.47), channel_id=1, source_target_pairs={{8,0},{16,8},{24,16},{32,24},{40,32},{48,40},{56,48},{64,56},{72,6... | collective-permute-start | bytes 24584 | tf_op jit(solution)/shard_map/ppermute | solution.py:381
  119.5 13.1 %all-to-all-start.3 = ((f32[8,8,128]{2,1,0:T(8,128)}), f32[8,8,128]{2,1,0:T(8,128)S(1)}, u32[]{:S(2)}, u32[]{:S(2)}) async-start(f32[8,8,128]{2,1,0:T(8,128)} %broadcast_in_dim.8), calls=%async_computation.3 | async-start | bytes 65536 | tf_op jit(solution)/shard_map/all_to_all | solution.py:437

commit v2 on v1

--- a/solution.py
+++ b/solution.py
@@ -2,7 +2,6 @@
 
 import jax
 import jax.numpy as jnp
-import numpy as np
 from jax import lax
 from jax.experimental import pallas as pl
 from jax.experimental.pallas import tpu as pltpu
@@ -19,18 +18,56 @@
 PREV = 5
 NEXT = 6
 
-_VM = pl.BlockSpec(memory_space=pltpu.VMEM)
+_HBM = pl.BlockSpec(memory_space=pltpu.HBM)
 
 
 def call(kernel, outs, scratch, args):
+    n_in, n_out = len(args), len(outs)
+
+    def run(*refs):
+        source, target = refs[:n_in], refs[n_in : n_in + n_out]
+        arrived, left = refs[n_in + n_out : n_in + n_out + 2]
+        held = refs[n_in + n_out + 2 :]
+        here, there = held[:n_in], held[n_in : n_in + n_out]
+        coming = {i: pltpu.make_async_copy(source[i], here[i], arrived.at[i]) for i in range(n_in)}
+        going = {i: pltpu.make_async_copy(there[i], target[i], left.at[i]) for i in range(n_out)}
+        sent = []
+        for i in range(n_in):
+            coming[i].start()
+
+        def need(*which):
+            for i in which:
+                coming.pop(i).wait()
+
+        def done(*which):
+            for i in which:
+                going[i].start()
+                sent.append(i)
+
+        kernel(need, done, *held)
+        need(*list(coming))
+        done(*[i for i in range(n_out) if i not in sent])
+        for i in range(n_out):
+            going[i].wait()
+
     return pl.pallas_call(
-        kernel,
+        run,
         out_shape=[jax.ShapeDtypeStruct(s, t) for s, t in outs],
-        in_specs=[_VM] * len(args),
-        out_specs=[_VM] * len(outs),
-        scratch_shapes=scratch,
-        compiler_params=pltpu.CompilerParams(vmem_limit_bytes=48 * 1024 * 1024),
+        in_specs=[_HBM] * n_in,
+        out_specs=[_HBM] * n_out,
+        scratch_shapes=[pltpu.SemaphoreType.DMA((n_in,)), pltpu.SemaphoreType.DMA((n_out,))]
+        + [pltpu.VMEM(a.shape, a.dtype) for a in args]
+        + [pltpu.VMEM(s, t) for s, t in outs]
+        + scratch,
+        compiler_params=pltpu.CompilerParams(vmem_limit_bytes=64 * 1024 * 1024),
     )(*args)
+
+
+def shift_both():
+    i = lax.broadcasted_iota(jnp.int32, (128, 256), 0)
+    j = lax.broadcasted_iota(jnp.int32, (128, 256), 1)
+    source = jnp.where(j < 128, j + 127, j + 1) % 128
+    return jnp.where(i == source, 1.0, 0.0).astype(BF16)
 
 
 def roll(value, shift, axis):
@@ -48,7 +85,17 @@
     return both[:8] + both[8:]
 
 
-def pack_y(feat, field, vel, cot, own_feat, own_fields, to_next, to_prev, turn):
+ORDER = [
+    ("l", 3), (0, 3), (1, 3), (2, 3), ("u", 3), ("u", 1), ("u", 2), ("u", 0), ("l", 0), ("l", 1),
+    (0, 0), (1, 0), (2, 0), ("l", 2), (0, 1), (0, 2), (1, 1), (1, 2), (2, 1), (2, 2),
+]
+UP, DOWN = (0, 7), (5, 13)
+
+
+def pack_y(
+    need, done, feat, field, vel, cot, own_feat, own_fields, to_next, to_prev, turn
+):
+    need(0)
     for c in range(16):
         turn[pl.ds(c, 32, stride=16), :] = feat[c].astype(F32)
     for zy in range(32):
@@ -59,31 +106,36 @@
             to_next[z * PREV + y - (8 - PREV)] = tile
         if y < NEXT:
             to_prev[z * NEXT + y] = tile
-    for i in range(20):
-        z = i % 4
-        source = field if i < 4 else cot if i < 8 else vel
-        plane = source[z] if i < 8 else source[i // 4 - 2, z]
-        tile = split(plane)
+    need(1, 2, 3)
+    for i, (kind, z) in enumerate(ORDER):
+        tile = split(field[z] if kind == "u" else cot[z] if kind == "l" else vel[kind, z])
         own_fields[i] = tile
         to_next[4 * PREV + i] = tile
         to_prev[4 * NEXT + i] = tile
 
 
-UP_FIELDS = [1, 2, 3, 7, 11, 15, 19]
-DOWN_FIELDS = [0, 1, 2, 4, 5, 8, 12, 16]
-
-
-def pack_z(own_feat, own_fields, before, after, to_up, to_down):
-    for out, z, fields in ((to_up, 3, UP_FIELDS), (to_down, 0, DOWN_FIELDS)):
-        out[0:PREV] = before[z * PREV : (z + 1) * PREV]
-        out[PREV : PREV + 8] = own_feat[z * 8 : (z + 1) * 8]
-        out[PREV + 8 : ROWS_IN] = after[z * NEXT : (z + 1) * NEXT]
-        at = ROWS_IN
-        for i in fields:
-            out[at] = before[4 * PREV + i]
-            out[at + 1] = own_fields[i]
-            out[at + 2] = after[4 * NEXT + i]
-            at += 3
+def pack_z(own_feat, own_fields, before, after, to_up, to_down, moved):
+    copies = []
+
+    def move(source, at, out, to, count):
+        copies.append(
+            pltpu.make_async_copy(
+                source.at[at : at + count], out.at[to : to + count], moved.at[len(copies)]
+            )
+        )
+
+    for out, z, (first, stop) in ((to_up, 3, UP), (to_down, 0, DOWN)):
+        n = stop - first
+        move(before, z * PREV, out, 0, PREV)
+        move(own_feat, z * 8, out, PREV, 8)
+        move(after, z * NEXT, out, PREV + 8, NEXT)
+        move(before, 4 * PREV + first, out, ROWS_IN, n)
+        move(own_fields, first, out, ROWS_IN + n, n)
+        move(after, 4 * NEXT + first, out, ROWS_IN + 2 * n, n)
+    for copy in copies:
+        copy.start()
+    for copy in copies:
+        copy.wait()
 
 
 def fill_columns(columns, shifted, z, rows):
@@ -96,12 +148,20 @@
                 ]
 
 
+U0, LAM2, U1, LAM1, FACE = slice(0, 10), slice(10, 17), slice(35, 39), slice(39, 47), 47
+VEL = (slice(17, 23), slice(23, 29), slice(29, 35))
+FAR = [(2, 2), (3, 1), (3, 2), (1, -2), (0, -1), (0, -2)]
+
+
 def stage_one(
-    own_feat, before, after, below, above, field, vel, cot, w_rows, shift,
-    send_up, send_down, gram, columns_own, coef, u0, lam2, velx, u1_part, lam_part, face3,
+    need, done, own_feat, before, after, below, above, field, vel, cot, w_rows,
+    send_up, send_down, send_far, gram, columns_own, coef, kept,
     shifted, columns,
 ):
-    shift_value = shift[...]
+    u0, lam2 = kept.at[U0], kept.at[LAM2]
+    velx = [kept.at[v] for v in VEL]
+    shift_value = shift_both()
+    need(0, 1, 2, 3, 4)
     for z in range(6):
         if z == 0:
             tiles = below[0:ROWS_IN].reshape(ROWS_IN * 16, 128)
@@ -122,28 +182,32 @@
         shifted[0, z] = both[:, :128]
         shifted[2, z] = both[:, 128:]
 
-    def extended(i, own):
+    need(5, 6, 7)
+
+    def extended(kind, z, own):
+        i = ORDER.index((kind, z))
         return jnp.concatenate(
             [join(before[4 * PREV + i]), own, join(after[4 * NEXT + i])], axis=0
         )
 
-    def received(source, slot):
-        at = ROWS_IN + 3 * slot
-        return jnp.concatenate([join(source[at + j]) for j in range(3)], axis=0)
+    def received(source, part, kind, z):
+        n = part[1] - part[0]
+        at = ROWS_IN + ORDER.index((kind, z)) - part[0]
+        return jnp.concatenate([join(source[at + n * j]) for j in range(3)], axis=0)
 
     for j in range(3):
-        u0[j] = received(below, j)
-        u0[7 + j] = received(above, j)
-        velx[j, 0] = received(below, 4 + j)
-        velx[j, 5] = received(above, 5 + j)
-    lam2[0] = received(below, 3)
-    lam2[5] = received(above, 3)
-    lam2[6] = received(above, 4)
+        u0[j] = received(below, UP, "u", 1 + j)
+        u0[7 + j] = received(above, DOWN, "u", j)
+        velx[j][0] = received(below, UP, j, 3)
+        velx[j][5] = received(above, DOWN, j, 0)
+    lam2[0] = received(below, UP, "l", 3)
+    lam2[5] = received(above, DOWN, "l", 0)
+    lam2[6] = received(above, DOWN, "l", 1)
     for z in range(4):
-        u0[3 + z] = extended(z, field[z])
-        lam2[1 + z] = extended(4 + z, cot[z])
+        u0[3 + z] = extended("u", z, field[z])
+        lam2[1 + z] = extended("l", z, cot[z])
         for d in range(3):
-            velx[d, 1 + z] = extended(8 + 4 * d + z, vel[d, z])
+            velx[d][1 + z] = extended(d, z, vel[d, z])
 
     def fill(z, carry):
         fill_columns(columns, shifted, z, ROWS_OUT)
@@ -151,6 +215,7 @@
 
     lax.fori_loop(0, 6, fill, 0)
 
+    need(8)
     w_value = w_rows[...]
     for p in range(4):
         plane = jnp.dot(
@@ -172,6 +237,7 @@
         gram[t * 144 : (t + 1) * 144, :] = total[:, t * 128 : (t + 1) * 128]
     gram[432:, :] = jnp.zeros((gram.shape[0] - 432, 128), F32)
     columns_own[...] = columns[:, 512:1536]
+    done(3, 4, 5)
 
     def a(p, k):
         value = coef[p, pl.ds(k, 24, stride=16), :]
@@ -184,6 +250,7 @@
 
     faces_z = []
     states = []
+    carried = {}
     for p in range(4):
         rate = 1.0 + H * coef[p, pl.ds(15, 24, stride=16), :]
         u = u0[3 + p]
@@ -192,7 +259,7 @@
         push(p + 2, lam * rate)
         for d in range(3):
             beyond = lam2[2 + p] if d == 0 else roll(lam, -1, d - 1)
-            drive = (-H) * (lam - beyond) * velx[d, 1 + p]
+            drive = (-H) * (lam - beyond) * velx[d][1 + p]
             face = None
             for s in range(-2, 3):
                 weight = a(p, 5 * d + s + 2)
@@ -201,41 +268,54 @@
                 back = drive * weight
                 if d == 0:
                     push(p + 2 + s, back)
+                    if (p, s) in FAR:
+                        carried[p, s] = velx[0][1 + p] * weight
                 else:
                     push(p + 2, roll(back, s, d - 1))
-            face = (H * velx[d, 1 + p]) * face
+            face = (H * velx[d][1 + p]) * face
             if d == 0:
                 faces_z.append(face)
                 state = state - (face if p == 0 else face - faces_z[p - 1])
             else:
                 state = state - (face - roll(face, 1, d - 1))
         states.append(state)
+    u1_part, lam_part = kept.at[U1], kept.at[LAM1]
     for p in range(4):
         u1_part[p] = states[p]
     for j in range(8):
         lam_part[j] = pushed[j]
-    face3[...] = faces_z[3]
-    ups = [states[1], states[2], states[3], faces_z[3], pushed[5], pushed[6], pushed[7]]
-    downs = [states[0], states[1], states[2], pushed[2], pushed[3], pushed[0], pushed[1]]
-    for j in range(7):
+    kept[FACE] = faces_z[3]
+    ups = [states[1], states[2], states[3], faces_z[3], pushed[5], pushed[6], pushed[7], pushed[4]]
+    downs = [states[0], states[1], states[2], pushed[2], pushed[3], pushed[0], pushed[1], pushed[4]]
+    for j in range(8):
         send_up[j] = ups[j][4:20]
         send_down[j] = downs[j][4:20]
+    for out, keys in ((send_up, FAR[:3]), (send_down, FAR[3:])):
+        out[8, 0:8, :] = carried[keys[0]][8:16]
+        out[8, 8:16, :] = carried[keys[1]][8:16]
+        out[9, 0:8, :] = carried[keys[2]][8:16]
+        out[9, 8:16, :] = carried[keys[2]][8:16]
+    send_far[...] = pushed[0][8:16]
 
 
 def stage_two(
-    below, above, u1_part, lam_part, face3, u0, lam2, velx, coef, columns_own, w_back, shift,
-    grad_w, grad_feat, lam0, push_up, push_down,
+    need, done, below, above, far, state, coef, columns_own, w_back,
+    grad_w, grad_feat, lam0,
     u1, lam1, turn, shifted, columns, row, turn_out,
 ):
+    u0, lam2, u1_part, lam_part = state.at[U0], state.at[LAM2], state.at[U1], state.at[LAM1]
+    velx = [state.at[v] for v in VEL]
+    need(0, 1, 2, 3, 4)
+
     def padded(value):
         zero = jnp.zeros((4, 128), F32)
         return jnp.concatenate([zero, value, zero], axis=0)
 
-    low = [padded(below[j]) for j in range(7)]
-    high = [padded(above[j]) for j in range(7)]
+    low = [padded(below[j]) for j in range(8)]
+    high = [padded(above[j]) for j in range(8)]
     for j in range(3):
         u1[j] = low[j]
-        u1[7 + j] = high[j] + (face3[...] if j == 0 else 0.0)
+        u1[7 + j] = high[j] + (state[FACE] if j == 0 else 0.0)
         u1[4 + j] = u1_part[1 + j]
     u1[3] = u1_part[0] + low[3]
     lam1[0] = low[4] + lam_part[1]
@@ -251,6 +331,20 @@
     def push(slot, value):
         pushed[slot] = value if pushed[slot] is None else pushed[slot] + value
 
+    own_rows = slice(8, 16)
+    lowest = lam_part[0][own_rows] + low[7][own_rows]
+    highest = high[7][own_rows] + far[...]
+    fall = [lowest, lam1[0, own_rows], lam1[1, own_rows]]
+    rise = [lam1[5, own_rows], lam1[6, own_rows], highest]
+    outer = [(-H) * (fall[0] - fall[1]), (-H) * (fall[1] - fall[2])]
+    inner = [(-H) * (rise[0] - rise[1]), (-H) * (rise[1] - rise[2])]
+    edge = [
+        outer[0] * below[8, 0:8, :] + outer[1] * below[8, 8:16, :],
+        outer[1] * below[9, 0:8, :],
+        inner[0] * above[9, 0:8, :],
+        inner[0] * above[8, 8:16, :] + inner[1] * above[8, 0:8, :],
+    ]
+
     for z in range(6):
         later, first = lam2[z], lam1[z]
         v, u = u1[z + 2], u0[z + 2]
@@ -259,7 +353,7 @@
         if own:
             push(z + 1, first * (1.0 + H * coef[p, pl.ds(15, 24, stride=16), :]))
         for d in range(3):
-            speed = velx[d, z]
+            speed = velx[d][z]
             beyond_later = lam2[z + 1] if d == 0 else roll(later, -1, d - 1)
             beyond_first = lam1[z + 1] if d == 0 else roll(first, -1, d - 1)
             drive_later = (-H) * (later - beyond_later) * speed
@@ -279,12 +373,10 @@
                         push(z + 1, roll(back, s, d - 1))
         turn[z, pl.ds(15, 24, stride=16), :] = H * later * v + H * first * u
     for p in range(4):
-        lam0[p] = pushed[2 + p][8:16]
-    for j in range(2):
-        push_up[j] = pushed[6 + j][8:16]
-        push_down[j] = pushed[j][8:16]
-
-    shift_value = shift[...]
+        lam0[p] = pushed[2 + p][own_rows] + edge[p]
+    done(2)
+
+    shift_value = shift_both()
     for z in range(6):
         tiles = turn[z, 7 * 16 : 17 * 16, :].astype(BF16)
         shifted[1, z] = tiles
@@ -298,6 +390,7 @@
 
     lax.fori_loop(0, 6, fill, 0)
 
+    need(5, 6)
     sum_w = None
     sum_g = None
     for p in range(4):
@@ -314,6 +407,7 @@
     row[:, 432:448] = sum_g
     for t in range(4):
         grad_w[t * 16 : (t + 1) * 16, :] = row[:, t * 128 : (t + 1) * 128]
+    done(0)
 
     w_value = w_back[...]
     for p in range(4):
@@ -342,7 +436,8 @@
     return parts[2] + parts[1] + parts[0]
 
 
-def finish_gram(scale, chunks, out, square, block, turn):
+def finish_gram(scale, need, done, chunks, out, square, block, turn):
+    need(0)
     for t in range(3):
         square[0:144, 48 + t * 128 : 48 + (t + 1) * 128] = chunks[t * 144 : (t + 1) * 144, :] * scale
     square[0:48, 0:48] = square[48:96, 48:96]
@@ -367,7 +462,8 @@
         out[:, t * 128 : t * 128 + wide] = turn[t, :, 0:wide]
 
 
-def finish_weight(scale_w, scale_g, chunks, out_w, out_g, row):
+def finish_weight(scale_w, scale_g, need, done, chunks, out_w, out_g, row):
+    need(0)
     for t in range(4):
         row[:, t * 128 : (t + 1) * 128] = chunks[t * 16 : (t + 1) * 16, :]
     out_w[...] = to_channel_major(row[:, 0:432] * scale_w)
@@ -387,10 +483,6 @@
     by_offset = weight.reshape(16, 16, 27)
     w_rows = by_offset.transpose(0, 2, 1).reshape(16, 432)
     w_back = by_offset.transpose(1, 2, 0)[:, ::-1, :].reshape(16, 432)
-    eye = np.eye(128)
-    shift = jnp.asarray(
-        np.concatenate([np.roll(eye, 1, axis=1), np.roll(eye, -1, axis=1)], axis=1), BF16
-    )
     tile = (16, 128)
     own_feat, own_fields, to_next, to_prev = call(
         pack_y,
@@ -400,32 +492,36 @@
         (features.reshape(16, 32, 128), field, velocity, cotangent),
     )
     before, after = neighbours(to_next, to_prev, "gy")
-    to_up, to_down = call(
+    to_up, to_down = pl.pallas_call(
         pack_z,
-        [((ROWS_IN + 3 * len(UP_FIELDS),) + tile, BF16), ((ROWS_IN + 3 * len(DOWN_FIELDS),) + tile, BF16)],
-        [],
-        (own_feat, own_fields, before, after),
-    )
+        out_shape=[
+            jax.ShapeDtypeStruct((ROWS_IN + 3 * (stop - first),) + tile, BF16)
+            for first, stop in (UP, DOWN)
+        ],
+        in_specs=[_HBM] * 4,
+        out_specs=[_HBM] * 2,
+        scratch_shapes=[pltpu.SemaphoreType.DMA((12,))],
+        compiler_params=pltpu.CompilerParams(vmem_limit_bytes=64 * 1024 * 1024),
+    )(own_feat, own_fields, before, after)
     below, above = neighbours(to_up, to_down, "gz")
-    send_up, send_down, gram, columns_own, coef, u0, lam2, velx, u1_part, lam_part, face3 = call(
+    send_up, send_down, send_far, gram, columns_own, coef, state = call(
         stage_one,
-        [((7, 16, 128), F32), ((7, 16, 128), F32), ((512, 128), F32), ((864, 1024), BF16),
-         ((4, 384, 128), F32), ((10, 24, 128), F32), ((7, 24, 128), F32), ((3, 6, 24, 128), F32),
-         ((4, 24, 128), F32), ((8, 24, 128), F32), ((24, 128), F32)],
+        [((10, 16, 128), F32), ((10, 16, 128), F32), ((8, 128), F32), ((512, 128), F32),
+         ((864, 1024), BF16), ((4, 384, 128), F32), ((48, 24, 128), F32)],
         [pltpu.VMEM((3, 6, ROWS_IN * 16, 128), BF16), pltpu.VMEM((864, ROWS_OUT * 128), BF16)],
-        (own_feat, before, after, below, above, field, velocity, cotangent, w_rows, shift),
+        (own_feat, before, after, below, above, field, velocity, cotangent, w_rows),
     )
     below1, above1 = neighbours(send_up, send_down, "gz")
+    far = lax.ppermute(send_far, "gz", [((i + 2) % nz, i) for i in range(nz)])
     gram_parts = lax.all_to_all(gram.reshape(nz, 512 // nz, 128), "gz", 0, 0)
     gram_sum = jnp.sum(gram_parts, axis=0)
-    grad_w, grad_feat, lam0, push_up, push_down = call(
+    grad_w, grad_feat, grad_field = call(
         stage_two,
-        [((64, 128), F32), ((16, 32, 128), BF16), ((4, 8, 128), F32), ((2, 8, 128), F32),
-         ((2, 8, 128), F32)],
+        [((64, 128), F32), ((16, 32, 128), BF16), ((4, 8, 128), F32)],
         [pltpu.VMEM((10, 24, 128), F32), pltpu.VMEM((7, 24, 128), F32),
          pltpu.VMEM((6, 384, 128), F32), pltpu.VMEM((3, 6, 160, 128), BF16),
          pltpu.VMEM((864, 1024), BF16), pltpu.VMEM((16, 512), F32), pltpu.VMEM((512, 128), F32)],
-        (below1, above1, u1_part, lam_part, face3, u0, lam2, velx, coef, columns_own, w_back, shift),
+        (below1, above1, far, state, coef, columns_own, w_back),
     )
     wr, gr = 64 // ny, 512 // nz
     mixed = jnp.concatenate(
@@ -435,8 +531,6 @@
     everyone = lax.all_to_all(jnp.broadcast_to(mixed[None], (nz, wr + gr, 128)), "gz", 0, 0)
     weight_sum = jnp.sum(everyone[:, :wr], axis=0)
     weight_all = lax.all_to_all(jnp.broadcast_to(weight_sum[None], (ny, wr, 128)), "gy", 0, 0)
-    low, high = neighbours(push_up, push_down, "gz")
-    grad_field = lam0 + jnp.concatenate([low, high], axis=0)
     (factor_patch,) = call(
         lambda *refs: finish_gram(1.0 / cells, *refs),
         [((432, 432), F32)],

time: 135 us -> 143 us (1.059)
  blocking collectives: 19.1 us -> 42.8 us
  Pallas kernels: 10.8 us -> 29.8 us
  starting transfers between devices: 60.5 us -> 45.7 us
  local copies, waits for them, and re-layouts: 19.1 us -> 4.98 us
  waiting for transfers between devices: 22.5 us -> 15.6 us
  other arithmetic: 0.76 us -> 2.52 us
    all_to_all x0 -> x1, blocking collectives: none -> 22.9 us  [body(): lax.all_to_all(jnp.broadcast_to(mixed[None], (nz, wr + gr, 128)), 'gz', 0...]
    pallas_call x6, Pallas kernels: 10.8 us -> 29.8 us  [the longest x5 18.3 us: call(): pl.pallas_call(run, out_shape=[jax.ShapeDtypeStruct(s, t) for s, t in out...]
    unnamed x44 -> x2, local copies, waits for them, and re-layouts: 15.1 us -> 0.6 us
    all_to_all x1 -> x0, starting transfers between devices: 10.2 us -> none  [body(): lax.all_to_all(jnp.broadcast_to(mixed[None], (nz, wr + gr, 128)), 'gz', 0...]
    ppermute x8 -> x6, starting transfers between devices: 39.8 us -> 30.3 us  [neighbours(): return (lax.ppermute(to_next, axis, up), lax.ppermute(to_prev, axis, down))]
    all_to_all x1 -> x0, waiting for transfers between devices: 6.37 us -> none  [body(): lax.all_to_all(jnp.broadcast_to(mixed[None], (nz, wr + gr, 128)), 'gz', 0...]
    ppermute x0 -> x1, starting transfers between devices: none -> 3.45 us  [body(): far = lax.ppermute(send_far, 'gz', [((i + 2) % nz, i) for i in range(nz)])]
    ppermute x8 -> x6, waiting for transfers between devices: 12 us -> 10.5 us  [neighbours(): return (lax.ppermute(to_next, axis, up), lax.ppermute(to_prev, axis, down))]
  transfers between devices with their start and end apart: 11 -> 9, of which waited for: 5 -> 4; matrix products, arithmetic and copies ran while one was open for 3% -> 3% of each run, Pallas kernels for 4% -> 6%
where the time goes in v2:
time: 143 us; the launch traced here: 142 us
  starting transfers between devices  45.7 us (32%)
  blocking collectives  42.8 us (30%)
  Pallas kernels  29.8 us (21%)
  waiting for transfers between devices  15.6 us (11%)
  local copies, waits for them, and re-layouts  4.98 us (3%)
  other arithmetic  2.52 us (2%)
    ppermute x6, starting transfers between devices, neighbours(): return (lax.ppermute(to_next, axis, up), lax.ppermute(to_prev, axis, down))  30.3 us
    all_to_all x1, blocking collectives, body(): lax.all_to_all(jnp.broadcast_to(mixed[None], (nz, wr + gr, 128)), 'gz', 0...  22.9 us
    all_to_all x1, blocking collectives, body(): mixed = jnp.sum(lax.all_to_all(mixed, 'gy', 0, 0), axis=0)  19.9 us
    pallas_call x5, Pallas kernels, call(): pl.pallas_call(run, out_shape=[jax.ShapeDtypeStruct(s, t) for s, t in out...  18.3 us
    pallas_call x1, Pallas kernels, body(): pl.pallas_call(pack_z, out_shape=[jax.ShapeDtypeStruct((ROWS_IN + 3 * (st...  11.5 us
    ppermute x6, waiting for transfers between devices, neighbours(): return (lax.ppermute(to_next, axis, up), lax.ppermute(to_prev, axis, down))  10.5 us
    all_to_all x1, starting transfers between devices, body(): lax.all_to_all(jnp.broadcast_to(weight_sum[None], (ny, wr, 128)), 'gy', 0...  6.45 us
    all_to_all x1, starting transfers between devices, body(): gram_parts = lax.all_to_all(gram.reshape(nz, 512 // nz, 128), 'gz', 0, 0)  5.47 us
  transfers between devices with their start and end apart: 9, of which 4 were waited for; matrix products, arithmetic and copies ran while one was open for 3% of the time, Pallas kernels for 6%

profile of v2, /device:TPU:1, one launch (start us, length us, event | category | flops | bytes accessed | tf_op | source)
XLA Modules:
  0.0 142.2 jit_solution(3447777682329333732)
XLA Ops:
  0.6 1.9 %shard_map.92 = (bf16[32,16,128]{2,1,0:T(8,128)(2,1)}, bf16[20,16,128]{2,1,0:T(8,128)(2,1)}, bf16[40,16,128]{2,1,0:T(8,128)(2,1)}, bf16[44,16,128]{2,1,0:T(8,128)(2,1)}) custom-call(bf16[16,32,128]{2,1,0:T(8,128)(2,1)} %bitcast.12, f32[4,8,128]{2,1,0:T(8,128)} %refs_5_.1, f32[3,4,8,128]{3,2,1,0:T(8,128)} %refs_6_.1, f32[4,8,128]{2,1,0:T(8,128)} %refs_7_.1), custom_call_target="tpu_custom_call" | custom-call | tf_op jit(solution)/shard_map/pallas_call | solution.py:53
  2.5 8.8 %collective-permute-start.1 = (bf16[44,16,128]{2,1,0:T(8,128)(2,1)}, bf16[44,16,128]{2,1,0:T(8,128)(2,1)}, u32[]{:S(2)}, u32[]{:S(2)}) collective-permute-start(bf16[44,16,128]{2,1,0:T(8,128)(2,1)} %get-tuple-element.25), channel_id=1, source_target_pairs={{1,0},{2,1},{3,2},{4,3},{5,4},{6,5},{7,6},{0,7},{9,8},{10,9},{11,1... | collective-permute-start | bytes 540680 | tf_op jit(solution)/shard_map/ppermute | solution.py:477
  11.3 1.9 %collective-permute-start = (bf16[40,16,128]{2,1,0:T(8,128)(2,1)}, bf16[40,16,128]{2,1,0:T(8,128)(2,1)}, u32[]{:S(2)}, u32[]{:S(2)}) collective-permute-start(bf16[40,16,128]{2,1,0:T(8,128)(2,1)} %get-tuple-element.24), channel_id=1, source_target_pairs={{0,1},{1,2},{2,3},{3,4},{4,5},{5,6},{6,7},{7,0},{8,9},{9,10},{10,1... | collective-permute-start | bytes 491528 | tf_op jit(solution)/shard_map/ppermute | solution.py:477
  13.3 4.3 %collective-permute-done.before.refs_1_ = bf16[40,16,128]{2,1,0:T(8,128)(2,1)} collective-permute-done((bf16[40,16,128]{2,1,0:T(8,128)(2,1)}, bf16[40,16,128]{2,1,0:T(8,128)(2,1)}, u32[]{:S(2)}, u32[]{:S(2)}) %collective-permute-start) | collective-permute-done | bytes 163872 | tf_op jit(solution)/shard_map/ppermute | solution.py:477
  17.6 0.0 collective-permute-done.1.after.refs_2_
  17.6 11.5 %shard_map.93 = (bf16[40,16,128]{2,1,0:T(8,128)(2,1)}, bf16[43,16,128]{2,1,0:T(8,128)(2,1)}) custom-call(bf16[32,16,128]{2,1,0:T(8,128)(2,1)} %get-tuple-element.23.own_feat.refs_0_, bf16[20,16,128]{2,1,0:T(8,128)(2,1)} %get-tuple-element.26.own_fields, bf16[40,16,128]{2,1,0:T(8,128)(2,1)} %collective-permute-done.before.refs_1_, ...), custom_call_target="tpu_custom_call" | custom-call | tf_op jit(solution)/shard_map/pallas_call | solution.py:495
  29.1 8.2 %collective-permute-start.3 = (bf16[43,16,128]{2,1,0:T(8,128)(2,1)}, bf16[43,16,128]{2,1,0:T(8,128)(2,1)}, u32[]{:S(2)}, u32[]{:S(2)}) collective-permute-start(bf16[43,16,128]{2,1,0:T(8,128)(2,1)} %get-tuple-element.28), channel_id=1, source_target_pairs={{8,0},{16,8},{24,16},{32,24},{40,32},{48,40},{56,48},{64,56},{72,6... | collective-permute-start | bytes 528392 | tf_op jit(solution)/shard_map/ppermute | solution.py:477
  37.3 1.9 %collective-permute-start.2 = (bf16[40,16,128]{2,1,0:T(8,128)(2,1)}, bf16[40,16,128]{2,1,0:T(8,128)(2,1)}, u32[]{:S(2)}, u32[]{:S(2)}) collective-permute-start(bf16[40,16,128]{2,1,0:T(8,128)(2,1)} %get-tuple-element.27), channel_id=1, source_target_pairs={{0,8},{8,16},{16,24},{24,32},{32,40},{40,48},{48,56},{56,64},{64,7... | collective-permute-start | bytes 491528 | tf_op jit(solution)/shard_map/ppermute | solution.py:477
  39.2 0.8 reshape.41
  40.1 0.0 copy-start
  40.1 0.6 copy-done
  40.7 0.2 copy.12
  40.9 0.8 reshape.42.refs_8_
  41.7 6.2 %collective-permute-done.2.refs_3_ = bf16[40,16,128]{2,1,0:T(8,128)(2,1)} collective-permute-done((bf16[40,16,128]{2,1,0:T(8,128)(2,1)}, bf16[40,16,128]{2,1,0:T(8,128)(2,1)}, u32[]{:S(2)}, u32[]{:S(2)}) %collective-permute-start.2) | collective-permute-done | bytes 163872 | tf_op jit(solution)/shard_map/ppermute | solution.py:477
  47.9 0.0 collective-permute-done.3.refs_4_
  47.9 6.6 %shard_map.94 = (f32[10,16,128]{2,1,0:T(8,128)}, f32[10,16,128]{2,1,0:T(8,128)}, f32[8,128]{1,0:T(8,128)}, f32[512,128]{1,0:T(8,128)}, bf16[864,1024]{1,0:T(8,12...) custom-call(bf16[32,16,128]{2,1,0:T(8,128)(2,1)} %get-tuple-element.23.own_feat.refs_0_, ...), custom_call_target="tpu_custom_call" | custom-call | tf_op jit(solution)/shard_map/pallas_call | solution.py:53
  54.5 5.5 %all-to-all-start = ((f32[64,8,128]{2,1,0:T(8,128)}), f32[64,8,128]{2,1,0:T(8,128)}, u32[]{:S(2)}, u32[]{:S(2)}) async-start(f32[64,8,128]{2,1,0:T(8,128)} %bitcast.11), calls=%async_computation | async-start | bytes 524288 | tf_op jit(solution)/shard_map/all_to_all | solution.py:516
  60.0 2.7 %collective-permute-start.4 = (f32[10,16,128]{2,1,0:T(8,128)}, f32[10,16,128]{2,1,0:T(8,128)}, u32[]{:S(2)}, u32[]{:S(2)}) collective-permute-start(f32[10,16,128]{2,1,0:T(8,128)} %get-tuple-element.29), channel_id=1, source_target_pairs={{0,8},{8,16},{16,24},{24,32},{32,40},{40,48},{48,56},{56,64},{64,7... | collective-permute-start | bytes 245768 | tf_op jit(solution)/shard_map/ppermute | solution.py:477
  62.7 6.8 %collective-permute-start.5 = (f32[10,16,128]{2,1,0:T(8,128)}, f32[10,16,128]{2,1,0:T(8,128)}, u32[]{:S(2)}, u32[]{:S(2)}) collective-permute-start(f32[10,16,128]{2,1,0:T(8,128)} %get-tuple-element.30), channel_id=1, source_target_pairs={{8,0},{16,8},{24,16},{32,24},{40,32},{48,40},{56,48},{64,56},{72,6... | collective-permute-start | bytes 245768 | tf_op jit(solution)/shard_map/ppermute | solution.py:477
  69.5 3.4 %collective-permute-start.6 = (f32[8,128]{1,0:T(8,128)}, f32[8,128]{1,0:T(8,128)}, u32[]{:S(2)}, u32[]{:S(2)}) collective-permute-start(f32[8,128]{1,0:T(8,128)} %get-tuple-element.31), channel_id=1, source_target_pairs={{16,0},{24,8},{32,16},{40,24},{48,32},{56,40},{64,48},{72,56},{80,... | collective-permute-start | bytes 12296 | tf_op jit(solution)/shard_map/ppermute | solution.py:515
  73.0 1.0 copy.13
  74.0 0.1 rev.3
  74.1 0.8 reshape.43.refs_6_
  74.9 1.2 collective-permute-done.6.refs_2_
  76.1 0.0 collective-permute-done.4.refs_0_
  76.1 0.0 collective-permute-done.5.refs_1_
  76.1 4.6 %shard_map.95 = (f32[64,128]{1,0:T(8,128)}, bf16[16,32,128]{2,1,0:T(8,128)(2,1)}, f32[4,8,128]{2,1,0:T(8,128)}) custom-call(f32[10,16,128]{2,1,0:T(8,128)} %collective-permute-done.4.refs_0_, f32[10,16,128]{2,1,0:T(8,128)} %collective-permute-done.5.refs_1_, f32[8,128]{1,0:T(8,128)} %collective-permute-done.6.refs_2_, ...), custom_call_target="tpu_custom_call" | custom-call | tf_op jit(solution)/shard_map/pallas_call | solution.py:53
  80.7 0.0 all-to-all-done
  80.7 1.0 reduce_sum.27
  81.7 0.8 pad_maximum_fusion
  82.5 19.9 %all_to_all.20 = f32[8,16,128]{2,1,0:T(8,128)S(1)} all-to-all(f32[8,16,128]{2,1,0:T(8,128)S(1)} %pad_maximum_fusion), channel_id=1, replica_groups=mesh['gz'=64,'gy'=8] {'gy'}, dimensions={0} | all-to-all | bytes 131072 | tf_op jit(solution)/shard_map/all_to_all | solution.py:530
  102.4 22.9 %all_to_all.21 = f32[64,16,128]{2,1,0:T(8,128)S(1)} all-to-all(f32[64,16,128]{2,1,0:T(8,128)S(1)} %broadcast_in_dim.7), channel_id=1, replica_groups=mesh['gz'=64,'gy'=8] {'gz'}, dimensions={0} | all-to-all | bytes 1048576 | tf_op jit(solution)/shard_map/all_to_all | solution.py:531
  125.4 0.7 slice_bitcast_fusion
  126.1 0.6 broadcast_in_dim.8
  126.7 6.4 %all-to-all-start.3 = ((f32[8,8,128]{2,1,0:T(8,128)}), f32[8,8,128]{2,1,0:T(8,128)}, u32[]{:S(2)}, u32[]{:S(2)}) async-start(f32[8,8,128]{2,1,0:T(8,128)} %broadcast_in_dim.8), calls=%async_computation.3 | async-start | bytes 65536 | tf_op jit(solution)/shard_map/all_to_all | solution.py:533
  133.2 3.4 %shard_map.97 = f32[432,432]{1,0:T(8,128)} custom-call(f32[512,128]{1,0:T(8,128)} %get-tuple-element.41.refs_0_), custom_call_target="tpu_custom_call" | custom-call | tf_op jit(solution)/shard_map/pallas_call | solution.py:53
  136.6 3.9 %all-to-all-done.3 = f32[8,8,128]{2,1,0:T(8,128)} async-done(((f32[8,8,128]{2,1,0:T(8,128)}), f32[8,8,128]{2,1,0:T(8,128)}, u32[]{:S(2)}, u32[]{:S(2)}) %all-to-all-start.3) | async-done | bytes 32800 | tf_op jit(solution)/shard_map/all_to_all | solution.py:533
  140.5 1.7 %shard_map.96 = (f32[16,432]{1,0:T(8,128)}, f32[16,16]{1,0:T(8,128)}) custom-call(f32[64,128]{1,0:T(8,128)} %bitcast.6.refs_0_), custom_call_target="tpu_custom_call" | custom-call | tf_op jit(solution)/shard_map/pallas_call | solution.py:53
  (3 shorter events, 0.1 us)
Async XLA Ops:
  2.5 15.0 %collective-permute-start.1 = (bf16[44,16,128]{2,1,0:T(8,128)(2,1)}, bf16[44,16,128]{2,1,0:T(8,128)(2,1)}, u32[]{:S(2)}, u32[]{:S(2)}) collective-permute-start(bf16[44,16,128]{2,1,0:T(8,128)(2,1)} %get-tuple-element.25), channel_id=1, source_target_pairs={{1,0},{2,1},{3,2},{4,3},{5,4},{6,5},{7,6},{0,7},{9,8},{10,9},{11,1... | collective-permute-start | bytes 540680 | tf_op jit(solution)/shard_map/ppermute | solution.py:477
  11.3 6.2 %collective-permute-start = (bf16[40,16,128]{2,1,0:T(8,128)(2,1)}, bf16[40,16,128]{2,1,0:T(8,128)(2,1)}, u32[]{:S(2)}, u32[]{:S(2)}) collective-permute-start(bf16[40,16,128]{2,1,0:T(8,128)(2,1)} %get-tuple-element.24), channel_id=1, source_target_pairs={{0,1},{1,2},{2,3},{3,4},{4,5},{5,6},{6,7},{7,0},{8,9},{9,10},{10,1... | collective-permute-start | bytes 491528 | tf_op jit(solution)/shard_map/ppermute | solution.py:477
  29.1 18.8 %collective-permute-start.3 = (bf16[43,16,128]{2,1,0:T(8,128)(2,1)}, bf16[43,16,128]{2,1,0:T(8,128)(2,1)}, u32[]{:S(2)}, u32[]{:S(2)}) collective-permute-start(bf16[43,16,128]{2,1,0:T(8,128)(2,1)} %get-tuple-element.28), channel_id=1, source_target_pairs={{8,0},{16,8},{24,16},{32,24},{40,32},{48,40},{56,48},{64,56},{72,6... | collective-permute-start | bytes 528392 | tf_op jit(solution)/shard_map/ppermute | solution.py:477
  37.3 10.6 %collective-permute-start.2 = (bf16[40,16,128]{2,1,0:T(8,128)(2,1)}, bf16[40,16,128]{2,1,0:T(8,128)(2,1)}, u32[]{:S(2)}, u32[]{:S(2)}) collective-permute-start(bf16[40,16,128]{2,1,0:T(8,128)(2,1)} %get-tuple-element.27), channel_id=1, source_target_pairs={{0,8},{8,16},{16,24},{24,32},{32,40},{40,48},{48,56},{56,64},{64,7... | collective-permute-start | bytes 491528 | tf_op jit(solution)/shard_map/ppermute | solution.py:477
  40.1 0.6 copy-start
  54.5 26.2 %all-to-all-start = ((f32[64,8,128]{2,1,0:T(8,128)}), f32[64,8,128]{2,1,0:T(8,128)}, u32[]{:S(2)}, u32[]{:S(2)}) async-start(f32[64,8,128]{2,1,0:T(8,128)} %bitcast.11), calls=%async_computation | async-start | bytes 524288 | tf_op jit(solution)/shard_map/all_to_all | solution.py:516
  60.0 16.1 %collective-permute-start.4 = (f32[10,16,128]{2,1,0:T(8,128)}, f32[10,16,128]{2,1,0:T(8,128)}, u32[]{:S(2)}, u32[]{:S(2)}) collective-permute-start(f32[10,16,128]{2,1,0:T(8,128)} %get-tuple-element.29), channel_id=1, source_target_pairs={{0,8},{8,16},{16,24},{24,32},{32,40},{40,48},{48,56},{56,64},{64,7... | collective-permute-start | bytes 245768 | tf_op jit(solution)/shard_map/ppermute | solution.py:477
  62.7 13.3 %collective-permute-start.5 = (f32[10,16,128]{2,1,0:T(8,128)}, f32[10,16,128]{2,1,0:T(8,128)}, u32[]{:S(2)}, u32[]{:S(2)}) collective-permute-start(f32[10,16,128]{2,1,0:T(8,128)} %get-tuple-element.30), channel_id=1, source_target_pairs={{8,0},{16,8},{24,16},{32,24},{40,32},{48,40},{56,48},{64,56},{72,6... | collective-permute-start | bytes 245768 | tf_op jit(solution)/shard_map/ppermute | solution.py:477
  69.5 6.6 %collective-permute-start.6 = (f32[8,128]{1,0:T(8,128)}, f32[8,128]{1,0:T(8,128)}, u32[]{:S(2)}, u32[]{:S(2)}) collective-permute-start(f32[8,128]{1,0:T(8,128)} %get-tuple-element.31), channel_id=1, source_target_pairs={{16,0},{24,8},{32,16},{40,24},{48,32},{56,40},{64,48},{72,56},{80,... | collective-permute-start | bytes 12296 | tf_op jit(solution)/shard_map/ppermute | solution.py:515
  126.7 13.8 %all-to-all-start.3 = ((f32[8,8,128]{2,1,0:T(8,128)}), f32[8,8,128]{2,1,0:T(8,128)}, u32[]{:S(2)}, u32[]{:S(2)}) async-start(f32[8,8,128]{2,1,0:T(8,128)} %broadcast_in_dim.8), calls=%async_computation.3 | async-start | bytes 65536 | tf_op jit(solution)/shard_map/all_to_all | solution.py:533

commit v3 on v2

--- a/solution.py
+++ b/solution.py
@@ -21,11 +21,13 @@
 _HBM = pl.BlockSpec(memory_space=pltpu.HBM)
 
 
-def call(kernel, outs, scratch, args):
+def call(kernel, outs, scratch, args, flops=1e6, follows=()):
     n_in, n_out = len(args), len(outs)
 
     def run(*refs):
-        source, target = refs[:n_in], refs[n_in : n_in + n_out]
+        source, refs = refs[:n_in], refs[n_in + len(follows) :]
+        target = refs[:n_out]
+        refs = (None,) * n_in + tuple(refs)
         arrived, left = refs[n_in + n_out : n_in + n_out + 2]
         held = refs[n_in + n_out + 2 :]
         here, there = held[:n_in], held[n_in : n_in + n_out]
@@ -53,13 +55,26 @@
     return pl.pallas_call(
         run,
         out_shape=[jax.ShapeDtypeStruct(s, t) for s, t in outs],
-        in_specs=[_HBM] * n_in,
+        in_specs=[_HBM] * (n_in + len(follows)),
         out_specs=[_HBM] * n_out,
         scratch_shapes=[pltpu.SemaphoreType.DMA((n_in,)), pltpu.SemaphoreType.DMA((n_out,))]
         + [pltpu.VMEM(a.shape, a.dtype) for a in args]
         + [pltpu.VMEM(s, t) for s, t in outs]
         + scratch,
         compiler_params=pltpu.CompilerParams(vmem_limit_bytes=64 * 1024 * 1024),
+        cost_estimate=pl.CostEstimate(flops=int(flops), bytes_accessed=4000000, transcendentals=0),
+    )(*args, *follows)
+
+
+def call_small(kernel, outs, scratch, args):
+    return pl.pallas_call(
+        kernel,
+        out_shape=[jax.ShapeDtypeStruct(s, t) for s, t in outs],
+        in_specs=[pl.BlockSpec(memory_space=pltpu.VMEM)] * len(args),
+        out_specs=[pl.BlockSpec(memory_space=pltpu.VMEM)] * len(outs),
+        scratch_shapes=scratch,
+        compiler_params=pltpu.CompilerParams(vmem_limit_bytes=16 * 1024 * 1024),
+        cost_estimate=pl.CostEstimate(flops=1000000, bytes_accessed=4000000, transcendentals=0),
     )(*args)
 
 
@@ -114,7 +129,7 @@
         to_prev[4 * NEXT + i] = tile
 
 
-def pack_z(own_feat, own_fields, before, after, to_up, to_down, moved):
+def pack_z(own_feat, own_fields, before, after, to_up, to_down, up, down, moved, left):
     copies = []
 
     def move(source, at, out, to, count):
@@ -124,7 +139,7 @@
             )
         )
 
-    for out, z, (first, stop) in ((to_up, 3, UP), (to_down, 0, DOWN)):
+    for out, z, (first, stop) in ((up, 3, UP), (down, 0, DOWN)):
         n = stop - first
         move(before, z * PREV, out, 0, PREV)
         move(own_feat, z * 8, out, PREV, 8)
@@ -134,8 +149,16 @@
         move(after, 4 * NEXT + first, out, ROWS_IN + 2 * n, n)
     for copy in copies:
         copy.start()
-    for copy in copies:
+    out_up = pltpu.make_async_copy(up, to_up, left.at[0])
+    out_down = pltpu.make_async_copy(down, to_down, left.at[1])
+    for copy in copies[:6]:
         copy.wait()
+    out_up.start()
+    for copy in copies[6:]:
+        copy.wait()
+    out_down.start()
+    out_up.wait()
+    out_down.wait()
 
 
 def fill_columns(columns, shifted, z, rows):
@@ -155,7 +178,7 @@
 
 def stage_one(
     need, done, own_feat, before, after, below, above, field, vel, cot, w_rows,
-    send_up, send_down, send_far, gram, columns_own, coef, kept,
+    send_up, send_down, send_far, columns_own, coef, kept,
     shifted, columns,
 ):
     u0, lam2 = kept.at[U0], kept.at[LAM2]
@@ -215,6 +238,8 @@
 
     lax.fori_loop(0, 6, fill, 0)
 
+    columns_own[...] = columns[:, 512:1536]
+    done(3)
     need(8)
     w_value = w_rows[...]
     for p in range(4):
@@ -224,20 +249,7 @@
         for y in range(ROWS_OUT):
             coef[p, (4 + y) * 16 : (5 + y) * 16, :] = plane[:, y * 128 : (y + 1) * 128]
 
-    total = None
-    for p in range(4):
-        part = lax.dot_general(
-            columns[p * 144 : (p + 1) * 144, 512:1536],
-            columns[p * 144 + 48 : p * 144 + 432, 512:1536],
-            NT,
-            preferred_element_type=F32,
-        )
-        total = part if total is None else total + part
-    for t in range(3):
-        gram[t * 144 : (t + 1) * 144, :] = total[:, t * 128 : (t + 1) * 128]
-    gram[432:, :] = jnp.zeros((gram.shape[0] - 432, 128), F32)
-    columns_own[...] = columns[:, 512:1536]
-    done(3, 4, 5)
+    done(4)
 
     def a(p, k):
         value = coef[p, pl.ds(k, 24, stride=16), :]
@@ -298,10 +310,26 @@
     send_far[...] = pushed[0][8:16]
 
 
+def patch_gram(need, done, columns_own, gram):
+    need(0)
+    total = None
+    for p in range(4):
+        part = lax.dot_general(
+            columns_own[p * 144 : (p + 1) * 144, :],
+            columns_own[p * 144 + 48 : p * 144 + 432, :],
+            NT,
+            preferred_element_type=F32,
+        )
+        total = part if total is None else total + part
+    for t in range(3):
+        gram[t * 144 : (t + 1) * 144, :] = total[:, t * 128 : (t + 1) * 128]
+    gram[432:, :] = jnp.zeros((gram.shape[0] - 432, 128), F32)
+
+
 def stage_two(
-    need, done, below, above, far, state, coef, columns_own, w_back,
-    grad_w, grad_feat, lam0,
-    u1, lam1, turn, shifted, columns, row, turn_out,
+    need, done, below, above, far, state, coef, columns_own,
+    grad_w, tiles, lam0,
+    u1, lam1, turn, row,
 ):
     u0, lam2, u1_part, lam_part = state.at[U0], state.at[LAM2], state.at[U1], state.at[LAM1]
     velx = [state.at[v] for v in VEL]
@@ -376,26 +404,16 @@
         lam0[p] = pushed[2 + p][own_rows] + edge[p]
     done(2)
 
-    shift_value = shift_both()
     for z in range(6):
-        tiles = turn[z, 7 * 16 : 17 * 16, :].astype(BF16)
-        shifted[1, z] = tiles
-        both = jnp.dot(tiles, shift_value, preferred_element_type=F32).astype(BF16)
-        shifted[0, z] = both[:, :128]
-        shifted[2, z] = both[:, 128:]
-
-    def fill(z, carry):
-        fill_columns(columns, shifted, z, 8)
-        return carry
-
-    lax.fori_loop(0, 6, fill, 0)
-
-    need(5, 6)
+        tiles[z] = turn[z, 7 * 16 : 17 * 16, :].astype(BF16)
+    done(1)
+    need(5)
     sum_w = None
     sum_g = None
     for p in range(4):
-        at = (p + 1) * 144 + 64
-        mine = columns[at : at + 16, :]
+        mine = jnp.concatenate(
+            [tiles[p + 1, (y + 1) * 16 : (y + 2) * 16, :] for y in range(8)], axis=1
+        )
         part_w = lax.dot_general(
             mine, columns_own[p * 144 : p * 144 + 432, :], NT, preferred_element_type=F32
         )
@@ -407,8 +425,23 @@
     row[:, 432:448] = sum_g
     for t in range(4):
         grad_w[t * 16 : (t + 1) * 16, :] = row[:, t * 128 : (t + 1) * 128]
-    done(0)
-
+
+
+def stage_three(need, done, tiles, w_back, grad_feat, shifted, columns, turn_out):
+    need(0)
+    shift_value = shift_both()
+    for z in range(6):
+        shifted[1, z] = tiles[z]
+        both = jnp.dot(tiles[z], shift_value, preferred_element_type=F32).astype(BF16)
+        shifted[0, z] = both[:, :128]
+        shifted[2, z] = both[:, 128:]
+
+    def fill(z, carry):
+        fill_columns(columns, shifted, z, 8)
+        return carry
+
+    lax.fori_loop(0, 6, fill, 0)
+    need(1)
     w_value = w_back[...]
     for p in range(4):
         plane = jnp.dot(
@@ -436,8 +469,7 @@
     return parts[2] + parts[1] + parts[0]
 
 
-def finish_gram(scale, need, done, chunks, out, square, block, turn):
-    need(0)
+def finish_gram(scale, chunks, out, square, block, turn):
     for t in range(3):
         square[0:144, 48 + t * 128 : 48 + (t + 1) * 128] = chunks[t * 144 : (t + 1) * 144, :] * scale
     square[0:48, 0:48] = square[48:96, 48:96]
@@ -462,8 +494,7 @@
         out[:, t * 128 : t * 128 + wide] = turn[t, :, 0:wide]
 
 
-def finish_weight(scale_w, scale_g, need, done, chunks, out_w, out_g, row):
-    need(0)
+def finish_weight(scale_w, scale_g, chunks, out_w, out_g, row):
     for t in range(4):
         row[:, t * 128 : (t + 1) * 128] = chunks[t * 16 : (t + 1) * 16, :]
     out_w[...] = to_channel_major(row[:, 0:432] * scale_w)
@@ -500,44 +531,55 @@
         ],
         in_specs=[_HBM] * 4,
         out_specs=[_HBM] * 2,
-        scratch_shapes=[pltpu.SemaphoreType.DMA((12,))],
+        scratch_shapes=[
+            pltpu.VMEM((ROWS_IN + 3 * (stop - first),) + tile, BF16) for first, stop in (UP, DOWN)
+        ]
+        + [pltpu.SemaphoreType.DMA((12,)), pltpu.SemaphoreType.DMA((2,))],
         compiler_params=pltpu.CompilerParams(vmem_limit_bytes=64 * 1024 * 1024),
     )(own_feat, own_fields, before, after)
     below, above = neighbours(to_up, to_down, "gz")
-    send_up, send_down, send_far, gram, columns_own, coef, state = call(
+    send_up, send_down, send_far, columns_own, coef, state = call(
         stage_one,
-        [((10, 16, 128), F32), ((10, 16, 128), F32), ((8, 128), F32), ((512, 128), F32),
-         ((864, 1024), BF16), ((4, 384, 128), F32), ((48, 24, 128), F32)],
+        [((10, 16, 128), F32), ((10, 16, 128), F32), ((8, 128), F32), ((864, 1024), BF16),
+         ((4, 384, 128), F32), ((48, 24, 128), F32)],
         [pltpu.VMEM((3, 6, ROWS_IN * 16, 128), BF16), pltpu.VMEM((864, ROWS_OUT * 128), BF16)],
         (own_feat, before, after, below, above, field, velocity, cotangent, w_rows),
     )
     below1, above1 = neighbours(send_up, send_down, "gz")
     far = lax.ppermute(send_far, "gz", [((i + 2) % nz, i) for i in range(nz)])
+    (gram,) = call(patch_gram, [((512, 128), F32)], [], (columns_own,), 5e8)
     gram_parts = lax.all_to_all(gram.reshape(nz, 512 // nz, 128), "gz", 0, 0)
     gram_sum = jnp.sum(gram_parts, axis=0)
-    grad_w, grad_feat, grad_field = call(
+    grad_w, tiles, grad_field = call(
         stage_two,
-        [((64, 128), F32), ((16, 32, 128), BF16), ((4, 8, 128), F32)],
+        [((64, 128), F32), ((6, 160, 128), BF16), ((4, 8, 128), F32)],
         [pltpu.VMEM((10, 24, 128), F32), pltpu.VMEM((7, 24, 128), F32),
-         pltpu.VMEM((6, 384, 128), F32), pltpu.VMEM((3, 6, 160, 128), BF16),
-         pltpu.VMEM((864, 1024), BF16), pltpu.VMEM((16, 512), F32), pltpu.VMEM((512, 128), F32)],
-        (below1, above1, far, state, coef, columns_own, w_back),
+         pltpu.VMEM((6, 384, 128), F32), pltpu.VMEM((16, 512), F32)],
+        (below1, above1, far, state, coef, columns_own),
     )
     wr, gr = 64 // ny, 512 // nz
     mixed = jnp.concatenate(
         [grad_w.reshape(ny, wr, 128), jnp.broadcast_to(gram_sum[None], (ny, gr, 128))], axis=1
+    )
+    (grad_feat,) = call(
+        stage_three,
+        [((16, 32, 128), BF16)],
+        [pltpu.VMEM((3, 6, 160, 128), BF16), pltpu.VMEM((864, 1024), BF16), pltpu.VMEM((512, 128), F32)],
+        (tiles, w_back),
+        1e8,
+        (mixed,),
     )
     mixed = jnp.sum(lax.all_to_all(mixed, "gy", 0, 0), axis=0)
     everyone = lax.all_to_all(jnp.broadcast_to(mixed[None], (nz, wr + gr, 128)), "gz", 0, 0)
     weight_sum = jnp.sum(everyone[:, :wr], axis=0)
     weight_all = lax.all_to_all(jnp.broadcast_to(weight_sum[None], (ny, wr, 128)), "gy", 0, 0)
-    (factor_patch,) = call(
+    (factor_patch,) = call_small(
         lambda *refs: finish_gram(1.0 / cells, *refs),
         [((432, 432), F32)],
         [pltpu.VMEM((432, 432), F32), pltpu.VMEM((256, 256), F32), pltpu.VMEM((4, 432, 128), F32)],
         (everyone[:, wr:].reshape(512, 128),),
     )
-    grad_weight, factor_grad = call(
+    grad_weight, factor_grad = call_small(
         lambda *refs: finish_weight(1.0 / math.sqrt(cells), 1.0 / cells, *refs),
         [((16, 432), F32), ((16, 16), F32)],
         [pltpu.VMEM((16, 512), F32)],

time: 143 us -> 135 us (0.944)
  Pallas kernels: 29.8 us -> 22.6 us
  waiting for transfers between devices: 15.6 us -> 13.6 us
    pallas_call x1, Pallas kernels: 11.5 us -> 1.72 us  [body(): pl.pallas_call(pack_z, out_shape=[jax.ShapeDtypeStruct((ROWS_IN + 3 * (st...]
    pallas_call x0 -> x2, Pallas kernels: none -> 4.17 us  [call_small(): pl.pallas_call(kernel, out_shape=[jax.ShapeDtypeStruct(s, t) for s, t in...]
    all_to_all x1, waiting for transfers between devices: 3.9 us -> 0.01 us  [body(): lax.all_to_all(jnp.broadcast_to(weight_sum[None], (ny, wr, 128)), 'gy', 0...]
    ppermute x1, waiting for transfers between devices: 1.19 us -> 3.11 us  [body(): far = lax.ppermute(send_far, 'gz', [((i + 2) % nz, i) for i in range(nz)])]
    unnamed x2 -> x8, local copies, waits for them, and re-layouts: 0.6 us -> 2.21 us
    pallas_call x5, Pallas kernels: 18.3 us -> 16.7 us  [call(): pl.pallas_call(run, out_shape=[jax.ShapeDtypeStruct(s, t) for s, t in out...]
  transfers between devices with their start and end apart: 9 -> 9, of which waited for: 4 -> 3; matrix products, arithmetic and copies ran while one was open for 3% -> 2% of each run, Pallas kernels for 6% -> 7%
where the time goes in v3:
time: 135 us; the launch traced here: 134 us
  starting transfers between devices  45.7 us (34%)
  blocking collectives  42.8 us (32%)
  Pallas kernels  22.6 us (17%)
  waiting for transfers between devices  13.6 us (10%)
  local copies, waits for them, and re-layouts  5.74 us (4%)
  other arithmetic  2.55 us (2%)
    ppermute x6, starting transfers between devices, neighbours(): return (lax.ppermute(to_next, axis, up), lax.ppermute(to_prev, axis, down))  30.3 us
    all_to_all x1, blocking collectives, body(): lax.all_to_all(jnp.broadcast_to(mixed[None], (nz, wr + gr, 128)), 'gz', 0...  22.9 us
    all_to_all x1, blocking collectives, body(): mixed = jnp.sum(lax.all_to_all(mixed, 'gy', 0, 0), axis=0)  19.9 us
    pallas_call x5, Pallas kernels, call(): pl.pallas_call(run, out_shape=[jax.ShapeDtypeStruct(s, t) for s, t in out...  16.7 us
    ppermute x6, waiting for transfers between devices, neighbours(): return (lax.ppermute(to_next, axis, up), lax.ppermute(to_prev, axis, down))  10.5 us
    all_to_all x1, starting transfers between devices, body(): lax.all_to_all(jnp.broadcast_to(weight_sum[None], (ny, wr, 128)), 'gy', 0...  6.45 us
    all_to_all x1, starting transfers between devices, body(): gram_parts = lax.all_to_all(gram.reshape(nz, 512 // nz, 128), 'gz', 0, 0)  5.48 us
    pallas_call x2, Pallas kernels, call_small(): pl.pallas_call(kernel, out_shape=[jax.ShapeDtypeStruct(s, t) for s, t in...  4.17 us
  transfers between devices with their start and end apart: 9, of which 3 were waited for; matrix products, arithmetic and copies ran while one was open for 2% of the time, Pallas kernels for 7%

profile of v3, /device:TPU:1, one launch (start us, length us, event | category | flops | bytes accessed | tf_op | source)
XLA Modules:
  0.0 133.9 jit_solution(5958361798073616467)
XLA Ops:
  0.6 1.9 %shard_map.92 = (bf16[32,16,128]{2,1,0:T(8,128)(2,1)}, bf16[20,16,128]{2,1,0:T(8,128)(2,1)}, bf16[40,16,128]{2,1,0:T(8,128)(2,1)}, bf16[44,16,128]{2,1,0:T(8,128)(2,1)}) custom-call(bf16[16,32,128]{2,1,0:T(8,128)(2,1)} %bitcast.13, f32[4,8,128]{2,1,0:T(8,128)} %refs_5_.1, f32[3,4,8,128]{3,2,1,0:T(8,128)} %refs_6_.1, f32[4,8,128]{2,1,0:T(8,128)} %refs_7_.1), custom_call_target="tpu_custom_call" | custom-call | flops 1000000 | bytes 4000000 | tf_op jit(solution)/shard_map/pallas_call | solution.py:55
  2.5 8.8 %collective-permute-start.1 = (bf16[44,16,128]{2,1,0:T(8,128)(2,1)}, bf16[44,16,128]{2,1,0:T(8,128)(2,1)}, u32[]{:S(2)}, u32[]{:S(2)}) collective-permute-start(bf16[44,16,128]{2,1,0:T(8,128)(2,1)} %get-tuple-element.24), channel_id=1, source_target_pairs={{1,0},{2,1},{3,2},{4,3},{5,4},{6,5},{7,6},{0,7},{9,8},{10,9},{11,1... | collective-permute-start | bytes 540680 | tf_op jit(solution)/shard_map/ppermute | solution.py:508
  11.3 1.9 %collective-permute-start = (bf16[40,16,128]{2,1,0:T(8,128)(2,1)}, bf16[40,16,128]{2,1,0:T(8,128)(2,1)}, u32[]{:S(2)}, u32[]{:S(2)}) collective-permute-start(bf16[40,16,128]{2,1,0:T(8,128)(2,1)} %get-tuple-element.23), channel_id=1, source_target_pairs={{0,1},{1,2},{2,3},{3,4},{4,5},{5,6},{6,7},{7,0},{8,9},{9,10},{10,1... | collective-permute-start | bytes 491528 | tf_op jit(solution)/shard_map/ppermute | solution.py:508
  13.3 4.3 %collective-permute-done.before.refs_1_ = bf16[40,16,128]{2,1,0:T(8,128)(2,1)} collective-permute-done((bf16[40,16,128]{2,1,0:T(8,128)(2,1)}, bf16[40,16,128]{2,1,0:T(8,128)(2,1)}, u32[]{:S(2)}, u32[]{:S(2)}) %collective-permute-start) | collective-permute-done | bytes 163872 | tf_op jit(solution)/shard_map/ppermute | solution.py:508
  17.6 0.0 collective-permute-done.1.after.refs_2_
  17.6 1.7 %shard_map.93 = (bf16[40,16,128]{2,1,0:T(8,128)(2,1)}, bf16[43,16,128]{2,1,0:T(8,128)(2,1)}) custom-call(bf16[32,16,128]{2,1,0:T(8,128)(2,1)} %get-tuple-element.22.own_feat.refs_0_, bf16[20,16,128]{2,1,0:T(8,128)(2,1)} %get-tuple-element.25.own_fields, bf16[40,16,128]{2,1,0:T(8,128)(2,1)} %collective-permute-done.before.refs_1_, ...), custom_call_target="tpu_custom_call" | custom-call | tf_op jit(solution)/shard_map/pallas_call | solution.py:526
  19.3 8.2 %collective-permute-start.3 = (bf16[43,16,128]{2,1,0:T(8,128)(2,1)}, bf16[43,16,128]{2,1,0:T(8,128)(2,1)}, u32[]{:S(2)}, u32[]{:S(2)}) collective-permute-start(bf16[43,16,128]{2,1,0:T(8,128)(2,1)} %get-tuple-element.27), channel_id=1, source_target_pairs={{8,0},{16,8},{24,16},{32,24},{40,32},{48,40},{56,48},{64,56},{72,6... | collective-permute-start | bytes 528392 | tf_op jit(solution)/shard_map/ppermute | solution.py:508
  27.5 1.9 %collective-permute-start.2 = (bf16[40,16,128]{2,1,0:T(8,128)(2,1)}, bf16[40,16,128]{2,1,0:T(8,128)(2,1)}, u32[]{:S(2)}, u32[]{:S(2)}) collective-permute-start(bf16[40,16,128]{2,1,0:T(8,128)(2,1)} %get-tuple-element.26), channel_id=1, source_target_pairs={{0,8},{8,16},{16,24},{24,32},{32,40},{40,48},{48,56},{56,64},{64,7... | collective-permute-start | bytes 491528 | tf_op jit(solution)/shard_map/ppermute | solution.py:508
  29.4 0.8 reshape.41
  30.3 0.0 copy-start.1
  30.3 0.6 copy-done.1
  30.9 0.2 copy.12
  31.1 0.8 reshape.42.refs_8_
  31.9 6.2 %collective-permute-done.2.refs_3_ = bf16[40,16,128]{2,1,0:T(8,128)(2,1)} collective-permute-done((bf16[40,16,128]{2,1,0:T(8,128)(2,1)}, bf16[40,16,128]{2,1,0:T(8,128)(2,1)}, u32[]{:S(2)}, u32[]{:S(2)}) %collective-permute-start.2) | collective-permute-done | bytes 163872 | tf_op jit(solution)/shard_map/ppermute | solution.py:508
  38.1 0.0 collective-permute-done.3.refs_4_
  38.1 4.8 %shard_map.94 = (f32[10,16,128]{2,1,0:T(8,128)}, f32[10,16,128]{2,1,0:T(8,128)}, f32[8,128]{1,0:T(8,128)}, bf16[864,1024]{1,0:T(8,128)(2,1)}, f32[4,384,128]{2,1,0:T(8,128)}, /*index=5*/f32[48,24,128]{2,1,0:T(8,128)}) custom-call(bf16[32,16,128]{2,1,0:T(8,128)(2,1)} %get-tuple-element.22.own_feat.refs_0_, ...), custom_call_target="tpu_custom_call" | custom-call | flops 1000000 | bytes 4000000 | tf_op jit(solution)/shard_map/pallas_call | solution.py:55
  42.9 3.3 %shard_map.96 = f32[512,128]{1,0:T(8,128)} custom-call(bf16[864,1024]{1,0:T(8,128)(2,1)} %get-tuple-element.33.refs_5_.refs_0_), custom_call_target="tpu_custom_call" | custom-call | flops 500000000 | bytes 4000000 | tf_op jit(solution)/shard_map/pallas_call | solution.py:55
  46.3 5.5 %all-to-all-start = ((f32[64,8,128]{2,1,0:T(8,128)}), f32[64,8,128]{2,1,0:T(8,128)}, u32[]{:S(2)}, u32[]{:S(2)}) async-start(f32[64,8,128]{2,1,0:T(8,128)} %bitcast.9), calls=%async_computation | async-start | bytes 524288 | tf_op jit(solution)/shard_map/all_to_all | solution.py:551
  51.8 2.7 %collective-permute-start.4 = (f32[10,16,128]{2,1,0:T(8,128)}, f32[10,16,128]{2,1,0:T(8,128)}, u32[]{:S(2)}, u32[]{:S(2)}) collective-permute-start(f32[10,16,128]{2,1,0:T(8,128)} %get-tuple-element.28), channel_id=1, source_target_pairs={{0,8},{8,16},{16,24},{24,32},{32,40},{40,48},{48,56},{56,64},{64,7... | collective-permute-start | bytes 245768 | tf_op jit(solution)/shard_map/ppermute | solution.py:508
  54.5 6.8 %collective-permute-start.5 = (f32[10,16,128]{2,1,0:T(8,128)}, f32[10,16,128]{2,1,0:T(8,128)}, u32[]{:S(2)}, u32[]{:S(2)}) collective-permute-start(f32[10,16,128]{2,1,0:T(8,128)} %get-tuple-element.29), channel_id=1, source_target_pairs={{8,0},{16,8},{24,16},{32,24},{40,32},{48,40},{56,48},{64,56},{72,6... | collective-permute-start | bytes 245768 | tf_op jit(solution)/shard_map/ppermute | solution.py:508
  61.3 3.4 %collective-permute-start.6 = (f32[8,128]{1,0:T(8,128)}, f32[8,128]{1,0:T(8,128)}, u32[]{:S(2)}, u32[]{:S(2)}) collective-permute-start(f32[8,128]{1,0:T(8,128)} %get-tuple-element.30), channel_id=1, source_target_pairs={{16,0},{24,8},{32,16},{40,24},{48,32},{56,40},{64,48},{72,56},{80,... | collective-permute-start | bytes 12296 | tf_op jit(solution)/shard_map/ppermute | solution.py:549
  64.7 3.1 %collective-permute-done.6.refs_2_ = f32[8,128]{1,0:T(8,128)} collective-permute-done((f32[8,128]{1,0:T(8,128)}, f32[8,128]{1,0:T(8,128)}, u32[]{:S(2)}, u32[]{:S(2)}) %collective-permute-start.6) | collective-permute-done | bytes 4128 | tf_op jit(solution)/shard_map/ppermute | solution.py:549
  67.8 0.0 collective-permute-done.4.refs_0_
  67.8 0.0 collective-permute-done.5.refs_1_
  67.8 3.9 %shard_map.95 = (f32[64,128]{1,0:T(8,128)}, bf16[6,160,128]{2,1,0:T(8,128)(2,1)}, f32[4,8,128]{2,1,0:T(8,128)}) custom-call(f32[10,16,128]{2,1,0:T(8,128)} %collective-permute-done.4.refs_0_, f32[10,16,128]{2,1,0:T(8,128)} %collective-permute-done.5.refs_1_, f32[8,128]{1,0:T(8,128)} %collective-permute-done.6.refs_2_, ...), custom_call_target="tpu_custom_call" | custom-call | flops 1000000 | bytes 4000000 | tf_op jit(solution)/shard_map/pallas_call | solution.py:55
  71.7 0.0 copy-start.2
  71.7 0.0 all-to-all-done
  71.7 1.1 reduce_sum.27
  72.8 0.8 pad_maximum_fusion.refs_2_
  73.6 0.0 copy-start.3
  73.6 0.6 copy-done.3
  74.2 19.9 %all_to_all.20 = f32[8,16,128]{2,1,0:T(8,128)S(1)} all-to-all(f32[8,16,128]{2,1,0:T(8,128)S(1)} %pad_maximum_fusion.refs_2_), channel_id=1, replica_groups=mesh['gz'=64,'gy'=8] {'gy'}, dimensions={0} | all-to-all | bytes 131072 | tf_op jit(solution)/shard_map/all_to_all | solution.py:572
  94.1 22.9 %all_to_all.21 = f32[64,16,128]{2,1,0:T(8,128)S(1)} all-to-all(f32[64,16,128]{2,1,0:T(8,128)S(1)} %broadcast_in_dim.7), channel_id=1, replica_groups=mesh['gz'=64,'gy'=8] {'gz'}, dimensions={0} | all-to-all | bytes 1048576 | tf_op jit(solution)/shard_map/all_to_all | solution.py:573
  117.1 0.7 slice_bitcast_fusion
  117.8 0.6 broadcast_in_dim.8
  118.4 6.5 %all-to-all-start.3 = ((f32[8,8,128]{2,1,0:T(8,128)}), f32[8,8,128]{2,1,0:T(8,128)}, u32[]{:S(2)}, u32[]{:S(2)}) async-start(f32[8,8,128]{2,1,0:T(8,128)} %broadcast_in_dim.8), calls=%async_computation.3 | async-start | bytes 65536 | tf_op jit(solution)/shard_map/all_to_all | solution.py:575
  124.9 0.0 copy-done.2
  124.9 0.2 copy.13
  125.1 0.1 rev.3
  125.2 0.8 reshape.43.refs_1_
  125.9 2.8 %shard_map.97 = bf16[16,32,128]{2,1,0:T(8,128)(2,1)} custom-call(bf16[6,160,128]{2,1,0:T(8,128)(2,1)} %get-tuple-element.35.refs_0_, bf16[16,432]{1,0:T(8,128)(2,1)} %reshape.43.refs_1_, f32[8,16,128]{2,1,0:T(8,128)} %copy-done.3), custom_call_target="tpu_custom_call" | custom-call | flops 100000000 | bytes 4000000 | tf_op jit(solution)/shard_map/pallas_call | solution.py:55
  128.8 0.0 copy-start
  128.8 0.9 copy-done
  129.7 2.5 %shard_map.99 = f32[432,432]{1,0:T(8,128)} custom-call(f32[512,128]{1,0:T(8,128)S(1)} %copy-done), custom_call_target="tpu_custom_call" | custom-call | flops 1000000 | bytes 4000000 | tf_op jit(solution)/shard_map/pallas_call | solution.py:70
  132.2 0.0 all-to-all-done.3
  132.2 1.7 %shard_map.98 = (f32[16,432]{1,0:T(8,128)}, f32[16,16]{1,0:T(8,128)}) custom-call(f32[64,128]{1,0:T(8,128)} %bitcast.6.refs_0_), custom_call_target="tpu_custom_call" | custom-call | flops 1000000 | bytes 4000000 | tf_op jit(solution)/shard_map/pallas_call | solution.py:70
  (3 shorter events, 0.1 us)
Async XLA Ops:
  2.5 15.0 %collective-permute-start.1 = (bf16[44,16,128]{2,1,0:T(8,128)(2,1)}, bf16[44,16,128]{2,1,0:T(8,128)(2,1)}, u32[]{:S(2)}, u32[]{:S(2)}) collective-permute-start(bf16[44,16,128]{2,1,0:T(8,128)(2,1)} %get-tuple-element.24), channel_id=1, source_target_pairs={{1,0},{2,1},{3,2},{4,3},{5,4},{6,5},{7,6},{0,7},{9,8},{10,9},{11,1... | collective-permute-start | bytes 540680 | tf_op jit(solution)/shard_map/ppermute | solution.py:508
  11.3 6.2 %collective-permute-start = (bf16[40,16,128]{2,1,0:T(8,128)(2,1)}, bf16[40,16,128]{2,1,0:T(8,128)(2,1)}, u32[]{:S(2)}, u32[]{:S(2)}) collective-permute-start(bf16[40,16,128]{2,1,0:T(8,128)(2,1)} %get-tuple-element.23), channel_id=1, source_target_pairs={{0,1},{1,2},{2,3},{3,4},{4,5},{5,6},{6,7},{7,0},{8,9},{9,10},{10,1... | collective-permute-start | bytes 491528 | tf_op jit(solution)/shard_map/ppermute | solution.py:508
  19.3 18.8 %collective-permute-start.3 = (bf16[43,16,128]{2,1,0:T(8,128)(2,1)}, bf16[43,16,128]{2,1,0:T(8,128)(2,1)}, u32[]{:S(2)}, u32[]{:S(2)}) collective-permute-start(bf16[43,16,128]{2,1,0:T(8,128)(2,1)} %get-tuple-element.27), channel_id=1, source_target_pairs={{8,0},{16,8},{24,16},{32,24},{40,32},{48,40},{56,48},{64,56},{72,6... | collective-permute-start | bytes 528392 | tf_op jit(solution)/shard_map/ppermute | solution.py:508
  27.5 10.6 %collective-permute-start.2 = (bf16[40,16,128]{2,1,0:T(8,128)(2,1)}, bf16[40,16,128]{2,1,0:T(8,128)(2,1)}, u32[]{:S(2)}, u32[]{:S(2)}) collective-permute-start(bf16[40,16,128]{2,1,0:T(8,128)(2,1)} %get-tuple-element.26), channel_id=1, source_target_pairs={{0,8},{8,16},{16,24},{24,32},{32,40},{40,48},{48,56},{56,64},{64,7... | collective-permute-start | bytes 491528 | tf_op jit(solution)/shard_map/ppermute | solution.py:508
  30.3 0.6 copy-start.1
  46.3 25.5 %all-to-all-start = ((f32[64,8,128]{2,1,0:T(8,128)}), f32[64,8,128]{2,1,0:T(8,128)}, u32[]{:S(2)}, u32[]{:S(2)}) async-start(f32[64,8,128]{2,1,0:T(8,128)} %bitcast.9), calls=%async_computation | async-start | bytes 524288 | tf_op jit(solution)/shard_map/all_to_all | solution.py:551
  51.8 16.1 %collective-permute-start.4 = (f32[10,16,128]{2,1,0:T(8,128)}, f32[10,16,128]{2,1,0:T(8,128)}, u32[]{:S(2)}, u32[]{:S(2)}) collective-permute-start(f32[10,16,128]{2,1,0:T(8,128)} %get-tuple-element.28), channel_id=1, source_target_pairs={{0,8},{8,16},{16,24},{24,32},{32,40},{40,48},{48,56},{56,64},{64,7... | collective-permute-start | bytes 245768 | tf_op jit(solution)/shard_map/ppermute | solution.py:508
  54.5 13.3 %collective-permute-start.5 = (f32[10,16,128]{2,1,0:T(8,128)}, f32[10,16,128]{2,1,0:T(8,128)}, u32[]{:S(2)}, u32[]{:S(2)}) collective-permute-start(f32[10,16,128]{2,1,0:T(8,128)} %get-tuple-element.29), channel_id=1, source_target_pairs={{8,0},{16,8},{24,16},{32,24},{40,32},{48,40},{56,48},{64,56},{72,6... | collective-permute-start | bytes 245768 | tf_op jit(solution)/shard_map/ppermute | solution.py:508
  61.3 6.6 %collective-permute-start.6 = (f32[8,128]{1,0:T(8,128)}, f32[8,128]{1,0:T(8,128)}, u32[]{:S(2)}, u32[]{:S(2)}) collective-permute-start(f32[8,128]{1,0:T(8,128)} %get-tuple-element.30), channel_id=1, source_target_pairs={{16,0},{24,8},{32,16},{40,24},{48,32},{56,40},{64,48},{72,56},{80,... | collective-permute-start | bytes 12296 | tf_op jit(solution)/shard_map/ppermute | solution.py:549
  71.7 53.1 %copy-start.2 = (bf16[16,16,27]{2,1,0:T(8,128)(2,1)S(1)}, bf16[16,16,27]{2,1,0:T(8,128)(2,1)}, u32[]{:S(2)}) copy-start(bf16[16,16,27]{2,1,0:T(8,128)(2,1)} %copy-done.1) | copy-start | bytes 41476
  73.6 0.6 copy-start.3
  118.4 13.8 %all-to-all-start.3 = ((f32[8,8,128]{2,1,0:T(8,128)}), f32[8,8,128]{2,1,0:T(8,128)}, u32[]{:S(2)}, u32[]{:S(2)}) async-start(f32[8,8,128]{2,1,0:T(8,128)} %broadcast_in_dim.8), calls=%async_computation.3 | async-start | bytes 65536 | tf_op jit(solution)/shard_map/all_to_all | solution.py:575
  128.8 1.0 copy-start

commit v4 on v3

--- a/solution.py
+++ b/solution.py
@@ -310,25 +310,43 @@
     send_far[...] = pushed[0][8:16]
 
 
-def patch_gram(need, done, columns_own, gram):
+def patch_gram(need, done, columns_own, gram, full, line):
     need(0)
     total = None
     for p in range(4):
         part = lax.dot_general(
             columns_own[p * 144 : (p + 1) * 144, :],
-            columns_own[p * 144 + 48 : p * 144 + 432, :],
+            columns_own[p * 144 : p * 144 + 432, :],
             NT,
             preferred_element_type=F32,
         )
         total = part if total is None else total + part
-    for t in range(3):
-        gram[t * 144 : (t + 1) * 144, :] = total[:, t * 128 : (t + 1) * 128]
-    gram[432:, :] = jnp.zeros((gram.shape[0] - 432, 128), F32)
+    full[:, 0:432] = total
+    line[...] = jnp.zeros((16, 1280), F32)
+
+    def put(dz, dy, dx, count, a, b, a_other):
+        to = dz * 400 + (dy + 2) * 80 + (dx + 2) * 16
+        at = dz * 144 + a_other * 48
+        group = (a * 3 + b) * 16
+        line[:, to : to + 16 * count] = full[group : group + 16, at : at + 16 * count]
+
+    for dz in range(3):
+        for a in range(3):
+            put(dz, a, 0, 3, 0, 0, a)
+            for b in (1, 2):
+                put(dz, a, -b, 1, 0, b, a)
+        for a in (1, 2):
+            put(dz, -a, 0, 3, a, 0, 0)
+            for b in (1, 2):
+                put(dz, -a, -b, 1, a, b, 0)
+    for t in range(10):
+        gram[t * 16 : (t + 1) * 16, :] = line[:, t * 128 : (t + 1) * 128]
+    gram[160:192, :] = jnp.zeros((32, 128), F32)
 
 
 def stage_two(
-    need, done, below, above, far, state, coef, columns_own,
-    grad_w, tiles, lam0,
+    need, done, below, above, far, state, coef, columns_own, gram,
+    mixed, tiles, lam0,
     u1, lam1, turn, row,
 ):
     u0, lam2, u1_part, lam_part = state.at[U0], state.at[LAM2], state.at[U1], state.at[LAM1]
@@ -423,8 +441,14 @@
     row[...] = jnp.zeros((16, 512), F32)
     row[:, 0:432] = sum_w
     row[:, 432:448] = sum_g
-    for t in range(4):
-        grad_w[t * 16 : (t + 1) * 16, :] = row[:, t * 128 : (t + 1) * 128]
+    parts = mixed.shape[0]
+    wr, gr = 64 // parts, 192 // parts
+    for r in range(0, 64, 8):
+        t, half = divmod(r, 16)
+        mixed[r // wr, r % wr : r % wr + 8, :] = row[half : half + 8, t * 128 : (t + 1) * 128]
+    need(6)
+    for n in range(parts):
+        mixed[n, wr : wr + gr, :] = gram[n * gr : (n + 1) * gr, :]
 
 
 def stage_three(need, done, tiles, w_back, grad_feat, shifted, columns, turn_out):
@@ -469,36 +493,53 @@
     return parts[2] + parts[1] + parts[0]
 
 
-def finish_gram(scale, chunks, out, square, block, turn):
-    for t in range(3):
-        square[0:144, 48 + t * 128 : 48 + (t + 1) * 128] = chunks[t * 144 : (t + 1) * 144, :] * scale
-    square[0:48, 0:48] = square[48:96, 48:96]
-    block[...] = jnp.zeros((256, 256), F32)
-    block[0:48, 0:96] = square[0:48, 48:144]
-    square[48:144, 0:48] = jnp.transpose(block[...])[0:96, 0:48]
+def total_to_all(parts, out):
+    total = parts[0]
+    for n in range(1, parts.shape[0]):
+        total = total + parts[n]
+    for n in range(out.shape[0]):
+        out[n] = total
+
+
+def finish(cells, chunks, out_w, out_p, out_g, line, row, square, block, turn):
+    parts = chunks.shape[0]
+    wr, gr = 64 // parts, 192 // parts
+    for r in range(0, 64, 8):
+        t, half = divmod(r, 16)
+        row[half : half + 8, t * 128 : (t + 1) * 128] = chunks[r // wr, r % wr : r % wr + 8, :]
+    for r in range(0, 160, 8):
+        t, half = divmod(r, 16)
+        line[half : half + 8, t * 128 : (t + 1) * 128] = chunks[
+            r // gr, wr + r % gr : wr + r % gr + 8, :
+        ] * (1.0 / cells)
+    out_g[...] = row[:, 432:448] * (1.0 / cells)
+    for dz in range(3):
+        for a in range(3):
+            for b in range(3):
+                group = (a * 3 + b) * 16
+                for a_other in range(3):
+                    to = dz * 144 + a_other * 48
+                    at = dz * 400 + (a_other - a + 2) * 80 + (2 - b) * 16
+                    square[group : group + 16, to : to + 48] = line[:, at : at + 48]
     square[144:288, 144:432] = square[0:144, 0:288]
     square[288:432, 288:432] = square[0:144, 0:144]
+    block[...] = jnp.zeros((256, 256), F32)
     block[0:144, 0:144] = square[0:144, 144:288]
     turned = jnp.transpose(block[...])[0:144, 0:144]
     square[144:288, 0:144] = turned
     square[288:432, 144:288] = turned
     block[0:144, 0:144] = square[0:144, 288:432]
     square[288:432, 0:144] = jnp.transpose(block[...])[0:144, 0:144]
+    square[432:448, :] = row[:, 0:432] * (1.0 / math.sqrt(cells))
     ready = to_channel_major(square[...])
+    out_w[...] = ready[432:448, :]
     for t in range(4):
         wide = min(128, 432 - t * 128)
         for o in range(27):
             turn[t, pl.ds(o, 16, stride=27), 0:wide] = ready[
                 o * 16 : (o + 1) * 16, t * 128 : t * 128 + wide
             ]
-        out[:, t * 128 : t * 128 + wide] = turn[t, :, 0:wide]
-
-
-def finish_weight(scale_w, scale_g, chunks, out_w, out_g, row):
-    for t in range(4):
-        row[:, t * 128 : (t + 1) * 128] = chunks[t * 16 : (t + 1) * 16, :]
-    out_w[...] = to_channel_major(row[:, 0:432] * scale_w)
-    out_g[...] = row[:, 432:448] * scale_g
+        out_p[:, t * 128 : t * 128 + wide] = turn[t, :, 0:wide]
 
 
 def neighbours(to_next, to_prev, axis):
@@ -547,19 +588,20 @@
     )
     below1, above1 = neighbours(send_up, send_down, "gz")
     far = lax.ppermute(send_far, "gz", [((i + 2) % nz, i) for i in range(nz)])
-    (gram,) = call(patch_gram, [((512, 128), F32)], [], (columns_own,), 5e8)
-    gram_parts = lax.all_to_all(gram.reshape(nz, 512 // nz, 128), "gz", 0, 0)
-    gram_sum = jnp.sum(gram_parts, axis=0)
-    grad_w, tiles, grad_field = call(
+    (gram,) = call(
+        patch_gram,
+        [((192, 128), F32)],
+        [pltpu.VMEM((144, 512), F32), pltpu.VMEM((16, 1280), F32)],
+        (columns_own,),
+        5e8,
+    )
+    rows = 256 // ny
+    mixed, tiles, grad_field = call(
         stage_two,
-        [((64, 128), F32), ((6, 160, 128), BF16), ((4, 8, 128), F32)],
+        [((ny, rows, 128), F32), ((6, 160, 128), BF16), ((4, 8, 128), F32)],
         [pltpu.VMEM((10, 24, 128), F32), pltpu.VMEM((7, 24, 128), F32),
          pltpu.VMEM((6, 384, 128), F32), pltpu.VMEM((16, 512), F32)],
-        (below1, above1, far, state, coef, columns_own),
-    )
-    wr, gr = 64 // ny, 512 // nz
-    mixed = jnp.concatenate(
-        [grad_w.reshape(ny, wr, 128), jnp.broadcast_to(gram_sum[None], (ny, gr, 128))], axis=1
+        (below1, above1, far, state, coef, columns_own, gram),
     )
     (grad_feat,) = call(
         stage_three,
@@ -569,21 +611,17 @@
         1e8,
         (mixed,),
     )
-    mixed = jnp.sum(lax.all_to_all(mixed, "gy", 0, 0), axis=0)
-    everyone = lax.all_to_all(jnp.broadcast_to(mixed[None], (nz, wr + gr, 128)), "gz", 0, 0)
-    weight_sum = jnp.sum(everyone[:, :wr], axis=0)
-    weight_all = lax.all_to_all(jnp.broadcast_to(weight_sum[None], (ny, wr, 128)), "gy", 0, 0)
-    (factor_patch,) = call_small(
-        lambda *refs: finish_gram(1.0 / cells, *refs),
-        [((432, 432), F32)],
-        [pltpu.VMEM((432, 432), F32), pltpu.VMEM((256, 256), F32), pltpu.VMEM((4, 432, 128), F32)],
-        (everyone[:, wr:].reshape(512, 128),),
-    )
-    grad_weight, factor_grad = call_small(
-        lambda *refs: finish_weight(1.0 / math.sqrt(cells), 1.0 / cells, *refs),
-        [((16, 432), F32), ((16, 16), F32)],
-        [pltpu.VMEM((16, 512), F32)],
-        (weight_all.reshape(64, 128),),
+    parts = lax.all_to_all(mixed, "gy", 0, 0)
+    (parts,) = call_small(total_to_all, [((nz, rows, 128), F32)], [], (parts,))
+    parts = lax.all_to_all(parts, "gz", 0, 0)
+    (parts,) = call_small(total_to_all, [((ny, rows, 128), F32)], [], (parts,))
+    parts = lax.all_to_all(parts, "gy", 0, 0)
+    grad_weight, factor_patch, factor_grad = call_small(
+        lambda *refs: finish(cells, *refs),
+        [((16, 432), F32), ((432, 432), F32), ((16, 16), F32)],
+        [pltpu.VMEM((16, 1280), F32), pltpu.VMEM((16, 512), F32), pltpu.VMEM((448, 432), F32),
+         pltpu.VMEM((256, 256), F32), pltpu.VMEM((4, 432, 128), F32)],
+        (parts,),
     )
     return (grad_field, grad_feat.reshape(16, 4, 8, 128), grad_weight, factor_patch, factor_grad)
 

time: 135 us -> 136 us (level)
  blocking collectives: 42.8 us -> 52.6 us
  starting transfers between devices: 45.7 us -> 39.2 us
  other arithmetic: 2.55 us -> 0 us
  local copies, waits for them, and re-layouts: 5.74 us -> 3.5 us
  waiting for transfers between devices: 13.6 us -> 15.6 us
    all_to_all x2, blocking collectives: 42.8 us -> 52.6 us  [the longest x1 30.8 us: body(): parts = lax.all_to_all(parts, 'gz', 0, 0)]
    all_to_all x2 -> x1, starting transfers between devices: 11.9 us -> 6.91 us  [body(): parts = lax.all_to_all(parts, 'gy', 0, 0)]
    all_to_all x2 -> x1, waiting for transfers between devices: 0.01 us -> 4.22 us  [body(): parts = lax.all_to_all(parts, 'gy', 0, 0)]
    ppermute x1, waiting for transfers between devices: 3.11 us -> 0.81 us  [body(): far = lax.ppermute(send_far, 'gz', [((i + 2) % nz, i) for i in range(nz)])]
    unnamed x8 -> x4, local copies, waits for them, and re-layouts: 2.21 us -> 0.61 us
    ppermute x1, starting transfers between devices: 3.45 us -> 1.92 us  [body(): far = lax.ppermute(send_far, 'gz', [((i + 2) % nz, i) for i in range(nz)])]
    pallas_call x2 -> x3, Pallas kernels: 4.17 us -> 4.26 us  [call_small(): pl.pallas_call(kernel, out_shape=[jax.ShapeDtypeStruct(s, t) for s, t in...]
  transfers between devices with their start and end apart: 9 -> 8, of which waited for: 3 -> 4; matrix products, arithmetic and copies ran while one was open for 2% -> 2% of each run, Pallas kernels for 7% -> 5%
where the time goes in v4:
time: 136 us; the launch traced here: 134 us
  blocking collectives  52.6 us (39%)
  starting transfers between devices  39.2 us (29%)
  Pallas kernels  22.9 us (17%)
  waiting for transfers between devices  15.6 us (11%)
  local copies, waits for them, and re-layouts  3.5 us (3%)
    all_to_all x1, blocking collectives, body(): parts = lax.all_to_all(parts, 'gz', 0, 0)  30.8 us
    ppermute x6, starting transfers between devices, neighbours(): return (lax.ppermute(to_next, axis, up), lax.ppermute(to_prev, axis, down))  30.3 us
    all_to_all x1, blocking collectives, body(): parts = lax.all_to_all(mixed, 'gy', 0, 0)  21.7 us
    pallas_call x5, Pallas kernels, call(): pl.pallas_call(run, out_shape=[jax.ShapeDtypeStruct(s, t) for s, t in out...  16.9 us
    ppermute x6, waiting for transfers between devices, neighbours(): return (lax.ppermute(to_next, axis, up), lax.ppermute(to_prev, axis, down))  10.5 us
    all_to_all x1, starting transfers between devices, body(): parts = lax.all_to_all(parts, 'gy', 0, 0)  6.91 us
    pallas_call x3, Pallas kernels, call_small(): pl.pallas_call(kernel, out_shape=[jax.ShapeDtypeStruct(s, t) for s, t in...  4.26 us
    all_to_all x1, waiting for transfers between devices, body(): parts = lax.all_to_all(parts, 'gy', 0, 0)  4.22 us
  transfers between devices with their start and end apart: 8, of which 4 were waited for; matrix products, arithmetic and copies ran while one was open for 2% of the time, Pallas kernels for 5%

profile of v4, /device:TPU:1, one launch (start us, length us, event | category | flops | bytes accessed | tf_op | source)
XLA Modules:
  0.0 134.5 jit_solution(3829829576075690600)
XLA Ops:
  0.6 1.9 %shard_map.92 = (bf16[32,16,128]{2,1,0:T(8,128)(2,1)}, bf16[20,16,128]{2,1,0:T(8,128)(2,1)}, bf16[40,16,128]{2,1,0:T(8,128)(2,1)}, bf16[44,16,128]{2,1,0:T(8,128)(2,1)}) custom-call(bf16[16,32,128]{2,1,0:T(8,128)(2,1)} %bitcast.6, f32[4,8,128]{2,1,0:T(8,128)} %refs_5_.1, f32[3,4,8,128]{3,2,1,0:T(8,128)} %refs_6_.1, f32[4,8,128]{2,1,0:T(8,128)} %refs_7_.1), custom_call_target="tpu_custom_call" | custom-call | flops 1000000 | bytes 4000000 | tf_op jit(solution)/shard_map/pallas_call | solution.py:55
  2.5 8.8 %collective-permute-start.1 = (bf16[44,16,128]{2,1,0:T(8,128)(2,1)}, bf16[44,16,128]{2,1,0:T(8,128)(2,1)}, u32[]{:S(2)}, u32[]{:S(2)}) collective-permute-start(bf16[44,16,128]{2,1,0:T(8,128)(2,1)} %get-tuple-element.25), channel_id=1, source_target_pairs={{1,0},{2,1},{3,2},{4,3},{5,4},{6,5},{7,6},{0,7},{9,8},{10,9},{11,1... | collective-permute-start | bytes 540680 | tf_op jit(solution)/shard_map/ppermute | solution.py:549
  11.3 1.9 %collective-permute-start = (bf16[40,16,128]{2,1,0:T(8,128)(2,1)}, bf16[40,16,128]{2,1,0:T(8,128)(2,1)}, u32[]{:S(2)}, u32[]{:S(2)}) collective-permute-start(bf16[40,16,128]{2,1,0:T(8,128)(2,1)} %get-tuple-element.24), channel_id=1, source_target_pairs={{0,1},{1,2},{2,3},{3,4},{4,5},{5,6},{6,7},{7,0},{8,9},{9,10},{10,1... | collective-permute-start | bytes 491528 | tf_op jit(solution)/shard_map/ppermute | solution.py:549
  13.3 4.3 %collective-permute-done.before.refs_1_ = bf16[40,16,128]{2,1,0:T(8,128)(2,1)} collective-permute-done((bf16[40,16,128]{2,1,0:T(8,128)(2,1)}, bf16[40,16,128]{2,1,0:T(8,128)(2,1)}, u32[]{:S(2)}, u32[]{:S(2)}) %collective-permute-start) | collective-permute-done | bytes 163872 | tf_op jit(solution)/shard_map/ppermute | solution.py:549
  17.6 0.0 collective-permute-done.1.after.refs_2_
  17.6 1.7 %shard_map.93 = (bf16[40,16,128]{2,1,0:T(8,128)(2,1)}, bf16[43,16,128]{2,1,0:T(8,128)(2,1)}) custom-call(bf16[32,16,128]{2,1,0:T(8,128)(2,1)} %get-tuple-element.23.own_feat.refs_0_, bf16[20,16,128]{2,1,0:T(8,128)(2,1)} %get-tuple-element.26.own_fields, bf16[40,16,128]{2,1,0:T(8,128)(2,1)} %collective-permute-done.before.refs_1_, ...), custom_call_target="tpu_custom_call" | custom-call | tf_op jit(solution)/shard_map/pallas_call | solution.py:567
  19.3 8.2 %collective-permute-start.3 = (bf16[43,16,128]{2,1,0:T(8,128)(2,1)}, bf16[43,16,128]{2,1,0:T(8,128)(2,1)}, u32[]{:S(2)}, u32[]{:S(2)}) collective-permute-start(bf16[43,16,128]{2,1,0:T(8,128)(2,1)} %get-tuple-element.28), channel_id=1, source_target_pairs={{8,0},{16,8},{24,16},{32,24},{40,32},{48,40},{56,48},{64,56},{72,6... | collective-permute-start | bytes 528392 | tf_op jit(solution)/shard_map/ppermute | solution.py:549
  27.5 1.9 %collective-permute-start.2 = (bf16[40,16,128]{2,1,0:T(8,128)(2,1)}, bf16[40,16,128]{2,1,0:T(8,128)(2,1)}, u32[]{:S(2)}, u32[]{:S(2)}) collective-permute-start(bf16[40,16,128]{2,1,0:T(8,128)(2,1)} %get-tuple-element.27), channel_id=1, source_target_pairs={{0,8},{8,16},{16,24},{24,32},{32,40},{40,48},{48,56},{56,64},{64,7... | collective-permute-start | bytes 491528 | tf_op jit(solution)/shard_map/ppermute | solution.py:549
  29.4 0.8 reshape.26
  30.3 0.0 copy-start
  30.3 0.6 copy-done
  30.9 0.2 copy.12
  31.1 0.8 reshape.27.refs_8_
  31.9 6.2 %collective-permute-done.2.refs_3_ = bf16[40,16,128]{2,1,0:T(8,128)(2,1)} collective-permute-done((bf16[40,16,128]{2,1,0:T(8,128)(2,1)}, bf16[40,16,128]{2,1,0:T(8,128)(2,1)}, u32[]{:S(2)}, u32[]{:S(2)}) %collective-permute-start.2) | collective-permute-done | bytes 163872 | tf_op jit(solution)/shard_map/ppermute | solution.py:549
  38.1 0.0 collective-permute-done.3.refs_4_
  38.1 4.8 %shard_map.94 = (f32[10,16,128]{2,1,0:T(8,128)}, f32[10,16,128]{2,1,0:T(8,128)}, f32[8,128]{1,0:T(8,128)}, bf16[864,1024]{1,0:T(8,128)(2,1)}, f32[4,384,128]{2,1,0:T(8,128)}, /*index=5*/f32[48,24,128]{2,1,0:T(8,128)}) custom-call(bf16[32,16,128]{2,1,0:T(8,128)(2,1)} %get-tuple-element.23.own_feat.refs_0_, ...), custom_call_target="tpu_custom_call" | custom-call | flops 1000000 | bytes 4000000 | tf_op jit(solution)/shard_map/pallas_call | solution.py:55
  42.9 1.9 %collective-permute-start.4 = (f32[10,16,128]{2,1,0:T(8,128)}, f32[10,16,128]{2,1,0:T(8,128)}, u32[]{:S(2)}, u32[]{:S(2)}) collective-permute-start(f32[10,16,128]{2,1,0:T(8,128)} %get-tuple-element.29), channel_id=1, source_target_pairs={{0,8},{8,16},{16,24},{24,32},{32,40},{40,48},{48,56},{56,64},{64,7... | collective-permute-start | bytes 245768 | tf_op jit(solution)/shard_map/ppermute | solution.py:549
  44.9 7.6 %collective-permute-start.5 = (f32[10,16,128]{2,1,0:T(8,128)}, f32[10,16,128]{2,1,0:T(8,128)}, u32[]{:S(2)}, u32[]{:S(2)}) collective-permute-start(f32[10,16,128]{2,1,0:T(8,128)} %get-tuple-element.30), channel_id=1, source_target_pairs={{8,0},{16,8},{24,16},{32,24},{40,32},{48,40},{56,48},{64,56},{72,6... | collective-permute-start | bytes 245768 | tf_op jit(solution)/shard_map/ppermute | solution.py:549
  52.5 1.9 %collective-permute-start.6 = (f32[8,128]{1,0:T(8,128)}, f32[8,128]{1,0:T(8,128)}, u32[]{:S(2)}, u32[]{:S(2)}) collective-permute-start(f32[8,128]{1,0:T(8,128)} %get-tuple-element.31), channel_id=1, source_target_pairs={{16,0},{24,8},{32,16},{40,24},{48,32},{56,40},{64,48},{72,56},{80,... | collective-permute-start | bytes 12296 | tf_op jit(solution)/shard_map/ppermute | solution.py:590
  54.4 3.4 %shard_map.95.refs_6_ = f32[192,128]{1,0:T(8,128)} custom-call(bf16[864,1024]{1,0:T(8,128)(2,1)} %get-tuple-element.34.refs_0_.refs_5_), custom_call_target="tpu_custom_call" | custom-call | flops 500000000 | bytes 4000000 | tf_op jit(solution)/shard_map/pallas_call | solution.py:55
  57.8 0.8 collective-permute-done.6.refs_2_
  58.6 0.0 collective-permute-done.4.refs_0_
  58.6 0.0 collective-permute-done.5.refs_1_
  58.6 3.9 %shard_map.96 = (f32[8,32,128]{2,1,0:T(8,128)}, bf16[6,160,128]{2,1,0:T(8,128)(2,1)}, f32[4,8,128]{2,1,0:T(8,128)}) custom-call(f32[10,16,128]{2,1,0:T(8,128)} %collective-permute-done.4.refs_0_, f32[10,16,128]{2,1,0:T(8,128)} %collective-permute-done.5.refs_1_, f32[8,128]{1,0:T(8,128)} %collective-permute-done.6.refs_2_, ...), custom_call_target="tpu_custom_call" | custom-call | flops 1000000 | bytes 4000000 | tf_op jit(solution)/shard_map/pallas_call | solution.py:55
  62.6 21.7 %all_to_all.15.parts = f32[8,32,128]{2,1,0:T(8,128)S(1)} all-to-all(f32[8,32,128]{2,1,0:T(8,128)} %get-tuple-element.37.refs_2_), channel_id=1, replica_groups=mesh['gz'=64,'gy'=8] {'gy'}, dimensions={0} | all-to-all | bytes 262144 | tf_op jit(solution)/shard_map/all_to_all | solution.py:614
  84.3 0.1 shard_map.98
  84.4 0.0 copy-start.1
  84.4 30.8 %all_to_all.16.parts = f32[64,32,128]{2,1,0:T(8,128)S(1)} all-to-all(f32[64,32,128]{2,1,0:T(8,128)S(1)} %shard_map.98), channel_id=1, replica_groups=mesh['gz'=64,'gy'=8] {'gz'}, dimensions={0} | all-to-all | bytes 2097152 | tf_op jit(solution)/shard_map/all_to_all | solution.py:616
  115.3 0.8 shard_map.99
  116.0 6.9 %all-to-all-start.2 = ((f32[8,32,128]{2,1,0:T(8,128)}), f32[8,32,128]{2,1,0:T(8,128)}, u32[]{:S(2)}, u32[]{:S(2)}) async-start(f32[8,32,128]{2,1,0:T(8,128)} %shard_map.99), calls=%async_computation.2 | async-start | bytes 262144 | tf_op jit(solution)/shard_map/all_to_all | solution.py:618
  122.9 0.0 copy-done.1
  122.9 0.2 copy.13
  123.1 0.1 rev.3
  123.2 0.8 reshape.28.refs_1_
  124.0 2.8 %shard_map.97 = bf16[16,32,128]{2,1,0:T(8,128)(2,1)} custom-call(bf16[6,160,128]{2,1,0:T(8,128)(2,1)} %get-tuple-element.36.refs_0_, bf16[16,432]{1,0:T(8,128)(2,1)} %reshape.28.refs_1_, f32[8,32,128]{2,1,0:T(8,128)} %get-tuple-element.37.refs_2_), custom_call_target="tpu_custom_call" | custom-call | flops 100000000 | bytes 4000000 | tf_op jit(solution)/shard_map/pallas_call | solution.py:55
  126.9 4.2 %all-to-all-done.2.refs_0_ = f32[8,32,128]{2,1,0:T(8,128)} async-done(((f32[8,32,128]{2,1,0:T(8,128)}), f32[8,32,128]{2,1,0:T(8,128)}, u32[]{:S(2)}, u32[]{:S(2)}) %all-to-all-start.2) | async-done | bytes 131104 | tf_op jit(solution)/shard_map/all_to_all | solution.py:618
  131.1 3.4 %shard_map.100 = (f32[16,432]{1,0:T(8,128)}, f32[432,432]{1,0:T(8,128)}, f32[16,16]{1,0:T(8,128)}) custom-call(f32[8,32,128]{2,1,0:T(8,128)} %all-to-all-done.2.refs_0_), custom_call_target="tpu_custom_call" | custom-call | flops 1000000 | bytes 4000000 | tf_op jit(solution)/shard_map/pallas_call | solution.py:70
Async XLA Ops:
  2.5 15.0 %collective-permute-start.1 = (bf16[44,16,128]{2,1,0:T(8,128)(2,1)}, bf16[44,16,128]{2,1,0:T(8,128)(2,1)}, u32[]{:S(2)}, u32[]{:S(2)}) collective-permute-start(bf16[44,16,128]{2,1,0:T(8,128)(2,1)} %get-tuple-element.25), channel_id=1, source_target_pairs={{1,0},{2,1},{3,2},{4,3},{5,4},{6,5},{7,6},{0,7},{9,8},{10,9},{11,1... | collective-permute-start | bytes 540680 | tf_op jit(solution)/shard_map/ppermute | solution.py:549
  11.3 6.2 %collective-permute-start = (bf16[40,16,128]{2,1,0:T(8,128)(2,1)}, bf16[40,16,128]{2,1,0:T(8,128)(2,1)}, u32[]{:S(2)}, u32[]{:S(2)}) collective-permute-start(bf16[40,16,128]{2,1,0:T(8,128)(2,1)} %get-tuple-element.24), channel_id=1, source_target_pairs={{0,1},{1,2},{2,3},{3,4},{4,5},{5,6},{6,7},{7,0},{8,9},{9,10},{10,1... | collective-permute-start | bytes 491528 | tf_op jit(solution)/shard_map/ppermute | solution.py:549
  19.3 18.8 %collective-permute-start.3 = (bf16[43,16,128]{2,1,0:T(8,128)(2,1)}, bf16[43,16,128]{2,1,0:T(8,128)(2,1)}, u32[]{:S(2)}, u32[]{:S(2)}) collective-permute-start(bf16[43,16,128]{2,1,0:T(8,128)(2,1)} %get-tuple-element.28), channel_id=1, source_target_pairs={{8,0},{16,8},{24,16},{32,24},{40,32},{48,40},{56,48},{64,56},{72,6... | collective-permute-start | bytes 528392 | tf_op jit(solution)/shard_map/ppermute | solution.py:549
  27.5 10.6 %collective-permute-start.2 = (bf16[40,16,128]{2,1,0:T(8,128)(2,1)}, bf16[40,16,128]{2,1,0:T(8,128)(2,1)}, u32[]{:S(2)}, u32[]{:S(2)}) collective-permute-start(bf16[40,16,128]{2,1,0:T(8,128)(2,1)} %get-tuple-element.27), channel_id=1, source_target_pairs={{0,8},{8,16},{16,24},{24,32},{32,40},{40,48},{48,56},{56,64},{64,7... | collective-permute-start | bytes 491528 | tf_op jit(solution)/shard_map/ppermute | solution.py:549
  30.3 0.6 copy-start
  42.9 15.7 %collective-permute-start.4 = (f32[10,16,128]{2,1,0:T(8,128)}, f32[10,16,128]{2,1,0:T(8,128)}, u32[]{:S(2)}, u32[]{:S(2)}) collective-permute-start(f32[10,16,128]{2,1,0:T(8,128)} %get-tuple-element.29), channel_id=1, source_target_pairs={{0,8},{8,16},{16,24},{24,32},{32,40},{40,48},{48,56},{56,64},{64,7... | collective-permute-start | bytes 245768 | tf_op jit(solution)/shard_map/ppermute | solution.py:549
  44.9 13.8 %collective-permute-start.5 = (f32[10,16,128]{2,1,0:T(8,128)}, f32[10,16,128]{2,1,0:T(8,128)}, u32[]{:S(2)}, u32[]{:S(2)}) collective-permute-start(f32[10,16,128]{2,1,0:T(8,128)} %get-tuple-element.30), channel_id=1, source_target_pairs={{8,0},{16,8},{24,16},{32,24},{40,32},{48,40},{56,48},{64,56},{72,6... | collective-permute-start | bytes 245768 | tf_op jit(solution)/shard_map/ppermute | solution.py:549
  52.5 6.2 %collective-permute-start.6 = (f32[8,128]{1,0:T(8,128)}, f32[8,128]{1,0:T(8,128)}, u32[]{:S(2)}, u32[]{:S(2)}) collective-permute-start(f32[8,128]{1,0:T(8,128)} %get-tuple-element.31), channel_id=1, source_target_pairs={{16,0},{24,8},{32,16},{40,24},{48,32},{56,40},{64,48},{72,56},{80,... | collective-permute-start | bytes 12296 | tf_op jit(solution)/shard_map/ppermute | solution.py:590
  84.4 38.5 %copy-start.1 = (bf16[16,16,27]{2,1,0:T(8,128)(2,1)S(1)}, bf16[16,16,27]{2,1,0:T(8,128)(2,1)}, u32[]{:S(2)}) copy-start(bf16[16,16,27]{2,1,0:T(8,128)(2,1)} %copy-done) | copy-start | bytes 41476
  116.0 15.1 %all-to-all-start.2 = ((f32[8,32,128]{2,1,0:T(8,128)}), f32[8,32,128]{2,1,0:T(8,128)}, u32[]{:S(2)}, u32[]{:S(2)}) async-start(f32[8,32,128]{2,1,0:T(8,128)} %shard_map.99), calls=%async_computation.2 | async-start | bytes 262144 | tf_op jit(solution)/shard_map/all_to_all | solution.py:618

commit v5 on v4

--- a/solution.py
+++ b/solution.py
@@ -441,14 +441,10 @@
     row[...] = jnp.zeros((16, 512), F32)
     row[:, 0:432] = sum_w
     row[:, 432:448] = sum_g
-    parts = mixed.shape[0]
-    wr, gr = 64 // parts, 192 // parts
-    for r in range(0, 64, 8):
-        t, half = divmod(r, 16)
-        mixed[r // wr, r % wr : r % wr + 8, :] = row[half : half + 8, t * 128 : (t + 1) * 128]
+    for t in range(4):
+        mixed[t * 16 : (t + 1) * 16, :] = row[:, t * 128 : (t + 1) * 128]
     need(6)
-    for n in range(parts):
-        mixed[n, wr : wr + gr, :] = gram[n * gr : (n + 1) * gr, :]
+    mixed[64:256, :] = gram[...]
 
 
 def stage_three(need, done, tiles, w_back, grad_feat, shifted, columns, turn_out):
@@ -502,16 +498,10 @@
 
 
 def finish(cells, chunks, out_w, out_p, out_g, line, row, square, block, turn):
-    parts = chunks.shape[0]
-    wr, gr = 64 // parts, 192 // parts
-    for r in range(0, 64, 8):
-        t, half = divmod(r, 16)
-        row[half : half + 8, t * 128 : (t + 1) * 128] = chunks[r // wr, r % wr : r % wr + 8, :]
-    for r in range(0, 160, 8):
-        t, half = divmod(r, 16)
-        line[half : half + 8, t * 128 : (t + 1) * 128] = chunks[
-            r // gr, wr + r % gr : wr + r % gr + 8, :
-        ] * (1.0 / cells)
+    for t in range(4):
+        row[:, t * 128 : (t + 1) * 128] = chunks[t * 16 : (t + 1) * 16, :]
+    for t in range(10):
+        line[:, t * 128 : (t + 1) * 128] = chunks[64 + t * 16 : 80 + t * 16, :] * (1.0 / cells)
     out_g[...] = row[:, 432:448] * (1.0 / cells)
     for dz in range(3):
         for a in range(3):
@@ -595,10 +585,9 @@
         (columns_own,),
         5e8,
     )
-    rows = 256 // ny
     mixed, tiles, grad_field = call(
         stage_two,
-        [((ny, rows, 128), F32), ((6, 160, 128), BF16), ((4, 8, 128), F32)],
+        [((256, 128), F32), ((6, 160, 128), BF16), ((4, 8, 128), F32)],
         [pltpu.VMEM((10, 24, 128), F32), pltpu.VMEM((7, 24, 128), F32),
          pltpu.VMEM((6, 384, 128), F32), pltpu.VMEM((16, 512), F32)],
         (below1, above1, far, state, coef, columns_own, gram),
@@ -611,11 +600,17 @@
         1e8,
         (mixed,),
     )
-    parts = lax.all_to_all(mixed, "gy", 0, 0)
-    (parts,) = call_small(total_to_all, [((nz, rows, 128), F32)], [], (parts,))
-    parts = lax.all_to_all(parts, "gz", 0, 0)
-    (parts,) = call_small(total_to_all, [((ny, rows, 128), F32)], [], (parts,))
-    parts = lax.all_to_all(parts, "gy", 0, 0)
+    half = nz // 2
+    line = [[(h * half + i) * ny + j for h in range(2) for j in range(ny)] for i in range(half)]
+    plane = [[(h * half + i) * ny + j for i in range(half)] for h in range(2) for j in range(ny)]
+    rows = 256 // len(line[0])
+    axes = ("gz", "gy")
+    parts = mixed.reshape(2 * ny, rows, 128)
+    parts = lax.all_to_all(parts, axes, 0, 0, axis_index_groups=line)
+    (parts,) = call_small(total_to_all, [((half, rows, 128), F32)], [], (parts,))
+    parts = lax.all_to_all(parts, axes, 0, 0, axis_index_groups=plane)
+    (parts,) = call_small(total_to_all, [((2 * ny, rows, 128), F32)], [], (parts,))
+    parts = lax.all_to_all(parts, axes, 0, 0, axis_index_groups=line).reshape(256, 128)
     grad_weight, factor_patch, factor_grad = call_small(
         lambda *refs: finish(cells, *refs),
         [((16, 432), F32), ((432, 432), F32), ((16, 16), F32)],

time: 136 us -> 121 us (0.89)
  blocking collectives: 52.6 us -> 39 us
  starting transfers between devices: 39.2 us -> 37.5 us
    all_to_all x2, blocking collectives: 52.6 us -> 39 us  [the longest x1 22.2 us: body(): parts = lax.all_to_all(parts, axes, 0, 0, axis_index_groups=line)]
    all_to_all x1, starting transfers between devices: 6.91 us -> 5.27 us  [body(): lax.all_to_all(parts, axes, 0, 0, axis_index_groups=line).reshape(256, 128)]
where the time goes in v5:
time: 121 us; the launch traced here: 120 us
  blocking collectives  39 us (32%)
  starting transfers between devices  37.5 us (31%)
  Pallas kernels  22.7 us (19%)
  waiting for transfers between devices  16.6 us (14%)
  local copies, waits for them, and re-layouts  3.5 us (3%)
    ppermute x6, starting transfers between devices, neighbours(): return (lax.ppermute(to_next, axis, up), lax.ppermute(to_prev, axis, down))  30.3 us
    all_to_all x1, blocking collectives, body(): parts = lax.all_to_all(parts, axes, 0, 0, axis_index_groups=line)  22.2 us
    pallas_call x5, Pallas kernels, call(): pl.pallas_call(run, out_shape=[jax.ShapeDtypeStruct(s, t) for s, t in out...  16.9 us
    all_to_all x1, blocking collectives, body(): parts = lax.all_to_all(parts, axes, 0, 0, axis_index_groups=plane)  16.8 us
    ppermute x6, waiting for transfers between devices, neighbours(): return (lax.ppermute(to_next, axis, up), lax.ppermute(to_prev, axis, down))  10.5 us
    all_to_all x1, starting transfers between devices, body(): lax.all_to_all(parts, axes, 0, 0, axis_index_groups=line).reshape(256, 128)  5.27 us
    all_to_all x1, waiting for transfers between devices, body(): lax.all_to_all(parts, axes, 0, 0, axis_index_groups=line).reshape(256, 128)  5.27 us
    pallas_call x3, Pallas kernels, call_small(): pl.pallas_call(kernel, out_shape=[jax.ShapeDtypeStruct(s, t) for s, t in...  4.11 us
  transfers between devices with their start and end apart: 8, of which 4 were waited for; matrix products, arithmetic and copies ran while one was open for 2% of the time, Pallas kernels for 5%

profile of v5, /device:TPU:1, one launch (start us, length us, event | category | flops | bytes accessed | tf_op | source)
XLA Modules:
  0.0 120.2 jit_solution(4019712213209818440)
XLA Ops:
  0.6 1.9 %shard_map.92 = (bf16[32,16,128]{2,1,0:T(8,128)(2,1)}, bf16[20,16,128]{2,1,0:T(8,128)(2,1)}, bf16[40,16,128]{2,1,0:T(8,128)(2,1)}, bf16[44,16,128]{2,1,0:T(8,128)(2,1)}) custom-call(bf16[16,32,128]{2,1,0:T(8,128)(2,1)} %bitcast.9, f32[4,8,128]{2,1,0:T(8,128)} %refs_5_.1, f32[3,4,8,128]{3,2,1,0:T(8,128)} %refs_6_.1, f32[4,8,128]{2,1,0:T(8,128)} %refs_7_.1), custom_call_target="tpu_custom_call" | custom-call | flops 1000000 | bytes 4000000 | tf_op jit(solution)/shard_map/pallas_call | solution.py:55
  2.5 8.8 %collective-permute-start.1 = (bf16[44,16,128]{2,1,0:T(8,128)(2,1)}, bf16[44,16,128]{2,1,0:T(8,128)(2,1)}, u32[]{:S(2)}, u32[]{:S(2)}) collective-permute-start(bf16[44,16,128]{2,1,0:T(8,128)(2,1)} %get-tuple-element.25), channel_id=1, source_target_pairs={{1,0},{2,1},{3,2},{4,3},{5,4},{6,5},{7,6},{0,7},{9,8},{10,9},{11,1... | collective-permute-start | bytes 540680 | tf_op jit(solution)/shard_map/ppermute | solution.py:539
  11.3 1.9 %collective-permute-start = (bf16[40,16,128]{2,1,0:T(8,128)(2,1)}, bf16[40,16,128]{2,1,0:T(8,128)(2,1)}, u32[]{:S(2)}, u32[]{:S(2)}) collective-permute-start(bf16[40,16,128]{2,1,0:T(8,128)(2,1)} %get-tuple-element.24), channel_id=1, source_target_pairs={{0,1},{1,2},{2,3},{3,4},{4,5},{5,6},{6,7},{7,0},{8,9},{9,10},{10,1... | collective-permute-start | bytes 491528 | tf_op jit(solution)/shard_map/ppermute | solution.py:539
  13.3 4.3 %collective-permute-done.before.refs_1_ = bf16[40,16,128]{2,1,0:T(8,128)(2,1)} collective-permute-done((bf16[40,16,128]{2,1,0:T(8,128)(2,1)}, bf16[40,16,128]{2,1,0:T(8,128)(2,1)}, u32[]{:S(2)}, u32[]{:S(2)}) %collective-permute-start) | collective-permute-done | bytes 163872 | tf_op jit(solution)/shard_map/ppermute | solution.py:539
  17.6 0.0 collective-permute-done.1.after.refs_2_
  17.6 1.7 %shard_map.93 = (bf16[40,16,128]{2,1,0:T(8,128)(2,1)}, bf16[43,16,128]{2,1,0:T(8,128)(2,1)}) custom-call(bf16[32,16,128]{2,1,0:T(8,128)(2,1)} %get-tuple-element.23.own_feat.refs_0_, bf16[20,16,128]{2,1,0:T(8,128)(2,1)} %get-tuple-element.26.own_fields, bf16[40,16,128]{2,1,0:T(8,128)(2,1)} %collective-permute-done.before.refs_1_, ...), custom_call_target="tpu_custom_call" | custom-call | tf_op jit(solution)/shard_map/pallas_call | solution.py:557
  19.3 8.2 %collective-permute-start.3 = (bf16[43,16,128]{2,1,0:T(8,128)(2,1)}, bf16[43,16,128]{2,1,0:T(8,128)(2,1)}, u32[]{:S(2)}, u32[]{:S(2)}) collective-permute-start(bf16[43,16,128]{2,1,0:T(8,128)(2,1)} %get-tuple-element.28), channel_id=1, source_target_pairs={{8,0},{16,8},{24,16},{32,24},{40,32},{48,40},{56,48},{64,56},{72,6... | collective-permute-start | bytes 528392 | tf_op jit(solution)/shard_map/ppermute | solution.py:539
  27.5 1.9 %collective-permute-start.2 = (bf16[40,16,128]{2,1,0:T(8,128)(2,1)}, bf16[40,16,128]{2,1,0:T(8,128)(2,1)}, u32[]{:S(2)}, u32[]{:S(2)}) collective-permute-start(bf16[40,16,128]{2,1,0:T(8,128)(2,1)} %get-tuple-element.27), channel_id=1, source_target_pairs={{0,8},{8,16},{16,24},{24,32},{32,40},{40,48},{48,56},{56,64},{64,7... | collective-permute-start | bytes 491528 | tf_op jit(solution)/shard_map/ppermute | solution.py:539
  29.4 0.8 reshape.32
  30.3 0.0 copy-start
  30.3 0.6 copy-done
  30.9 0.2 copy.12
  31.1 0.8 reshape.33.refs_8_
  31.9 6.2 %collective-permute-done.2.refs_3_ = bf16[40,16,128]{2,1,0:T(8,128)(2,1)} collective-permute-done((bf16[40,16,128]{2,1,0:T(8,128)(2,1)}, bf16[40,16,128]{2,1,0:T(8,128)(2,1)}, u32[]{:S(2)}, u32[]{:S(2)}) %collective-permute-start.2) | collective-permute-done | bytes 163872 | tf_op jit(solution)/shard_map/ppermute | solution.py:539
  38.1 0.0 collective-permute-done.3.refs_4_
  38.1 4.8 %shard_map.94 = (f32[10,16,128]{2,1,0:T(8,128)}, f32[10,16,128]{2,1,0:T(8,128)}, f32[8,128]{1,0:T(8,128)}, bf16[864,1024]{1,0:T(8,128)(2,1)}, f32[4,384,128]{2,1,0:T(8,128)}, /*index=5*/f32[48,24,128]{2,1,0:T(8,128)}) custom-call(bf16[32,16,128]{2,1,0:T(8,128)(2,1)} %get-tuple-element.23.own_feat.refs_0_, ...), custom_call_target="tpu_custom_call" | custom-call | flops 1000000 | bytes 4000000 | tf_op jit(solution)/shard_map/pallas_call | solution.py:55
  42.9 1.9 %collective-permute-start.4 = (f32[10,16,128]{2,1,0:T(8,128)}, f32[10,16,128]{2,1,0:T(8,128)}, u32[]{:S(2)}, u32[]{:S(2)}) collective-permute-start(f32[10,16,128]{2,1,0:T(8,128)} %get-tuple-element.29), channel_id=1, source_target_pairs={{0,8},{8,16},{16,24},{24,32},{32,40},{40,48},{48,56},{56,64},{64,7... | collective-permute-start | bytes 245768 | tf_op jit(solution)/shard_map/ppermute | solution.py:539
  44.9 7.6 %collective-permute-start.5 = (f32[10,16,128]{2,1,0:T(8,128)}, f32[10,16,128]{2,1,0:T(8,128)}, u32[]{:S(2)}, u32[]{:S(2)}) collective-permute-start(f32[10,16,128]{2,1,0:T(8,128)} %get-tuple-element.30), channel_id=1, source_target_pairs={{8,0},{16,8},{24,16},{32,24},{40,32},{48,40},{56,48},{64,56},{72,6... | collective-permute-start | bytes 245768 | tf_op jit(solution)/shard_map/ppermute | solution.py:539
  52.5 1.9 %collective-permute-start.6 = (f32[8,128]{1,0:T(8,128)}, f32[8,128]{1,0:T(8,128)}, u32[]{:S(2)}, u32[]{:S(2)}) collective-permute-start(f32[8,128]{1,0:T(8,128)} %get-tuple-element.31), channel_id=1, source_target_pairs={{16,0},{24,8},{32,16},{40,24},{48,32},{56,40},{64,48},{72,56},{80,... | collective-permute-start | bytes 12296 | tf_op jit(solution)/shard_map/ppermute | solution.py:580
  54.4 3.4 %shard_map.95.refs_6_ = f32[192,128]{1,0:T(8,128)} custom-call(bf16[864,1024]{1,0:T(8,128)(2,1)} %get-tuple-element.34.refs_0_.refs_5_), custom_call_target="tpu_custom_call" | custom-call | flops 500000000 | bytes 4000000 | tf_op jit(solution)/shard_map/pallas_call | solution.py:55
  57.8 0.8 collective-permute-done.6.refs_2_
  58.6 0.0 collective-permute-done.4.refs_0_
  58.6 0.0 collective-permute-done.5.refs_1_
  58.6 3.9 %shard_map.96 = (f32[256,128]{1,0:T(8,128)}, bf16[6,160,128]{2,1,0:T(8,128)(2,1)}, f32[4,8,128]{2,1,0:T(8,128)}) custom-call(f32[10,16,128]{2,1,0:T(8,128)} %collective-permute-done.4.refs_0_, f32[10,16,128]{2,1,0:T(8,128)} %collective-permute-done.5.refs_1_, f32[8,128]{1,0:T(8,128)} %collective-permute-done.6.refs_2_, ...), custom_call_target="tpu_custom_call" | custom-call | flops 1000000 | bytes 4000000 | tf_op jit(solution)/shard_map/pallas_call | solution.py:55
  62.6 0.0 copy-start.1
  62.6 22.2 %all_to_all.15.parts = f32[16,16,128]{2,1,0:T(8,128)S(1)} all-to-all(f32[16,16,128]{2,1,0:T(8,128)} %bitcast.8), channel_id=1, replica_groups={{0,1,2,3,4,5,6,7,256,257,258,259,260,261,262,263},{8,9,10,11,12,13,14,1..., dimensions={0} | all-to-all | bytes 262144 | tf_op jit(solution)/shard_map/all_to_all | solution.py:609
  84.9 16.8 %all_to_all.16.parts = f32[32,16,128]{2,1,0:T(8,128)S(1)} all-to-all(f32[32,16,128]{2,1,0:T(8,128)S(1)} %shard_map.98), channel_id=1, replica_groups={{0,8,16,24,32,40,48,56,64,72,80,88,96,104,112,120,128,136,144,152,160,1..., dimensions={0} | all-to-all | bytes 524288 | tf_op jit(solution)/shard_map/all_to_all | solution.py:611
  101.6 0.7 shard_map.99
  102.3 5.3 %all-to-all-start.2 = ((f32[16,16,128]{2,1,0:T(8,128)}), f32[16,16,128]{2,1,0:T(8,128)}, u32[]{:S(2)}, u32[]{:S(2)}) async-start(f32[16,16,128]{2,1,0:T(8,128)} %shard_map.99), calls=%async_computation.2 | async-start | bytes 262144 | tf_op jit(solution)/shard_map/all_to_all | solution.py:613
  107.6 0.0 copy-done.1
  107.6 0.2 copy.13
  107.8 0.1 rev.3
  107.9 0.8 reshape.34.refs_1_
  108.7 2.8 %shard_map.97 = bf16[16,32,128]{2,1,0:T(8,128)(2,1)} custom-call(bf16[6,160,128]{2,1,0:T(8,128)(2,1)} %get-tuple-element.36.refs_0_, bf16[16,432]{1,0:T(8,128)(2,1)} %reshape.34.refs_1_, f32[256,128]{1,0:T(8,128)} %get-tuple-element.37.refs_2_), custom_call_target="tpu_custom_call" | custom-call | flops 100000000 | bytes 4000000 | tf_op jit(solution)/shard_map/pallas_call | solution.py:55
  111.5 5.3 %all-to-all-done.2 = f32[16,16,128]{2,1,0:T(8,128)} async-done(((f32[16,16,128]{2,1,0:T(8,128)}), f32[16,16,128]{2,1,0:T(8,128)}, u32[]{:S(2)}, u32[]{:S(2)}) %all-to-all-start.2) | async-done | bytes 131104 | tf_op jit(solution)/shard_map/all_to_all | solution.py:613
  116.8 3.4 %shard_map.100 = (f32[16,432]{1,0:T(8,128)}, f32[432,432]{1,0:T(8,128)}, f32[16,16]{1,0:T(8,128)}) custom-call(f32[256,128]{1,0:T(8,128)} %bitcast.5.refs_0_), custom_call_target="tpu_custom_call" | custom-call | flops 1000000 | bytes 4000000 | tf_op jit(solution)/shard_map/pallas_call | solution.py:70
  (1 shorter events, 0.0 us)
Async XLA Ops:
  2.5 15.0 %collective-permute-start.1 = (bf16[44,16,128]{2,1,0:T(8,128)(2,1)}, bf16[44,16,128]{2,1,0:T(8,128)(2,1)}, u32[]{:S(2)}, u32[]{:S(2)}) collective-permute-start(bf16[44,16,128]{2,1,0:T(8,128)(2,1)} %get-tuple-element.25), channel_id=1, source_target_pairs={{1,0},{2,1},{3,2},{4,3},{5,4},{6,5},{7,6},{0,7},{9,8},{10,9},{11,1... | collective-permute-start | bytes 540680 | tf_op jit(solution)/shard_map/ppermute | solution.py:539
  11.3 6.2 %collective-permute-start = (bf16[40,16,128]{2,1,0:T(8,128)(2,1)}, bf16[40,16,128]{2,1,0:T(8,128)(2,1)}, u32[]{:S(2)}, u32[]{:S(2)}) collective-permute-start(bf16[40,16,128]{2,1,0:T(8,128)(2,1)} %get-tuple-element.24), channel_id=1, source_target_pairs={{0,1},{1,2},{2,3},{3,4},{4,5},{5,6},{6,7},{7,0},{8,9},{9,10},{10,1... | collective-permute-start | bytes 491528 | tf_op jit(solution)/shard_map/ppermute | solution.py:539
  19.3 18.8 %collective-permute-start.3 = (bf16[43,16,128]{2,1,0:T(8,128)(2,1)}, bf16[43,16,128]{2,1,0:T(8,128)(2,1)}, u32[]{:S(2)}, u32[]{:S(2)}) collective-permute-start(bf16[43,16,128]{2,1,0:T(8,128)(2,1)} %get-tuple-element.28), channel_id=1, source_target_pairs={{8,0},{16,8},{24,16},{32,24},{40,32},{48,40},{56,48},{64,56},{72,6... | collective-permute-start | bytes 528392 | tf_op jit(solution)/shard_map/ppermute | solution.py:539
  27.5 10.6 %collective-permute-start.2 = (bf16[40,16,128]{2,1,0:T(8,128)(2,1)}, bf16[40,16,128]{2,1,0:T(8,128)(2,1)}, u32[]{:S(2)}, u32[]{:S(2)}) collective-permute-start(bf16[40,16,128]{2,1,0:T(8,128)(2,1)} %get-tuple-element.27), channel_id=1, source_target_pairs={{0,8},{8,16},{16,24},{24,32},{32,40},{40,48},{48,56},{56,64},{64,7... | collective-permute-start | bytes 491528 | tf_op jit(solution)/shard_map/ppermute | solution.py:539
  30.3 0.6 copy-start
  42.9 15.7 %collective-permute-start.4 = (f32[10,16,128]{2,1,0:T(8,128)}, f32[10,16,128]{2,1,0:T(8,128)}, u32[]{:S(2)}, u32[]{:S(2)}) collective-permute-start(f32[10,16,128]{2,1,0:T(8,128)} %get-tuple-element.29), channel_id=1, source_target_pairs={{0,8},{8,16},{16,24},{24,32},{32,40},{40,48},{48,56},{56,64},{64,7... | collective-permute-start | bytes 245768 | tf_op jit(solution)/shard_map/ppermute | solution.py:539
  44.9 13.8 %collective-permute-start.5 = (f32[10,16,128]{2,1,0:T(8,128)}, f32[10,16,128]{2,1,0:T(8,128)}, u32[]{:S(2)}, u32[]{:S(2)}) collective-permute-start(f32[10,16,128]{2,1,0:T(8,128)} %get-tuple-element.30), channel_id=1, source_target_pairs={{8,0},{16,8},{24,16},{32,24},{40,32},{48,40},{56,48},{64,56},{72,6... | collective-permute-start | bytes 245768 | tf_op jit(solution)/shard_map/ppermute | solution.py:539
  52.5 6.2 %collective-permute-start.6 = (f32[8,128]{1,0:T(8,128)}, f32[8,128]{1,0:T(8,128)}, u32[]{:S(2)}, u32[]{:S(2)}) collective-permute-start(f32[8,128]{1,0:T(8,128)} %get-tuple-element.31), channel_id=1, source_target_pairs={{16,0},{24,8},{32,16},{40,24},{48,32},{56,40},{64,48},{72,56},{80,... | collective-permute-start | bytes 12296 | tf_op jit(solution)/shard_map/ppermute | solution.py:580
  62.6 45.1 %copy-start.1 = (bf16[16,16,27]{2,1,0:T(8,128)(2,1)S(1)}, bf16[16,16,27]{2,1,0:T(8,128)(2,1)}, u32[]{:S(2)}) copy-start(bf16[16,16,27]{2,1,0:T(8,128)(2,1)} %copy-done) | copy-start | bytes 41476
  102.3 14.5 %all-to-all-start.2 = ((f32[16,16,128]{2,1,0:T(8,128)}), f32[16,16,128]{2,1,0:T(8,128)}, u32[]{:S(2)}, u32[]{:S(2)}) async-start(f32[16,16,128]{2,1,0:T(8,128)} %shard_map.99), calls=%async_computation.2 | async-start | bytes 262144 | tf_op jit(solution)/shard_map/all_to_all | solution.py:613

commit v6 on v5

--- a/solution.py
+++ b/solution.py
@@ -147,6 +147,10 @@
         move(before, 4 * PREV + first, out, ROWS_IN, n)
         move(own_fields, first, out, ROWS_IN + n, n)
         move(after, 4 * NEXT + first, out, ROWS_IN + 2 * n, n)
+    second = ROWS_IN + 3 * (DOWN[1] - DOWN[0])
+    move(before, 2 * PREV - 1, down, second, 1)
+    move(own_feat, 8, down, second + 1, 8)
+    move(after, NEXT, down, second + 9, 1)
     for copy in copies:
         copy.start()
     out_up = pltpu.make_async_copy(up, to_up, left.at[0])
@@ -165,7 +169,7 @@
     for a in range(3):
         for b in range(3):
             at = pl.multiple_of(z * 144 + (a * 3 + b) * 16, 16)
-            for y in range(rows):
+            for y in rows:
                 columns[pl.ds(at, 16), y * 128 : (y + 1) * 128] = shifted[
                     b, z, (y + a) * 16 : (y + a + 1) * 16, :
                 ]
@@ -178,8 +182,8 @@
 
 def stage_one(
     need, done, own_feat, before, after, below, above, field, vel, cot, w_rows,
-    send_up, send_down, send_far, columns_own, coef, kept,
-    shifted, columns,
+    send_up, send_down, columns_own, coef, kept,
+    shifted, columns, coef_above,
 ):
     u0, lam2 = kept.at[U0], kept.at[LAM2]
     velx = [kept.at[v] for v in VEL]
@@ -204,6 +208,12 @@
         both = jnp.dot(tiles, shift_value, preferred_element_type=F32).astype(BF16)
         shifted[0, z] = both[:, :128]
         shifted[2, z] = both[:, 128:]
+    second = ROWS_IN + 3 * (DOWN[1] - DOWN[0])
+    tiles = above[second : second + 10].reshape(160, 128)
+    both = jnp.dot(tiles, shift_value, preferred_element_type=F32).astype(BF16)
+    shifted[0, 6, 64:224, :] = both[:, :128]
+    shifted[1, 6, 64:224, :] = tiles
+    shifted[2, 6, 64:224, :] = both[:, 128:]
 
     need(5, 6, 7)
 
@@ -233,13 +243,14 @@
             velx[d][1 + z] = extended(d, z, vel[d, z])
 
     def fill(z, carry):
-        fill_columns(columns, shifted, z, ROWS_OUT)
+        fill_columns(columns, shifted, z, range(ROWS_OUT))
         return carry
 
     lax.fori_loop(0, 6, fill, 0)
-
-    columns_own[...] = columns[:, 512:1536]
-    done(3)
+    fill_columns(columns, shifted, 6, range(4, 12))
+
+    columns_own[...] = columns[0:864, 512:1536]
+    done(2)
     need(8)
     w_value = w_rows[...]
     for p in range(4):
@@ -249,7 +260,10 @@
         for y in range(ROWS_OUT):
             coef[p, (4 + y) * 16 : (5 + y) * 16, :] = plane[:, y * 128 : (y + 1) * 128]
 
-    done(4)
+    done(3)
+    plane = jnp.dot(w_value, columns[576:1008, 512:1536], preferred_element_type=F32)
+    for y in range(8):
+        coef_above[y * 16 : (y + 1) * 16, :] = plane[:, y * 128 : (y + 1) * 128]
 
     def a(p, k):
         value = coef[p, pl.ds(k, 24, stride=16), :]
@@ -307,7 +321,9 @@
         out[8, 8:16, :] = carried[keys[1]][8:16]
         out[9, 0:8, :] = carried[keys[2]][8:16]
         out[9, 8:16, :] = carried[keys[2]][8:16]
-    send_far[...] = pushed[0][8:16]
+    face = (-H) * (lam2[5, 8:16] - lam2[6, 8:16]) * velx[0][5, 8:16]
+    face = face * (BASE[0] + coef_above[pl.ds(0, 8, stride=16), :])
+    send_down[7, 4:12, :] = pushed[4][8:16] + face
 
 
 def patch_gram(need, done, columns_own, gram, full, line):
@@ -345,13 +361,13 @@
 
 
 def stage_two(
-    need, done, below, above, far, state, coef, columns_own, gram,
+    need, done, below, above, state, coef, columns_own, gram,
     mixed, tiles, lam0,
     u1, lam1, turn, row,
 ):
     u0, lam2, u1_part, lam_part = state.at[U0], state.at[LAM2], state.at[U1], state.at[LAM1]
     velx = [state.at[v] for v in VEL]
-    need(0, 1, 2, 3, 4)
+    need(0, 1, 2, 3)
 
     def padded(value):
         zero = jnp.zeros((4, 128), F32)
@@ -379,7 +395,7 @@
 
     own_rows = slice(8, 16)
     lowest = lam_part[0][own_rows] + low[7][own_rows]
-    highest = high[7][own_rows] + far[...]
+    highest = high[7][own_rows]
     fall = [lowest, lam1[0, own_rows], lam1[1, own_rows]]
     rise = [lam1[5, own_rows], lam1[6, own_rows], highest]
     outer = [(-H) * (fall[0] - fall[1]), (-H) * (fall[1] - fall[2])]
@@ -425,7 +441,7 @@
     for z in range(6):
         tiles[z] = turn[z, 7 * 16 : 17 * 16, :].astype(BF16)
     done(1)
-    need(5)
+    need(4)
     sum_w = None
     sum_g = None
     for p in range(4):
@@ -443,7 +459,7 @@
     row[:, 432:448] = sum_g
     for t in range(4):
         mixed[t * 16 : (t + 1) * 16, :] = row[:, t * 128 : (t + 1) * 128]
-    need(6)
+    need(5)
     mixed[64:256, :] = gram[...]
 
 
@@ -457,7 +473,7 @@
         shifted[2, z] = both[:, 128:]
 
     def fill(z, carry):
-        fill_columns(columns, shifted, z, 8)
+        fill_columns(columns, shifted, z, range(8))
         return carry
 
     lax.fori_loop(0, 6, fill, 0)
@@ -554,30 +570,26 @@
         (features.reshape(16, 32, 128), field, velocity, cotangent),
     )
     before, after = neighbours(to_next, to_prev, "gy")
+    along_z = (ROWS_IN + 3 * (UP[1] - UP[0]), ROWS_IN + 3 * (DOWN[1] - DOWN[0]) + 10)
     to_up, to_down = pl.pallas_call(
         pack_z,
-        out_shape=[
-            jax.ShapeDtypeStruct((ROWS_IN + 3 * (stop - first),) + tile, BF16)
-            for first, stop in (UP, DOWN)
-        ],
+        out_shape=[jax.ShapeDtypeStruct((n,) + tile, BF16) for n in along_z],
         in_specs=[_HBM] * 4,
         out_specs=[_HBM] * 2,
-        scratch_shapes=[
-            pltpu.VMEM((ROWS_IN + 3 * (stop - first),) + tile, BF16) for first, stop in (UP, DOWN)
-        ]
-        + [pltpu.SemaphoreType.DMA((12,)), pltpu.SemaphoreType.DMA((2,))],
+        scratch_shapes=[pltpu.VMEM((n,) + tile, BF16) for n in along_z]
+        + [pltpu.SemaphoreType.DMA((15,)), pltpu.SemaphoreType.DMA((2,))],
         compiler_params=pltpu.CompilerParams(vmem_limit_bytes=64 * 1024 * 1024),
     )(own_feat, own_fields, before, after)
     below, above = neighbours(to_up, to_down, "gz")
-    send_up, send_down, send_far, columns_own, coef, state = call(
+    send_up, send_down, columns_own, coef, state = call(
         stage_one,
-        [((10, 16, 128), F32), ((10, 16, 128), F32), ((8, 128), F32), ((864, 1024), BF16),
+        [((10, 16, 128), F32), ((10, 16, 128), F32), ((864, 1024), BF16),
          ((4, 384, 128), F32), ((48, 24, 128), F32)],
-        [pltpu.VMEM((3, 6, ROWS_IN * 16, 128), BF16), pltpu.VMEM((864, ROWS_OUT * 128), BF16)],
+        [pltpu.VMEM((3, 7, ROWS_IN * 16, 128), BF16), pltpu.VMEM((1008, ROWS_OUT * 128), BF16),
+         pltpu.VMEM((128, 128), F32)],
         (own_feat, before, after, below, above, field, velocity, cotangent, w_rows),
     )
     below1, above1 = neighbours(send_up, send_down, "gz")
-    far = lax.ppermute(send_far, "gz", [((i + 2) % nz, i) for i in range(nz)])
     (gram,) = call(
         patch_gram,
         [((192, 128), F32)],
@@ -590,7 +602,7 @@
         [((256, 128), F32), ((6, 160, 128), BF16), ((4, 8, 128), F32)],
         [pltpu.VMEM((10, 24, 128), F32), pltpu.VMEM((7, 24, 128), F32),
          pltpu.VMEM((6, 384, 128), F32), pltpu.VMEM((16, 512), F32)],
-        (below1, above1, far, state, coef, columns_own, gram),
+        (below1, above1, state, coef, columns_own, gram),
     )
     (grad_feat,) = call(
         stage_three,

time: 121 us -> 120 us (level)
  starting transfers between devices: 37.5 us -> 35.6 us
  blocking collectives: 39 us -> 40.4 us
    all_to_all x1, blocking collectives: 16.8 us -> 19.3 us  [body(): parts = lax.all_to_all(parts, axes, 0, 0, axis_index_groups=plane)]
    ppermute x1 -> x0, starting transfers between devices: 1.92 us -> none  [body(): far = lax.ppermute(send_far, 'gz', [((i + 2) % nz, i) for i in range(nz)])]
  transfers between devices with their start and end apart: 8 -> 7, of which waited for: 4 -> 3; matrix products, arithmetic and copies ran while one was open for 2% -> 2% of each run, Pallas kernels for 5% -> 5%
where the time goes in v6:
time: 120 us; the launch traced here: 119 us
  blocking collectives  40.4 us (34%)
  starting transfers between devices  35.6 us (30%)
  Pallas kernels  22.8 us (19%)
  waiting for transfers between devices  15.8 us (13%)
  local copies, waits for them, and re-layouts  3.5 us (3%)
    ppermute x6, starting transfers between devices, neighbours(): return (lax.ppermute(to_next, axis, up), lax.ppermute(to_prev, axis, down))  30.3 us
    all_to_all x1, blocking collectives, body(): parts = lax.all_to_all(parts, axes, 0, 0, axis_index_groups=line)  21.1 us
    all_to_all x1, blocking collectives, body(): parts = lax.all_to_all(parts, axes, 0, 0, axis_index_groups=plane)  19.3 us
    pallas_call x5, Pallas kernels, call(): pl.pallas_call(run, out_shape=[jax.ShapeDtypeStruct(s, t) for s, t in out...  16.9 us
    ppermute x6, waiting for transfers between devices, neighbours(): return (lax.ppermute(to_next, axis, up), lax.ppermute(to_prev, axis, down))  10.5 us
    all_to_all x1, starting transfers between devices, body(): lax.all_to_all(parts, axes, 0, 0, axis_index_groups=line).reshape(256, 128)  5.27 us
    all_to_all x1, waiting for transfers between devices, body(): lax.all_to_all(parts, axes, 0, 0, axis_index_groups=line).reshape(256, 128)  5.27 us
    pallas_call x3, Pallas kernels, call_small(): pl.pallas_call(kernel, out_shape=[jax.ShapeDtypeStruct(s, t) for s, t in...  4.12 us
  transfers between devices with their start and end apart: 7, of which 3 were waited for; matrix products, arithmetic and copies ran while one was open for 2% of the time, Pallas kernels for 5%

profile of v6, /device:TPU:1, one launch (start us, length us, event | category | flops | bytes accessed | tf_op | source)
XLA Modules:
  0.0 118.9 jit_solution(423607219864629721)
XLA Ops:
  0.6 1.9 %shard_map.92 = (bf16[32,16,128]{2,1,0:T(8,128)(2,1)}, bf16[20,16,128]{2,1,0:T(8,128)(2,1)}, bf16[40,16,128]{2,1,0:T(8,128)(2,1)}, bf16[44,16,128]{2,1,0:T(8,128)(2,1)}) custom-call(bf16[16,32,128]{2,1,0:T(8,128)(2,1)} %bitcast.9, f32[4,8,128]{2,1,0:T(8,128)} %refs_5_.1, f32[3,4,8,128]{3,2,1,0:T(8,128)} %refs_6_.1, f32[4,8,128]{2,1,0:T(8,128)} %refs_7_.1), custom_call_target="tpu_custom_call" | custom-call | flops 1000000 | bytes 4000000 | tf_op jit(solution)/shard_map/pallas_call | solution.py:55
  2.5 8.8 %collective-permute-start.1 = (bf16[44,16,128]{2,1,0:T(8,128)(2,1)}, bf16[44,16,128]{2,1,0:T(8,128)(2,1)}, u32[]{:S(2)}, u32[]{:S(2)}) collective-permute-start(bf16[44,16,128]{2,1,0:T(8,128)(2,1)} %get-tuple-element.24), channel_id=1, source_target_pairs={{1,0},{2,1},{3,2},{4,3},{5,4},{6,5},{7,6},{0,7},{9,8},{10,9},{11,1... | collective-permute-start | bytes 540680 | tf_op jit(solution)/shard_map/ppermute | solution.py:555
  11.3 1.9 %collective-permute-start = (bf16[40,16,128]{2,1,0:T(8,128)(2,1)}, bf16[40,16,128]{2,1,0:T(8,128)(2,1)}, u32[]{:S(2)}, u32[]{:S(2)}) collective-permute-start(bf16[40,16,128]{2,1,0:T(8,128)(2,1)} %get-tuple-element.23), channel_id=1, source_target_pairs={{0,1},{1,2},{2,3},{3,4},{4,5},{5,6},{6,7},{7,0},{8,9},{9,10},{10,1... | collective-permute-start | bytes 491528 | tf_op jit(solution)/shard_map/ppermute | solution.py:555
  13.3 4.3 %collective-permute-done.before.refs_1_ = bf16[40,16,128]{2,1,0:T(8,128)(2,1)} collective-permute-done((bf16[40,16,128]{2,1,0:T(8,128)(2,1)}, bf16[40,16,128]{2,1,0:T(8,128)(2,1)}, u32[]{:S(2)}, u32[]{:S(2)}) %collective-permute-start) | collective-permute-done | bytes 163872 | tf_op jit(solution)/shard_map/ppermute | solution.py:555
  17.6 0.0 collective-permute-done.1.after.refs_2_
  17.6 1.8 %shard_map.93 = (bf16[40,16,128]{2,1,0:T(8,128)(2,1)}, bf16[53,16,128]{2,1,0:T(8,128)(2,1)}) custom-call(bf16[32,16,128]{2,1,0:T(8,128)(2,1)} %get-tuple-element.22.own_feat.refs_0_, bf16[20,16,128]{2,1,0:T(8,128)(2,1)} %get-tuple-element.25.own_fields, bf16[40,16,128]{2,1,0:T(8,128)(2,1)} %collective-permute-done.before.refs_1_, ...), custom_call_target="tpu_custom_call" | custom-call | tf_op jit(solution)/shard_map/pallas_call | solution.py:574
  19.4 8.2 %collective-permute-start.3 = (bf16[53,16,128]{2,1,0:T(8,128)(2,1)}, bf16[53,16,128]{2,1,0:T(8,128)(2,1)}, u32[]{:S(2)}, u32[]{:S(2)}) collective-permute-start(bf16[53,16,128]{2,1,0:T(8,128)(2,1)} %get-tuple-element.27), channel_id=1, source_target_pairs={{8,0},{16,8},{24,16},{32,24},{40,32},{48,40},{56,48},{64,56},{72,6... | collective-permute-start | bytes 651272 | tf_op jit(solution)/shard_map/ppermute | solution.py:555
  27.6 1.9 %collective-permute-start.2 = (bf16[40,16,128]{2,1,0:T(8,128)(2,1)}, bf16[40,16,128]{2,1,0:T(8,128)(2,1)}, u32[]{:S(2)}, u32[]{:S(2)}) collective-permute-start(bf16[40,16,128]{2,1,0:T(8,128)(2,1)} %get-tuple-element.26), channel_id=1, source_target_pairs={{0,8},{8,16},{16,24},{24,32},{32,40},{40,48},{48,56},{56,64},{64,7... | collective-permute-start | bytes 491528 | tf_op jit(solution)/shard_map/ppermute | solution.py:555
  29.5 0.8 reshape.32
  30.3 0.0 copy-start
  30.4 0.6 copy-done
  31.0 0.2 copy.12
  31.2 0.8 reshape.33.refs_8_
  31.9 6.2 %collective-permute-done.2.refs_3_ = bf16[40,16,128]{2,1,0:T(8,128)(2,1)} collective-permute-done((bf16[40,16,128]{2,1,0:T(8,128)(2,1)}, bf16[40,16,128]{2,1,0:T(8,128)(2,1)}, u32[]{:S(2)}, u32[]{:S(2)}) %collective-permute-start.2) | collective-permute-done | bytes 163872 | tf_op jit(solution)/shard_map/ppermute | solution.py:555
  38.2 0.0 collective-permute-done.3.refs_4_
  38.2 4.9 %shard_map.94 = (f32[10,16,128]{2,1,0:T(8,128)}, f32[10,16,128]{2,1,0:T(8,128)}, bf16[864,1024]{1,0:T(8,128)(2,1)}, f32[4,384,128]{2,1,0:T(8,128)}, f32[48,24,128]{2,1,0:T(8,128)}) custom-call(bf16[32,16,128]{2,1,0:T(8,128)(2,1)} %get-tuple-element.22.own_feat.refs_0_, bf16[40,16,128]{2,1,0:T(8,128)(2,1)} %collective-permute-done.before.refs_1_, ...), custom_call_target="tpu_custom_call" | custom-call | flops 1000000 | bytes 4000000 | tf_op jit(solution)/shard_map/pallas_call | solution.py:55
  43.1 1.9 %collective-permute-start.4 = (f32[10,16,128]{2,1,0:T(8,128)}, f32[10,16,128]{2,1,0:T(8,128)}, u32[]{:S(2)}, u32[]{:S(2)}) collective-permute-start(f32[10,16,128]{2,1,0:T(8,128)} %get-tuple-element.28), channel_id=1, source_target_pairs={{0,8},{8,16},{16,24},{24,32},{32,40},{40,48},{48,56},{56,64},{64,7... | collective-permute-start | bytes 245768 | tf_op jit(solution)/shard_map/ppermute | solution.py:555
  45.0 7.6 %collective-permute-start.5 = (f32[10,16,128]{2,1,0:T(8,128)}, f32[10,16,128]{2,1,0:T(8,128)}, u32[]{:S(2)}, u32[]{:S(2)}) collective-permute-start(f32[10,16,128]{2,1,0:T(8,128)} %get-tuple-element.29), channel_id=1, source_target_pairs={{8,0},{16,8},{24,16},{32,24},{40,32},{48,40},{56,48},{64,56},{72,6... | collective-permute-start | bytes 245768 | tf_op jit(solution)/shard_map/ppermute | solution.py:555
  52.6 3.4 %shard_map.95.refs_5_ = f32[192,128]{1,0:T(8,128)} custom-call(bf16[864,1024]{1,0:T(8,128)(2,1)} %get-tuple-element.32.refs_0_.refs_4_), custom_call_target="tpu_custom_call" | custom-call | flops 500000000 | bytes 4000000 | tf_op jit(solution)/shard_map/pallas_call | solution.py:55
  56.0 0.0 collective-permute-done.4.refs_0_
  56.0 0.0 collective-permute-done.5.refs_1_
  56.0 3.9 %shard_map.96 = (f32[256,128]{1,0:T(8,128)}, bf16[6,160,128]{2,1,0:T(8,128)(2,1)}, f32[4,8,128]{2,1,0:T(8,128)}) custom-call(f32[10,16,128]{2,1,0:T(8,128)} %collective-permute-done.4.refs_0_, f32[10,16,128]{2,1,0:T(8,128)} %collective-permute-done.5.refs_1_, f32[48,24,128]{2,1,0:T(8,128)} %get-tuple-element.30.refs_2_, ...), custom_call_target="tpu_custom_call" | custom-call | flops 1000000 | bytes 4000000 | tf_op jit(solution)/shard_map/pallas_call | solution.py:55
  59.9 0.0 copy-start.1
  59.9 21.1 %all_to_all.15.parts = f32[16,16,128]{2,1,0:T(8,128)S(1)} all-to-all(f32[16,16,128]{2,1,0:T(8,128)} %bitcast.8), channel_id=1, replica_groups={{0,1,2,3,4,5,6,7,256,257,258,259,260,261,262,263},{8,9,10,11,12,13,14,1..., dimensions={0} | all-to-all | bytes 262144 | tf_op jit(solution)/shard_map/all_to_all | solution.py:621
  81.1 19.3 %all_to_all.16.parts = f32[32,16,128]{2,1,0:T(8,128)S(1)} all-to-all(f32[32,16,128]{2,1,0:T(8,128)S(1)} %shard_map.98), channel_id=1, replica_groups={{0,8,16,24,32,40,48,56,64,72,80,88,96,104,112,120,128,136,144,152,160,1..., dimensions={0} | all-to-all | bytes 524288 | tf_op jit(solution)/shard_map/all_to_all | solution.py:623
  100.3 0.7 shard_map.99
  101.0 5.3 %all-to-all-start.2 = ((f32[16,16,128]{2,1,0:T(8,128)}), f32[16,16,128]{2,1,0:T(8,128)}, u32[]{:S(2)}, u32[]{:S(2)}) async-start(f32[16,16,128]{2,1,0:T(8,128)} %shard_map.99), calls=%async_computation.2 | async-start | bytes 262144 | tf_op jit(solution)/shard_map/all_to_all | solution.py:625
  106.3 0.0 copy-done.1
  106.3 0.2 copy.13
  106.5 0.1 rev.3
  106.6 0.8 reshape.34.refs_1_
  107.4 2.8 %shard_map.97 = bf16[16,32,128]{2,1,0:T(8,128)(2,1)} custom-call(bf16[6,160,128]{2,1,0:T(8,128)(2,1)} %get-tuple-element.34.refs_0_, bf16[16,432]{1,0:T(8,128)(2,1)} %reshape.34.refs_1_, f32[256,128]{1,0:T(8,128)} %get-tuple-element.35.refs_2_), custom_call_target="tpu_custom_call" | custom-call | flops 100000000 | bytes 4000000 | tf_op jit(solution)/shard_map/pallas_call | solution.py:55
  110.2 5.3 %all-to-all-done.2 = f32[16,16,128]{2,1,0:T(8,128)} async-done(((f32[16,16,128]{2,1,0:T(8,128)}), f32[16,16,128]{2,1,0:T(8,128)}, u32[]{:S(2)}, u32[]{:S(2)}) %all-to-all-start.2) | async-done | bytes 131104 | tf_op jit(solution)/shard_map/all_to_all | solution.py:625
  115.5 3.4 %shard_map.100 = (f32[16,432]{1,0:T(8,128)}, f32[432,432]{1,0:T(8,128)}, f32[16,16]{1,0:T(8,128)}) custom-call(f32[256,128]{1,0:T(8,128)} %bitcast.5.refs_0_), custom_call_target="tpu_custom_call" | custom-call | flops 1000000 | bytes 4000000 | tf_op jit(solution)/shard_map/pallas_call | solution.py:70
  (1 shorter events, 0.0 us)
Async XLA Ops:
  2.5 15.0 %collective-permute-start.1 = (bf16[44,16,128]{2,1,0:T(8,128)(2,1)}, bf16[44,16,128]{2,1,0:T(8,128)(2,1)}, u32[]{:S(2)}, u32[]{:S(2)}) collective-permute-start(bf16[44,16,128]{2,1,0:T(8,128)(2,1)} %get-tuple-element.24), channel_id=1, source_target_pairs={{1,0},{2,1},{3,2},{4,3},{5,4},{6,5},{7,6},{0,7},{9,8},{10,9},{11,1... | collective-permute-start | bytes 540680 | tf_op jit(solution)/shard_map/ppermute | solution.py:555
  11.3 6.2 %collective-permute-start = (bf16[40,16,128]{2,1,0:T(8,128)(2,1)}, bf16[40,16,128]{2,1,0:T(8,128)(2,1)}, u32[]{:S(2)}, u32[]{:S(2)}) collective-permute-start(bf16[40,16,128]{2,1,0:T(8,128)(2,1)} %get-tuple-element.23), channel_id=1, source_target_pairs={{0,1},{1,2},{2,3},{3,4},{4,5},{5,6},{6,7},{7,0},{8,9},{9,10},{10,1... | collective-permute-start | bytes 491528 | tf_op jit(solution)/shard_map/ppermute | solution.py:555
  19.4 18.8 %collective-permute-start.3 = (bf16[53,16,128]{2,1,0:T(8,128)(2,1)}, bf16[53,16,128]{2,1,0:T(8,128)(2,1)}, u32[]{:S(2)}, u32[]{:S(2)}) collective-permute-start(bf16[53,16,128]{2,1,0:T(8,128)(2,1)} %get-tuple-element.27), channel_id=1, source_target_pairs={{8,0},{16,8},{24,16},{32,24},{40,32},{48,40},{56,48},{64,56},{72,6... | collective-permute-start | bytes 651272 | tf_op jit(solution)/shard_map/ppermute | solution.py:555
  27.6 10.6 %collective-permute-start.2 = (bf16[40,16,128]{2,1,0:T(8,128)(2,1)}, bf16[40,16,128]{2,1,0:T(8,128)(2,1)}, u32[]{:S(2)}, u32[]{:S(2)}) collective-permute-start(bf16[40,16,128]{2,1,0:T(8,128)(2,1)} %get-tuple-element.26), channel_id=1, source_target_pairs={{0,8},{8,16},{16,24},{24,32},{32,40},{40,48},{48,56},{56,64},{64,7... | collective-permute-start | bytes 491528 | tf_op jit(solution)/shard_map/ppermute | solution.py:555
  30.3 0.6 copy-start
  43.1 12.9 %collective-permute-start.4 = (f32[10,16,128]{2,1,0:T(8,128)}, f32[10,16,128]{2,1,0:T(8,128)}, u32[]{:S(2)}, u32[]{:S(2)}) collective-permute-start(f32[10,16,128]{2,1,0:T(8,128)} %get-tuple-element.28), channel_id=1, source_target_pairs={{0,8},{8,16},{16,24},{24,32},{32,40},{40,48},{48,56},{56,64},{64,7... | collective-permute-start | bytes 245768 | tf_op jit(solution)/shard_map/ppermute | solution.py:555
  45.0 11.0 %collective-permute-start.5 = (f32[10,16,128]{2,1,0:T(8,128)}, f32[10,16,128]{2,1,0:T(8,128)}, u32[]{:S(2)}, u32[]{:S(2)}) collective-permute-start(f32[10,16,128]{2,1,0:T(8,128)} %get-tuple-element.29), channel_id=1, source_target_pairs={{8,0},{16,8},{24,16},{32,24},{40,32},{48,40},{56,48},{64,56},{72,6... | collective-permute-start | bytes 245768 | tf_op jit(solution)/shard_map/ppermute | solution.py:555
  59.9 46.4 %copy-start.1 = (bf16[16,16,27]{2,1,0:T(8,128)(2,1)S(1)}, bf16[16,16,27]{2,1,0:T(8,128)(2,1)}, u32[]{:S(2)}) copy-start(bf16[16,16,27]{2,1,0:T(8,128)(2,1)} %copy-done) | copy-start | bytes 41476
  101.0 14.5 %all-to-all-start.2 = ((f32[16,16,128]{2,1,0:T(8,128)}), f32[16,16,128]{2,1,0:T(8,128)}, u32[]{:S(2)}, u32[]{:S(2)}) async-start(f32[16,16,128]{2,1,0:T(8,128)} %shard_map.99), calls=%async_computation.2 | async-start | bytes 262144 | tf_op jit(solution)/shard_map/all_to_all | solution.py:625

commit v7 on v6

--- a/solution.py
+++ b/solution.py
@@ -326,7 +326,10 @@
     send_down[7, 4:12, :] = pushed[4][8:16] + face
 
 
-def patch_gram(need, done, columns_own, gram, full, line):
+def patch_gram(need, done, columns_own, down, gram, down_out, full, line):
+    need(1)
+    down_out[...] = down[...]
+    done(1)
     need(0)
     total = None
     for p in range(4):
@@ -493,8 +496,7 @@
     one = value.astype(BF16)
     rest = value - one.astype(F32)
     two = rest.astype(BF16)
-    three = (rest - two.astype(F32)).astype(BF16)
-    return one, two, three
+    return one, two
 
 
 def to_channel_major(value):
@@ -502,7 +504,7 @@
     j = lax.broadcasted_iota(jnp.int32, (432, 432), 1)
     place = jnp.where((i % 16) * 27 + i // 16 == j, 1.0, 0.0).astype(BF16)
     parts = [jnp.dot(v, place, preferred_element_type=F32) for v in pieces(value)]
-    return parts[2] + parts[1] + parts[0]
+    return parts[1] + parts[0]
 
 
 def total_to_all(parts, out):
@@ -589,14 +591,14 @@
          pltpu.VMEM((128, 128), F32)],
         (own_feat, before, after, below, above, field, velocity, cotangent, w_rows),
     )
+    gram, send_down = call(
+        patch_gram,
+        [((192, 128), F32), ((10, 16, 128), F32)],
+        [pltpu.VMEM((144, 512), F32), pltpu.VMEM((16, 1280), F32)],
+        (columns_own, send_down),
+        5e8,
+    )
     below1, above1 = neighbours(send_up, send_down, "gz")
-    (gram,) = call(
-        patch_gram,
-        [((192, 128), F32)],
-        [pltpu.VMEM((144, 512), F32), pltpu.VMEM((16, 1280), F32)],
-        (columns_own,),
-        5e8,
-    )
     mixed, tiles, grad_field = call(
         stage_two,
         [((256, 128), F32), ((6, 160, 128), BF16), ((4, 8, 128), F32)],

time: 120 us -> 123 us (1.025)
  waiting for transfers between devices: 15.8 us -> 17.6 us
  blocking collectives: 40.4 us -> 42 us
    ppermute x6, waiting for transfers between devices: 10.5 us -> 12.3 us  [neighbours(): return (lax.ppermute(to_next, axis, up), lax.ppermute(to_prev, axis, down))]
  transfers between devices with their start and end apart: 7 -> 7, of which waited for: 3 -> 4; matrix products, arithmetic and copies ran while one was open for 2% -> 2% of each run, Pallas kernels for 5% -> 5%
where the time goes in v7:
time: 123 us; the launch traced here: 122 us
  blocking collectives  42 us (34%)
  starting transfers between devices  35.6 us (29%)
  Pallas kernels  22.6 us (18%)
  waiting for transfers between devices  17.6 us (14%)
  local copies, waits for them, and re-layouts  3.51 us (3%)
    ppermute x6, starting transfers between devices, neighbours(): return (lax.ppermute(to_next, axis, up), lax.ppermute(to_prev, axis, down))  30.3 us
    all_to_all x1, blocking collectives, body(): parts = lax.all_to_all(parts, axes, 0, 0, axis_index_groups=line)  21.7 us
    all_to_all x1, blocking collectives, body(): parts = lax.all_to_all(parts, axes, 0, 0, axis_index_groups=plane)  20.4 us
    pallas_call x5, Pallas kernels, call(): pl.pallas_call(run, out_shape=[jax.ShapeDtypeStruct(s, t) for s, t in out...  17 us
    ppermute x6, waiting for transfers between devices, neighbours(): return (lax.ppermute(to_next, axis, up), lax.ppermute(to_prev, axis, down))  12.3 us
    all_to_all x1, starting transfers between devices, body(): lax.all_to_all(parts, axes, 0, 0, axis_index_groups=line).reshape(256, 128)  5.27 us
    all_to_all x1, waiting for transfers between devices, body(): lax.all_to_all(parts, axes, 0, 0, axis_index_groups=line).reshape(256, 128)  5.27 us
    pallas_call x3, Pallas kernels, call_small(): pl.pallas_call(kernel, out_shape=[jax.ShapeDtypeStruct(s, t) for s, t in...  3.88 us
  transfers between devices with their start and end apart: 7, of which 4 were waited for; matrix products, arithmetic and copies ran while one was open for 2% of the time, Pallas kernels for 5%

profile of v7, /device:TPU:1, one launch (start us, length us, event | category | flops | bytes accessed | tf_op | source)
XLA Modules:
  0.0 122.1 jit_solution(11587557950272084004)
XLA Ops:
  0.6 1.9 %shard_map.92 = (bf16[32,16,128]{2,1,0:T(8,128)(2,1)}, bf16[20,16,128]{2,1,0:T(8,128)(2,1)}, bf16[40,16,128]{2,1,0:T(8,128)(2,1)}, bf16[44,16,128]{2,1,0:T(8,128)(2,1)}) custom-call(bf16[16,32,128]{2,1,0:T(8,128)(2,1)} %bitcast.9, f32[4,8,128]{2,1,0:T(8,128)} %refs_5_.1, f32[3,4,8,128]{3,2,1,0:T(8,128)} %refs_6_.1, f32[4,8,128]{2,1,0:T(8,128)} %refs_7_.1), custom_call_target="tpu_custom_call" | custom-call | flops 1000000 | bytes 4000000 | tf_op jit(solution)/shard_map/pallas_call | solution.py:55
  2.5 8.8 %collective-permute-start.1 = (bf16[44,16,128]{2,1,0:T(8,128)(2,1)}, bf16[44,16,128]{2,1,0:T(8,128)(2,1)}, u32[]{:S(2)}, u32[]{:S(2)}) collective-permute-start(bf16[44,16,128]{2,1,0:T(8,128)(2,1)} %get-tuple-element.26), channel_id=1, source_target_pairs={{1,0},{2,1},{3,2},{4,3},{5,4},{6,5},{7,6},{0,7},{9,8},{10,9},{11,1... | collective-permute-start | bytes 540680 | tf_op jit(solution)/shard_map/ppermute | solution.py:557
  11.3 1.9 %collective-permute-start = (bf16[40,16,128]{2,1,0:T(8,128)(2,1)}, bf16[40,16,128]{2,1,0:T(8,128)(2,1)}, u32[]{:S(2)}, u32[]{:S(2)}) collective-permute-start(bf16[40,16,128]{2,1,0:T(8,128)(2,1)} %get-tuple-element.25), channel_id=1, source_target_pairs={{0,1},{1,2},{2,3},{3,4},{4,5},{5,6},{6,7},{7,0},{8,9},{9,10},{10,1... | collective-permute-start | bytes 491528 | tf_op jit(solution)/shard_map/ppermute | solution.py:557
  13.3 4.3 %collective-permute-done.before.refs_1_ = bf16[40,16,128]{2,1,0:T(8,128)(2,1)} collective-permute-done((bf16[40,16,128]{2,1,0:T(8,128)(2,1)}, bf16[40,16,128]{2,1,0:T(8,128)(2,1)}, u32[]{:S(2)}, u32[]{:S(2)}) %collective-permute-start) | collective-permute-done | bytes 163872 | tf_op jit(solution)/shard_map/ppermute | solution.py:557
  17.6 0.0 collective-permute-done.1.after.refs_2_
  17.6 1.8 %shard_map.93 = (bf16[40,16,128]{2,1,0:T(8,128)(2,1)}, bf16[53,16,128]{2,1,0:T(8,128)(2,1)}) custom-call(bf16[32,16,128]{2,1,0:T(8,128)(2,1)} %get-tuple-element.24.own_feat.refs_0_, bf16[20,16,128]{2,1,0:T(8,128)(2,1)} %get-tuple-element.27.own_fields, bf16[40,16,128]{2,1,0:T(8,128)(2,1)} %collective-permute-done.before.refs_1_, ...), custom_call_target="tpu_custom_call" | custom-call | tf_op jit(solution)/shard_map/pallas_call | solution.py:576
  19.4 8.2 %collective-permute-start.3 = (bf16[53,16,128]{2,1,0:T(8,128)(2,1)}, bf16[53,16,128]{2,1,0:T(8,128)(2,1)}, u32[]{:S(2)}, u32[]{:S(2)}) collective-permute-start(bf16[53,16,128]{2,1,0:T(8,128)(2,1)} %get-tuple-element.29), channel_id=1, source_target_pairs={{8,0},{16,8},{24,16},{32,24},{40,32},{48,40},{56,48},{64,56},{72,6... | collective-permute-start | bytes 651272 | tf_op jit(solution)/shard_map/ppermute | solution.py:557
  27.6 1.9 %collective-permute-start.2 = (bf16[40,16,128]{2,1,0:T(8,128)(2,1)}, bf16[40,16,128]{2,1,0:T(8,128)(2,1)}, u32[]{:S(2)}, u32[]{:S(2)}) collective-permute-start(bf16[40,16,128]{2,1,0:T(8,128)(2,1)} %get-tuple-element.28), channel_id=1, source_target_pairs={{0,8},{8,16},{16,24},{24,32},{32,40},{40,48},{48,56},{56,64},{64,7... | collective-permute-start | bytes 491528 | tf_op jit(solution)/shard_map/ppermute | solution.py:557
  29.5 0.8 reshape.32
  30.3 0.0 copy-start
  30.4 0.6 copy-done
  31.0 0.2 copy.12
  31.2 0.8 reshape.33.refs_8_
  31.9 6.2 %collective-permute-done.2.refs_3_ = bf16[40,16,128]{2,1,0:T(8,128)(2,1)} collective-permute-done((bf16[40,16,128]{2,1,0:T(8,128)(2,1)}, bf16[40,16,128]{2,1,0:T(8,128)(2,1)}, u32[]{:S(2)}, u32[]{:S(2)}) %collective-permute-start.2) | collective-permute-done | bytes 163872 | tf_op jit(solution)/shard_map/ppermute | solution.py:557
  38.2 0.0 collective-permute-done.3.refs_4_
  38.2 4.9 %shard_map.94 = (f32[10,16,128]{2,1,0:T(8,128)}, f32[10,16,128]{2,1,0:T(8,128)}, bf16[864,1024]{1,0:T(8,128)(2,1)}, f32[4,384,128]{2,1,0:T(8,128)}, f32[48,24,128]{2,1,0:T(8,128)}) custom-call(bf16[32,16,128]{2,1,0:T(8,128)(2,1)} %get-tuple-element.24.own_feat.refs_0_, bf16[40,16,128]{2,1,0:T(8,128)(2,1)} %collective-permute-done.before.refs_1_, ...), custom_call_target="tpu_custom_call" | custom-call | flops 1000000 | bytes 4000000 | tf_op jit(solution)/shard_map/pallas_call | solution.py:55
  43.1 1.9 %collective-permute-start.4 = (f32[10,16,128]{2,1,0:T(8,128)}, f32[10,16,128]{2,1,0:T(8,128)}, u32[]{:S(2)}, u32[]{:S(2)}) collective-permute-start(f32[10,16,128]{2,1,0:T(8,128)} %get-tuple-element.30), channel_id=1, source_target_pairs={{0,8},{8,16},{16,24},{24,32},{32,40},{40,48},{48,56},{56,64},{64,7... | collective-permute-start | bytes 245768 | tf_op jit(solution)/shard_map/ppermute | solution.py:557
  45.0 3.4 %shard_map.95 = (f32[192,128]{1,0:T(8,128)}, f32[10,16,128]{2,1,0:T(8,128)}) custom-call(bf16[864,1024]{1,0:T(8,128)(2,1)} %get-tuple-element.31.refs_0_.refs_4_, f32[10,16,128]{2,1,0:T(8,128)} %get-tuple-element.32.refs_1_), custom_call_target="tpu_custom_call" | custom-call | flops 500000000 | bytes 4000000 | tf_op jit(solution)/shard_map/pallas_call | solution.py:55
  48.5 7.6 %collective-permute-start.5 = (f32[10,16,128]{2,1,0:T(8,128)}, f32[10,16,128]{2,1,0:T(8,128)}, u32[]{:S(2)}, u32[]{:S(2)}) collective-permute-start(f32[10,16,128]{2,1,0:T(8,128)} %get-tuple-element.33), channel_id=1, source_target_pairs={{8,0},{16,8},{24,16},{32,24},{40,32},{48,40},{56,48},{64,56},{72,6... | collective-permute-start | bytes 245768 | tf_op jit(solution)/shard_map/ppermute | solution.py:557
  56.1 0.0 collective-permute-done.4.refs_0_
  56.1 1.8 %collective-permute-done.5.refs_1_ = f32[10,16,128]{2,1,0:T(8,128)} collective-permute-done((f32[10,16,128]{2,1,0:T(8,128)}, f32[10,16,128]{2,1,0:T(8,128)}, u32[]{:S(2)}, u32[]{:S(2)}) %collective-permute-start.5) | collective-permute-done | bytes 81952 | tf_op jit(solution)/shard_map/ppermute | solution.py:557
  57.8 3.9 %shard_map.96 = (f32[256,128]{1,0:T(8,128)}, bf16[6,160,128]{2,1,0:T(8,128)(2,1)}, f32[4,8,128]{2,1,0:T(8,128)}) custom-call(f32[10,16,128]{2,1,0:T(8,128)} %collective-permute-done.4.refs_0_, f32[10,16,128]{2,1,0:T(8,128)} %collective-permute-done.5.refs_1_, f32[48,24,128]{2,1,0:T(8,128)} %get-tuple-element.34.refs_2_, ...), custom_call_target="tpu_custom_call" | custom-call | flops 1000000 | bytes 4000000 | tf_op jit(solution)/shard_map/pallas_call | solution.py:55
  61.7 0.0 copy-start.1
  61.7 21.7 %all_to_all.15.parts = f32[16,16,128]{2,1,0:T(8,128)S(1)} all-to-all(f32[16,16,128]{2,1,0:T(8,128)} %bitcast.8), channel_id=1, replica_groups={{0,1,2,3,4,5,6,7,256,257,258,259,260,261,262,263},{8,9,10,11,12,13,14,1..., dimensions={0} | all-to-all | bytes 262144 | tf_op jit(solution)/shard_map/all_to_all | solution.py:623
  83.5 20.4 %all_to_all.16.parts = f32[32,16,128]{2,1,0:T(8,128)S(1)} all-to-all(f32[32,16,128]{2,1,0:T(8,128)S(1)} %shard_map.98), channel_id=1, replica_groups={{0,8,16,24,32,40,48,56,64,72,80,88,96,104,112,120,128,136,144,152,160,1..., dimensions={0} | all-to-all | bytes 524288 | tf_op jit(solution)/shard_map/all_to_all | solution.py:625
  103.8 0.7 shard_map.99
  104.5 5.3 %all-to-all-start.2 = ((f32[16,16,128]{2,1,0:T(8,128)}), f32[16,16,128]{2,1,0:T(8,128)}, u32[]{:S(2)}, u32[]{:S(2)}) async-start(f32[16,16,128]{2,1,0:T(8,128)} %shard_map.99), calls=%async_computation.2 | async-start | bytes 262144 | tf_op jit(solution)/shard_map/all_to_all | solution.py:627
  109.8 0.0 copy-done.1
  109.8 0.2 copy.13
  110.0 0.1 rev.3
  110.1 0.8 reshape.34.refs_1_
  110.9 2.8 %shard_map.97 = bf16[16,32,128]{2,1,0:T(8,128)(2,1)} custom-call(bf16[6,160,128]{2,1,0:T(8,128)(2,1)} %get-tuple-element.38.refs_0_, bf16[16,432]{1,0:T(8,128)(2,1)} %reshape.34.refs_1_, f32[256,128]{1,0:T(8,128)} %get-tuple-element.39.refs_2_), custom_call_target="tpu_custom_call" | custom-call | flops 100000000 | bytes 4000000 | tf_op jit(solution)/shard_map/pallas_call | solution.py:55
  113.7 5.3 %all-to-all-done.2 = f32[16,16,128]{2,1,0:T(8,128)} async-done(((f32[16,16,128]{2,1,0:T(8,128)}), f32[16,16,128]{2,1,0:T(8,128)}, u32[]{:S(2)}, u32[]{:S(2)}) %all-to-all-start.2) | async-done | bytes 131104 | tf_op jit(solution)/shard_map/all_to_all | solution.py:627
  119.0 3.1 %shard_map.100 = (f32[16,432]{1,0:T(8,128)}, f32[432,432]{1,0:T(8,128)}, f32[16,16]{1,0:T(8,128)}) custom-call(f32[256,128]{1,0:T(8,128)} %bitcast.5.refs_0_), custom_call_target="tpu_custom_call" | custom-call | flops 1000000 | bytes 4000000 | tf_op jit(solution)/shard_map/pallas_call | solution.py:70
  (1 shorter events, 0.0 us)
Async XLA Ops:
  2.5 15.0 %collective-permute-start.1 = (bf16[44,16,128]{2,1,0:T(8,128)(2,1)}, bf16[44,16,128]{2,1,0:T(8,128)(2,1)}, u32[]{:S(2)}, u32[]{:S(2)}) collective-permute-start(bf16[44,16,128]{2,1,0:T(8,128)(2,1)} %get-tuple-element.26), channel_id=1, source_target_pairs={{1,0},{2,1},{3,2},{4,3},{5,4},{6,5},{7,6},{0,7},{9,8},{10,9},{11,1... | collective-permute-start | bytes 540680 | tf_op jit(solution)/shard_map/ppermute | solution.py:557
  11.3 6.2 %collective-permute-start = (bf16[40,16,128]{2,1,0:T(8,128)(2,1)}, bf16[40,16,128]{2,1,0:T(8,128)(2,1)}, u32[]{:S(2)}, u32[]{:S(2)}) collective-permute-start(bf16[40,16,128]{2,1,0:T(8,128)(2,1)} %get-tuple-element.25), channel_id=1, source_target_pairs={{0,1},{1,2},{2,3},{3,4},{4,5},{5,6},{6,7},{7,0},{8,9},{9,10},{10,1... | collective-permute-start | bytes 491528 | tf_op jit(solution)/shard_map/ppermute | solution.py:557
  19.4 18.8 %collective-permute-start.3 = (bf16[53,16,128]{2,1,0:T(8,128)(2,1)}, bf16[53,16,128]{2,1,0:T(8,128)(2,1)}, u32[]{:S(2)}, u32[]{:S(2)}) collective-permute-start(bf16[53,16,128]{2,1,0:T(8,128)(2,1)} %get-tuple-element.29), channel_id=1, source_target_pairs={{8,0},{16,8},{24,16},{32,24},{40,32},{48,40},{56,48},{64,56},{72,6... | collective-permute-start | bytes 651272 | tf_op jit(solution)/shard_map/ppermute | solution.py:557
  27.6 10.6 %collective-permute-start.2 = (bf16[40,16,128]{2,1,0:T(8,128)(2,1)}, bf16[40,16,128]{2,1,0:T(8,128)(2,1)}, u32[]{:S(2)}, u32[]{:S(2)}) collective-permute-start(bf16[40,16,128]{2,1,0:T(8,128)(2,1)} %get-tuple-element.28), channel_id=1, source_target_pairs={{0,8},{8,16},{16,24},{24,32},{32,40},{40,48},{48,56},{56,64},{64,7... | collective-permute-start | bytes 491528 | tf_op jit(solution)/shard_map/ppermute | solution.py:557
  30.3 0.6 copy-start
  43.1 13.0 %collective-permute-start.4 = (f32[10,16,128]{2,1,0:T(8,128)}, f32[10,16,128]{2,1,0:T(8,128)}, u32[]{:S(2)}, u32[]{:S(2)}) collective-permute-start(f32[10,16,128]{2,1,0:T(8,128)} %get-tuple-element.30), channel_id=1, source_target_pairs={{0,8},{8,16},{16,24},{24,32},{32,40},{40,48},{48,56},{56,64},{64,7... | collective-permute-start | bytes 245768 | tf_op jit(solution)/shard_map/ppermute | solution.py:557
  48.5 9.4 %collective-permute-start.5 = (f32[10,16,128]{2,1,0:T(8,128)}, f32[10,16,128]{2,1,0:T(8,128)}, u32[]{:S(2)}, u32[]{:S(2)}) collective-permute-start(f32[10,16,128]{2,1,0:T(8,128)} %get-tuple-element.33), channel_id=1, source_target_pairs={{8,0},{16,8},{24,16},{32,24},{40,32},{48,40},{56,48},{64,56},{72,6... | collective-permute-start | bytes 245768 | tf_op jit(solution)/shard_map/ppermute | solution.py:557
  61.7 48.1 %copy-start.1 = (bf16[16,16,27]{2,1,0:T(8,128)(2,1)S(1)}, bf16[16,16,27]{2,1,0:T(8,128)(2,1)}, u32[]{:S(2)}) copy-start(bf16[16,16,27]{2,1,0:T(8,128)(2,1)} %copy-done) | copy-start | bytes 41476
  104.5 14.5 %all-to-all-start.2 = ((f32[16,16,128]{2,1,0:T(8,128)}), f32[16,16,128]{2,1,0:T(8,128)}, u32[]{:S(2)}, u32[]{:S(2)}) async-start(f32[16,16,128]{2,1,0:T(8,128)} %shard_map.99), calls=%async_computation.2 | async-start | bytes 262144 | tf_op jit(solution)/shard_map/all_to_all | solution.py:627

commit v8 on v6

--- a/solution.py
+++ b/solution.py
@@ -493,8 +493,7 @@
     one = value.astype(BF16)
     rest = value - one.astype(F32)
     two = rest.astype(BF16)
-    three = (rest - two.astype(F32)).astype(BF16)
-    return one, two, three
+    return one, two
 
 
 def to_channel_major(value):
@@ -502,7 +501,7 @@
     j = lax.broadcasted_iota(jnp.int32, (432, 432), 1)
     place = jnp.where((i % 16) * 27 + i // 16 == j, 1.0, 0.0).astype(BF16)
     parts = [jnp.dot(v, place, preferred_element_type=F32) for v in pieces(value)]
-    return parts[2] + parts[1] + parts[0]
+    return parts[1] + parts[0]
 
 
 def total_to_all(parts, out):
@@ -564,13 +563,13 @@
     tile = (16, 128)
     own_feat, own_fields, to_next, to_prev = call(
         pack_y,
-        [((32,) + tile, BF16), ((20,) + tile, BF16), ((4 * PREV + 20,) + tile, BF16),
+        [((32,) + tile, BF16), ((20,) + tile, BF16), ((4 * NEXT + 20,) + tile, BF16),
          ((4 * NEXT + 20,) + tile, BF16)],
         [pltpu.VMEM((512, 128), F32)],
         (features.reshape(16, 32, 128), field, velocity, cotangent),
     )
     before, after = neighbours(to_next, to_prev, "gy")
-    along_z = (ROWS_IN + 3 * (UP[1] - UP[0]), ROWS_IN + 3 * (DOWN[1] - DOWN[0]) + 10)
+    along_z = (ROWS_IN + 3 * (DOWN[1] - DOWN[0]) + 10,) * 2
     to_up, to_down = pl.pallas_call(
         pack_z,
         out_shape=[jax.ShapeDtypeStruct((n,) + tile, BF16) for n in along_z],
@@ -613,15 +612,22 @@
         (mixed,),
     )
     half = nz // 2
-    line = [[(h * half + i) * ny + j for h in range(2) for j in range(ny)] for i in range(half)]
-    plane = [[(h * half + i) * ny + j for i in range(half)] for h in range(2) for j in range(ny)]
-    rows = 256 // len(line[0])
+    line = [
+        [(h * half + 2 * m + q) * ny + j for h in range(2) for q in range(2) for j in range(ny)]
+        for m in range(half // 2)
+    ]
+    plane = [
+        [(h * half + 2 * m + q) * ny + j for m in range(half // 2)]
+        for h in range(2) for q in range(2) for j in range(ny)
+    ]
+    near, far = len(line[0]), len(plane[0])
+    rows = 256 // near
     axes = ("gz", "gy")
-    parts = mixed.reshape(2 * ny, rows, 128)
+    parts = mixed.reshape(near, rows, 128)
     parts = lax.all_to_all(parts, axes, 0, 0, axis_index_groups=line)
-    (parts,) = call_small(total_to_all, [((half, rows, 128), F32)], [], (parts,))
+    (parts,) = call_small(total_to_all, [((far, rows, 128), F32)], [], (parts,))
     parts = lax.all_to_all(parts, axes, 0, 0, axis_index_groups=plane)
-    (parts,) = call_small(total_to_all, [((2 * ny, rows, 128), F32)], [], (parts,))
+    (parts,) = call_small(total_to_all, [((near, rows, 128), F32)], [], (parts,))
     parts = lax.all_to_all(parts, axes, 0, 0, axis_index_groups=line).reshape(256, 128)
     grad_weight, factor_patch, factor_grad = call_small(
         lambda *refs: finish(cells, *refs),

time: 120 us -> 114 us (0.950)
  waiting for transfers between devices: 15.8 us -> 12.4 us
  blocking collectives: 40.4 us -> 37.3 us
    ppermute x6, waiting for transfers between devices: 10.5 us -> 7.23 us  [neighbours(): return (lax.ppermute(to_next, axis, up), lax.ppermute(to_prev, axis, down))]
    all_to_all x1, blocking collectives: 19.3 us -> 16.9 us  [body(): parts = lax.all_to_all(parts, axes, 0, 0, axis_index_groups=plane)]
  transfers between devices with their start and end apart: 7 -> 7, of which waited for: 3 -> 3; matrix products, arithmetic and copies ran while one was open for 2% -> 3% of each run, Pallas kernels for 5% -> 6%
where the time goes in v8:
time: 114 us; the launch traced here: 113 us
  blocking collectives  37.3 us (33%)
  starting transfers between devices  35.7 us (31%)
  Pallas kernels  22.6 us (20%)
  waiting for transfers between devices  12.4 us (11%)
  local copies, waits for them, and re-layouts  4.33 us (4%)
    ppermute x6, starting transfers between devices, neighbours(): return (lax.ppermute(to_next, axis, up), lax.ppermute(to_prev, axis, down))  30.2 us
    all_to_all x1, blocking collectives, body(): parts = lax.all_to_all(parts, axes, 0, 0, axis_index_groups=line)  20.4 us
    pallas_call x5, Pallas kernels, call(): pl.pallas_call(run, out_shape=[jax.ShapeDtypeStruct(s, t) for s, t in out...  17 us
    all_to_all x1, blocking collectives, body(): parts = lax.all_to_all(parts, axes, 0, 0, axis_index_groups=plane)  16.9 us
    ppermute x6, waiting for transfers between devices, neighbours(): return (lax.ppermute(to_next, axis, up), lax.ppermute(to_prev, axis, down))  7.23 us
    all_to_all x1, starting transfers between devices, body(): lax.all_to_all(parts, axes, 0, 0, axis_index_groups=line).reshape(256, 128)  5.55 us
    all_to_all x1, waiting for transfers between devices, body(): lax.all_to_all(parts, axes, 0, 0, axis_index_groups=line).reshape(256, 128)  5.2 us
    pallas_call x3, Pallas kernels, call_small(): pl.pallas_call(kernel, out_shape=[jax.ShapeDtypeStruct(s, t) for s, t in...  3.86 us
  transfers between devices with their start and end apart: 7, of which 3 were waited for; matrix products, arithmetic and copies ran while one was open for 3% of the time, Pallas kernels for 6%

profile of v8, /device:TPU:1, one launch (start us, length us, event | category | flops | bytes accessed | tf_op | source)
XLA Modules:
  0.0 113.2 jit_solution(15265227830546825780)
XLA Ops:
  0.6 1.9 %shard_map.92 = (bf16[32,16,128]{2,1,0:T(8,128)(2,1)}, bf16[20,16,128]{2,1,0:T(8,128)(2,1)}, bf16[44,16,128]{2,1,0:T(8,128)(2,1)}, bf16[44,16,128]{2,1,0:T(8,128)(2,1)}) custom-call(bf16[16,32,128]{2,1,0:T(8,128)(2,1)} %bitcast.9, f32[4,8,128]{2,1,0:T(8,128)} %refs_5_.1, f32[3,4,8,128]{3,2,1,0:T(8,128)} %refs_6_.1, f32[4,8,128]{2,1,0:T(8,128)} %refs_7_.1), custom_call_target="tpu_custom_call" | custom-call | flops 1000000 | bytes 4000000 | tf_op jit(solution)/shard_map/pallas_call | solution.py:55
  2.5 7.2 %collective-permute-start = (bf16[44,16,128]{2,1,0:T(8,128)(2,1)}, bf16[44,16,128]{2,1,0:T(8,128)(2,1)}, u32[]{:S(2)}, u32[]{:S(2)}) collective-permute-start(bf16[44,16,128]{2,1,0:T(8,128)(2,1)} %get-tuple-element.23), channel_id=1, source_target_pairs={{0,1},{1,2},{2,3},{3,4},{4,5},{5,6},{6,7},{7,0},{8,9},{9,10},{10,1... | collective-permute-start | bytes 540680 | tf_op jit(solution)/shard_map/ppermute | solution.py:554
  9.8 3.5 %collective-permute-start.1 = (bf16[44,16,128]{2,1,0:T(8,128)(2,1)}, bf16[44,16,128]{2,1,0:T(8,128)(2,1)}, u32[]{:S(2)}, u32[]{:S(2)}) collective-permute-start(bf16[44,16,128]{2,1,0:T(8,128)(2,1)} %get-tuple-element.24), channel_id=1, source_target_pairs={{1,0},{2,1},{3,2},{4,3},{5,4},{6,5},{7,6},{0,7},{9,8},{10,9},{11,1... | collective-permute-start | bytes 540680 | tf_op jit(solution)/shard_map/ppermute | solution.py:554
  13.3 0.0 collective-permute-done.before.refs_1_
  13.3 6.5 %collective-permute-done.1.after.refs_2_ = bf16[44,16,128]{2,1,0:T(8,128)(2,1)} collective-permute-done((bf16[44,16,128]{2,1,0:T(8,128)(2,1)}, bf16[44,16,128]{2,1,0:T(8,128)(2,1)}, u32[]{:S(2)}, u32[]{:S(2)}) %collective-permute-start.1) | collective-permute-done | bytes 180256 | tf_op jit(solution)/shard_map/ppermute | solution.py:554
  19.8 1.8 %shard_map.93 = (bf16[53,16,128]{2,1,0:T(8,128)(2,1)}, bf16[53,16,128]{2,1,0:T(8,128)(2,1)}) custom-call(bf16[32,16,128]{2,1,0:T(8,128)(2,1)} %get-tuple-element.22.own_feat.refs_0_, bf16[20,16,128]{2,1,0:T(8,128)(2,1)} %get-tuple-element.25.own_fields, bf16[44,16,128]{2,1,0:T(8,128)(2,1)} %collective-permute-done.before.refs_1_, ...), custom_call_target="tpu_custom_call" | custom-call | tf_op jit(solution)/shard_map/pallas_call | solution.py:573
  21.6 3.1 %collective-permute-start.2 = (bf16[53,16,128]{2,1,0:T(8,128)(2,1)}, bf16[53,16,128]{2,1,0:T(8,128)(2,1)}, u32[]{:S(2)}, u32[]{:S(2)}) collective-permute-start(bf16[53,16,128]{2,1,0:T(8,128)(2,1)} %get-tuple-element.26), channel_id=1, source_target_pairs={{0,8},{8,16},{16,24},{24,32},{32,40},{40,48},{48,56},{56,64},{64,7... | collective-permute-start | bytes 651272 | tf_op jit(solution)/shard_map/ppermute | solution.py:554
  24.7 6.4 %collective-permute-start.3 = (bf16[53,16,128]{2,1,0:T(8,128)(2,1)}, bf16[53,16,128]{2,1,0:T(8,128)(2,1)}, u32[]{:S(2)}, u32[]{:S(2)}) collective-permute-start(bf16[53,16,128]{2,1,0:T(8,128)(2,1)} %get-tuple-element.27), channel_id=1, source_target_pairs={{8,0},{16,8},{24,16},{32,24},{40,32},{48,40},{56,48},{64,56},{72,6... | collective-permute-start | bytes 651272 | tf_op jit(solution)/shard_map/ppermute | solution.py:554
  31.1 0.8 reshape.32
  32.0 0.0 copy-start
  32.0 0.6 copy-done
  32.6 0.2 copy.12
  32.8 0.8 reshape.33.refs_8_
  33.6 0.0 collective-permute-done.2.refs_3_
  33.6 0.7 collective-permute-done.3.refs_4_
  34.3 4.9 %shard_map.94 = (f32[10,16,128]{2,1,0:T(8,128)}, f32[10,16,128]{2,1,0:T(8,128)}, bf16[864,1024]{1,0:T(8,128)(2,1)}, f32[4,384,128]{2,1,0:T(8,128)}, f32[48,24,128]{2,1,0:T(8,128)}) custom-call(bf16[32,16,128]{2,1,0:T(8,128)(2,1)} %get-tuple-element.22.own_feat.refs_0_, bf16[44,16,128]{2,1,0:T(8,128)(2,1)} %collective-permute-done.before.refs_1_, ...), custom_call_target="tpu_custom_call" | custom-call | flops 1000000 | bytes 4000000 | tf_op jit(solution)/shard_map/pallas_call | solution.py:55
  39.2 1.9 %collective-permute-start.4 = (f32[10,16,128]{2,1,0:T(8,128)}, f32[10,16,128]{2,1,0:T(8,128)}, u32[]{:S(2)}, u32[]{:S(2)}) collective-permute-start(f32[10,16,128]{2,1,0:T(8,128)} %get-tuple-element.28), channel_id=1, source_target_pairs={{0,8},{8,16},{16,24},{24,32},{32,40},{40,48},{48,56},{56,64},{64,7... | collective-permute-start | bytes 245768 | tf_op jit(solution)/shard_map/ppermute | solution.py:554
  41.1 8.0 %collective-permute-start.5 = (f32[10,16,128]{2,1,0:T(8,128)}, f32[10,16,128]{2,1,0:T(8,128)}, u32[]{:S(2)}, u32[]{:S(2)}) collective-permute-start(f32[10,16,128]{2,1,0:T(8,128)} %get-tuple-element.29), channel_id=1, source_target_pairs={{8,0},{16,8},{24,16},{32,24},{40,32},{48,40},{56,48},{64,56},{72,6... | collective-permute-start | bytes 245768 | tf_op jit(solution)/shard_map/ppermute | solution.py:554
  49.2 3.4 %shard_map.95.refs_5_ = f32[192,128]{1,0:T(8,128)} custom-call(bf16[864,1024]{1,0:T(8,128)(2,1)} %get-tuple-element.32.refs_0_.refs_4_), custom_call_target="tpu_custom_call" | custom-call | flops 500000000 | bytes 4000000 | tf_op jit(solution)/shard_map/pallas_call | solution.py:55
  52.6 0.0 collective-permute-done.4.refs_0_
  52.6 0.0 collective-permute-done.5.refs_1_
  52.6 3.9 %shard_map.96 = (f32[256,128]{1,0:T(8,128)}, bf16[6,160,128]{2,1,0:T(8,128)(2,1)}, f32[4,8,128]{2,1,0:T(8,128)}) custom-call(f32[10,16,128]{2,1,0:T(8,128)} %collective-permute-done.4.refs_0_, f32[10,16,128]{2,1,0:T(8,128)} %collective-permute-done.5.refs_1_, f32[48,24,128]{2,1,0:T(8,128)} %get-tuple-element.30.refs_2_, ...), custom_call_target="tpu_custom_call" | custom-call | flops 1000000 | bytes 4000000 | tf_op jit(solution)/shard_map/pallas_call | solution.py:55
  56.5 20.4 %all_to_all.15.parts = f32[32,8,128]{2,1,0:T(8,128)S(1)} all-to-all(f32[32,8,128]{2,1,0:T(8,128)} %bitcast.8), channel_id=1, replica_groups={{0,1,2,3,4,5,6,7,8,9,10,11,12,13,14,15,256,257,258,259,260,261,262,263,..., dimensions={0} | all-to-all | bytes 262144 | tf_op jit(solution)/shard_map/all_to_all | solution.py:627
  76.9 16.9 %all_to_all.16.parts = f32[16,8,128]{2,1,0:T(8,128)S(1)} all-to-all(f32[16,8,128]{2,1,0:T(8,128)S(1)} %shard_map.98), channel_id=1, replica_groups={{0,16,32,48,64,80,96,112,128,144,160,176,192,208,224,240},{1,17,33,49,6..., dimensions={0} | all-to-all | bytes 131072 | tf_op jit(solution)/shard_map/all_to_all | solution.py:629
  93.9 0.7 shard_map.99
  94.6 5.5 %all-to-all-start.2 = ((f32[32,8,128]{2,1,0:T(8,128)}), f32[32,8,128]{2,1,0:T(8,128)}, u32[]{:S(2)}, u32[]{:S(2)}) async-start(f32[32,8,128]{2,1,0:T(8,128)} %shard_map.99), calls=%async_computation.2 | async-start | bytes 262144 | tf_op jit(solution)/shard_map/all_to_all | solution.py:631
  100.1 1.0 copy.13
  101.1 0.1 rev.3
  101.2 0.8 reshape.34.refs_1_
  102.0 2.8 %shard_map.97 = bf16[16,32,128]{2,1,0:T(8,128)(2,1)} custom-call(bf16[6,160,128]{2,1,0:T(8,128)(2,1)} %get-tuple-element.34.refs_0_, bf16[16,432]{1,0:T(8,128)(2,1)} %reshape.34.refs_1_, f32[256,128]{1,0:T(8,128)} %get-tuple-element.35.refs_2_), custom_call_target="tpu_custom_call" | custom-call | flops 100000000 | bytes 4000000 | tf_op jit(solution)/shard_map/pallas_call | solution.py:55
  104.9 5.2 %all-to-all-done.2 = f32[32,8,128]{2,1,0:T(8,128)} async-done(((f32[32,8,128]{2,1,0:T(8,128)}), f32[32,8,128]{2,1,0:T(8,128)}, u32[]{:S(2)}, u32[]{:S(2)}) %all-to-all-start.2) | async-done | bytes 131104 | tf_op jit(solution)/shard_map/all_to_all | solution.py:631
  110.1 3.1 %shard_map.100 = (f32[16,432]{1,0:T(8,128)}, f32[432,432]{1,0:T(8,128)}, f32[16,16]{1,0:T(8,128)}) custom-call(f32[256,128]{1,0:T(8,128)} %bitcast.5.refs_0_), custom_call_target="tpu_custom_call" | custom-call | flops 1000000 | bytes 4000000 | tf_op jit(solution)/shard_map/pallas_call | solution.py:70
  (1 shorter events, 0.0 us)
Async XLA Ops:
  2.5 10.7 %collective-permute-start = (bf16[44,16,128]{2,1,0:T(8,128)(2,1)}, bf16[44,16,128]{2,1,0:T(8,128)(2,1)}, u32[]{:S(2)}, u32[]{:S(2)}) collective-permute-start(bf16[44,16,128]{2,1,0:T(8,128)(2,1)} %get-tuple-element.23), channel_id=1, source_target_pairs={{0,1},{1,2},{2,3},{3,4},{4,5},{5,6},{6,7},{7,0},{8,9},{9,10},{10,1... | collective-permute-start | bytes 540680 | tf_op jit(solution)/shard_map/ppermute | solution.py:554
  9.8 10.1 %collective-permute-start.1 = (bf16[44,16,128]{2,1,0:T(8,128)(2,1)}, bf16[44,16,128]{2,1,0:T(8,128)(2,1)}, u32[]{:S(2)}, u32[]{:S(2)}) collective-permute-start(bf16[44,16,128]{2,1,0:T(8,128)(2,1)} %get-tuple-element.24), channel_id=1, source_target_pairs={{1,0},{2,1},{3,2},{4,3},{5,4},{6,5},{7,6},{0,7},{9,8},{10,9},{11,1... | collective-permute-start | bytes 540680 | tf_op jit(solution)/shard_map/ppermute | solution.py:554
  21.6 12.0 %collective-permute-start.2 = (bf16[53,16,128]{2,1,0:T(8,128)(2,1)}, bf16[53,16,128]{2,1,0:T(8,128)(2,1)}, u32[]{:S(2)}, u32[]{:S(2)}) collective-permute-start(bf16[53,16,128]{2,1,0:T(8,128)(2,1)} %get-tuple-element.26), channel_id=1, source_target_pairs={{0,8},{8,16},{16,24},{24,32},{32,40},{40,48},{48,56},{56,64},{64,7... | collective-permute-start | bytes 651272 | tf_op jit(solution)/shard_map/ppermute | solution.py:554
  24.7 9.5 %collective-permute-start.3 = (bf16[53,16,128]{2,1,0:T(8,128)(2,1)}, bf16[53,16,128]{2,1,0:T(8,128)(2,1)}, u32[]{:S(2)}, u32[]{:S(2)}) collective-permute-start(bf16[53,16,128]{2,1,0:T(8,128)(2,1)} %get-tuple-element.27), channel_id=1, source_target_pairs={{8,0},{16,8},{24,16},{32,24},{40,32},{48,40},{56,48},{64,56},{72,6... | collective-permute-start | bytes 651272 | tf_op jit(solution)/shard_map/ppermute | solution.py:554
  32.0 0.6 copy-start
  39.2 13.4 %collective-permute-start.4 = (f32[10,16,128]{2,1,0:T(8,128)}, f32[10,16,128]{2,1,0:T(8,128)}, u32[]{:S(2)}, u32[]{:S(2)}) collective-permute-start(f32[10,16,128]{2,1,0:T(8,128)} %get-tuple-element.28), channel_id=1, source_target_pairs={{0,8},{8,16},{16,24},{24,32},{32,40},{40,48},{48,56},{56,64},{64,7... | collective-permute-start | bytes 245768 | tf_op jit(solution)/shard_map/ppermute | solution.py:554
  41.1 11.5 %collective-permute-start.5 = (f32[10,16,128]{2,1,0:T(8,128)}, f32[10,16,128]{2,1,0:T(8,128)}, u32[]{:S(2)}, u32[]{:S(2)}) collective-permute-start(f32[10,16,128]{2,1,0:T(8,128)} %get-tuple-element.29), channel_id=1, source_target_pairs={{8,0},{16,8},{24,16},{32,24},{40,32},{48,40},{56,48},{64,56},{72,6... | collective-permute-start | bytes 245768 | tf_op jit(solution)/shard_map/ppermute | solution.py:554
  94.6 15.5 %all-to-all-start.2 = ((f32[32,8,128]{2,1,0:T(8,128)}), f32[32,8,128]{2,1,0:T(8,128)}, u32[]{:S(2)}, u32[]{:S(2)}) async-start(f32[32,8,128]{2,1,0:T(8,128)} %shard_map.99), calls=%async_computation.2 | async-start | bytes 262144 | tf_op jit(solution)/shard_map/all_to_all | solution.py:631

commit v9 on v8

--- a/solution.py
+++ b/solution.py
@@ -613,12 +613,12 @@
     )
     half = nz // 2
     line = [
-        [(h * half + 2 * m + q) * ny + j for h in range(2) for q in range(2) for j in range(ny)]
-        for m in range(half // 2)
+        [(h * half + 4 * m + q) * ny + j for h in range(2) for q in range(4) for j in range(ny)]
+        for m in range(half // 4)
     ]
     plane = [
-        [(h * half + 2 * m + q) * ny + j for m in range(half // 2)]
-        for h in range(2) for q in range(2) for j in range(ny)
+        [(h * half + 4 * m + q) * ny + j for m in range(half // 4)]
+        for h in range(2) for q in range(4) for j in range(ny)
     ]
     near, far = len(line[0]), len(plane[0])
     rows = 256 // near

time: 114 us -> 114 us (level)
  blocking collectives: 37.3 us -> 34.6 us
  starting transfers between devices: 35.7 us -> 37.9 us
    all_to_all x1, blocking collectives: 16.9 us -> 13.2 us  [body(): parts = lax.all_to_all(parts, axes, 0, 0, axis_index_groups=plane)]
    all_to_all x1, starting transfers between devices: 5.55 us -> 7.7 us  [body(): lax.all_to_all(parts, axes, 0, 0, axis_index_groups=line).reshape(256, 128)]
where the time goes in v9:
time: 114 us; the launch traced here: 113 us
  starting transfers between devices  37.9 us (33%)
  blocking collectives  34.6 us (30%)
  Pallas kernels  22.7 us (20%)
  waiting for transfers between devices  12.8 us (11%)
  local copies, waits for them, and re-layouts  4.33 us (4%)
    ppermute x6, starting transfers between devices, neighbours(): return (lax.ppermute(to_next, axis, up), lax.ppermute(to_prev, axis, down))  30.2 us
    all_to_all x1, blocking collectives, body(): parts = lax.all_to_all(parts, axes, 0, 0, axis_index_groups=line)  21.5 us
    pallas_call x5, Pallas kernels, call(): pl.pallas_call(run, out_shape=[jax.ShapeDtypeStruct(s, t) for s, t in out...  17 us
    all_to_all x1, blocking collectives, body(): parts = lax.all_to_all(parts, axes, 0, 0, axis_index_groups=plane)  13.2 us
    all_to_all x1, starting transfers between devices, body(): lax.all_to_all(parts, axes, 0, 0, axis_index_groups=line).reshape(256, 128)  7.7 us
    ppermute x6, waiting for transfers between devices, neighbours(): return (lax.ppermute(to_next, axis, up), lax.ppermute(to_prev, axis, down))  7.23 us
    all_to_all x1, waiting for transfers between devices, body(): lax.all_to_all(parts, axes, 0, 0, axis_index_groups=line).reshape(256, 128)  5.53 us
    pallas_call x3, Pallas kernels, call_small(): pl.pallas_call(kernel, out_shape=[jax.ShapeDtypeStruct(s, t) for s, t in...  3.89 us
  transfers between devices with their start and end apart: 7, of which 3 were waited for; matrix products, arithmetic and copies ran while one was open for 3% of the time, Pallas kernels for 6%

profile of v9, /device:TPU:1, one launch (start us, length us, event | category | flops | bytes accessed | tf_op | source)
XLA Modules:
  0.0 113.0 jit_solution(9582065186041586849)
XLA Ops:
  0.6 1.9 %shard_map.92 = (bf16[32,16,128]{2,1,0:T(8,128)(2,1)}, bf16[20,16,128]{2,1,0:T(8,128)(2,1)}, bf16[44,16,128]{2,1,0:T(8,128)(2,1)}, bf16[44,16,128]{2,1,0:T(8,128)(2,1)}) custom-call(bf16[16,32,128]{2,1,0:T(8,128)(2,1)} %bitcast.9, f32[4,8,128]{2,1,0:T(8,128)} %refs_5_.1, f32[3,4,8,128]{3,2,1,0:T(8,128)} %refs_6_.1, f32[4,8,128]{2,1,0:T(8,128)} %refs_7_.1), custom_call_target="tpu_custom_call" | custom-call | flops 1000000 | bytes 4000000 | tf_op jit(solution)/shard_map/pallas_call | solution.py:55
  2.5 7.2 %collective-permute-start = (bf16[44,16,128]{2,1,0:T(8,128)(2,1)}, bf16[44,16,128]{2,1,0:T(8,128)(2,1)}, u32[]{:S(2)}, u32[]{:S(2)}) collective-permute-start(bf16[44,16,128]{2,1,0:T(8,128)(2,1)} %get-tuple-element.23), channel_id=1, source_target_pairs={{0,1},{1,2},{2,3},{3,4},{4,5},{5,6},{6,7},{7,0},{8,9},{9,10},{10,1... | collective-permute-start | bytes 540680 | tf_op jit(solution)/shard_map/ppermute | solution.py:554
  9.8 3.5 %collective-permute-start.1 = (bf16[44,16,128]{2,1,0:T(8,128)(2,1)}, bf16[44,16,128]{2,1,0:T(8,128)(2,1)}, u32[]{:S(2)}, u32[]{:S(2)}) collective-permute-start(bf16[44,16,128]{2,1,0:T(8,128)(2,1)} %get-tuple-element.24), channel_id=1, source_target_pairs={{1,0},{2,1},{3,2},{4,3},{5,4},{6,5},{7,6},{0,7},{9,8},{10,9},{11,1... | collective-permute-start | bytes 540680 | tf_op jit(solution)/shard_map/ppermute | solution.py:554
  13.3 0.0 collective-permute-done.before.refs_1_
  13.3 6.5 %collective-permute-done.1.after.refs_2_ = bf16[44,16,128]{2,1,0:T(8,128)(2,1)} collective-permute-done((bf16[44,16,128]{2,1,0:T(8,128)(2,1)}, bf16[44,16,128]{2,1,0:T(8,128)(2,1)}, u32[]{:S(2)}, u32[]{:S(2)}) %collective-permute-start.1) | collective-permute-done | bytes 180256 | tf_op jit(solution)/shard_map/ppermute | solution.py:554
  19.8 1.8 %shard_map.93 = (bf16[53,16,128]{2,1,0:T(8,128)(2,1)}, bf16[53,16,128]{2,1,0:T(8,128)(2,1)}) custom-call(bf16[32,16,128]{2,1,0:T(8,128)(2,1)} %get-tuple-element.22.own_feat.refs_0_, bf16[20,16,128]{2,1,0:T(8,128)(2,1)} %get-tuple-element.25.own_fields, bf16[44,16,128]{2,1,0:T(8,128)(2,1)} %collective-permute-done.before.refs_1_, ...), custom_call_target="tpu_custom_call" | custom-call | tf_op jit(solution)/shard_map/pallas_call | solution.py:573
  21.6 3.1 %collective-permute-start.2 = (bf16[53,16,128]{2,1,0:T(8,128)(2,1)}, bf16[53,16,128]{2,1,0:T(8,128)(2,1)}, u32[]{:S(2)}, u32[]{:S(2)}) collective-permute-start(bf16[53,16,128]{2,1,0:T(8,128)(2,1)} %get-tuple-element.26), channel_id=1, source_target_pairs={{0,8},{8,16},{16,24},{24,32},{32,40},{40,48},{48,56},{56,64},{64,7... | collective-permute-start | bytes 651272 | tf_op jit(solution)/shard_map/ppermute | solution.py:554
  24.7 6.4 %collective-permute-start.3 = (bf16[53,16,128]{2,1,0:T(8,128)(2,1)}, bf16[53,16,128]{2,1,0:T(8,128)(2,1)}, u32[]{:S(2)}, u32[]{:S(2)}) collective-permute-start(bf16[53,16,128]{2,1,0:T(8,128)(2,1)} %get-tuple-element.27), channel_id=1, source_target_pairs={{8,0},{16,8},{24,16},{32,24},{40,32},{48,40},{56,48},{64,56},{72,6... | collective-permute-start | bytes 651272 | tf_op jit(solution)/shard_map/ppermute | solution.py:554
  31.1 0.8 reshape.32
  32.0 0.0 copy-start
  32.0 0.6 copy-done
  32.6 0.2 copy.12
  32.8 0.8 reshape.33.refs_8_
  33.6 0.0 collective-permute-done.2.refs_3_
  33.6 0.7 collective-permute-done.3.refs_4_
  34.3 4.9 %shard_map.94 = (f32[10,16,128]{2,1,0:T(8,128)}, f32[10,16,128]{2,1,0:T(8,128)}, bf16[864,1024]{1,0:T(8,128)(2,1)}, f32[4,384,128]{2,1,0:T(8,128)}, f32[48,24,128]{2,1,0:T(8,128)}) custom-call(bf16[32,16,128]{2,1,0:T(8,128)(2,1)} %get-tuple-element.22.own_feat.refs_0_, bf16[44,16,128]{2,1,0:T(8,128)(2,1)} %collective-permute-done.before.refs_1_, ...), custom_call_target="tpu_custom_call" | custom-call | flops 1000000 | bytes 4000000 | tf_op jit(solution)/shard_map/pallas_call | solution.py:55
  39.2 1.9 %collective-permute-start.4 = (f32[10,16,128]{2,1,0:T(8,128)}, f32[10,16,128]{2,1,0:T(8,128)}, u32[]{:S(2)}, u32[]{:S(2)}) collective-permute-start(f32[10,16,128]{2,1,0:T(8,128)} %get-tuple-element.28), channel_id=1, source_target_pairs={{0,8},{8,16},{16,24},{24,32},{32,40},{40,48},{48,56},{56,64},{64,7... | collective-permute-start | bytes 245768 | tf_op jit(solution)/shard_map/ppermute | solution.py:554
  41.1 8.0 %collective-permute-start.5 = (f32[10,16,128]{2,1,0:T(8,128)}, f32[10,16,128]{2,1,0:T(8,128)}, u32[]{:S(2)}, u32[]{:S(2)}) collective-permute-start(f32[10,16,128]{2,1,0:T(8,128)} %get-tuple-element.29), channel_id=1, source_target_pairs={{8,0},{16,8},{24,16},{32,24},{40,32},{48,40},{56,48},{64,56},{72,6... | collective-permute-start | bytes 245768 | tf_op jit(solution)/shard_map/ppermute | solution.py:554
  49.2 3.4 %shard_map.95.refs_5_ = f32[192,128]{1,0:T(8,128)} custom-call(bf16[864,1024]{1,0:T(8,128)(2,1)} %get-tuple-element.32.refs_0_.refs_4_), custom_call_target="tpu_custom_call" | custom-call | flops 500000000 | bytes 4000000 | tf_op jit(solution)/shard_map/pallas_call | solution.py:55
  52.6 0.0 collective-permute-done.4.refs_0_
  52.6 0.0 collective-permute-done.5.refs_1_
  52.6 3.9 %shard_map.96 = (f32[256,128]{1,0:T(8,128)}, bf16[6,160,128]{2,1,0:T(8,128)(2,1)}, f32[4,8,128]{2,1,0:T(8,128)}) custom-call(f32[10,16,128]{2,1,0:T(8,128)} %collective-permute-done.4.refs_0_, f32[10,16,128]{2,1,0:T(8,128)} %collective-permute-done.5.refs_1_, f32[48,24,128]{2,1,0:T(8,128)} %get-tuple-element.30.refs_2_, ...), custom_call_target="tpu_custom_call" | custom-call | flops 1000000 | bytes 4000000 | tf_op jit(solution)/shard_map/pallas_call | solution.py:55
  56.5 21.5 %all_to_all.15.parts = f32[64,4,128]{2,1,0:T(4,128)S(1)} all-to-all(f32[64,4,128]{2,1,0:T(4,128)} %bitcast.8), channel_id=1, replica_groups={{0,1,2,3,4,5,6,7,8,9,10,11,12,13,14,15,16,17,18,19,20,21,22,23,24,25,26..., dimensions={0} | all-to-all | bytes 262144 | tf_op jit(solution)/shard_map/all_to_all | solution.py:627
  78.0 0.1 shard_map.98
  78.1 13.2 %all_to_all.16.parts = f32[8,4,128]{2,1,0:T(4,128)S(1)} all-to-all(f32[8,4,128]{2,1,0:T(4,128)S(1)} %shard_map.98), channel_id=1, replica_groups={{0,32,64,96,128,160,192,224},{1,33,65,97,129,161,193,225},{2,34,66,98,1..., dimensions={0} | all-to-all | bytes 32768 | tf_op jit(solution)/shard_map/all_to_all | solution.py:629
  91.2 0.7 shard_map.99
  91.9 7.7 %all-to-all-start.2 = ((f32[64,4,128]{2,1,0:T(4,128)}), f32[64,4,128]{2,1,0:T(4,128)}, u32[]{:S(2)}, u32[]{:S(2)}) async-start(f32[64,4,128]{2,1,0:T(4,128)} %shard_map.99), calls=%async_computation.2 | async-start | bytes 262144 | tf_op jit(solution)/shard_map/all_to_all | solution.py:631
  99.6 1.0 copy.13
  100.6 0.1 rev.3
  100.7 0.8 reshape.34.refs_1_
  101.5 2.8 %shard_map.97 = bf16[16,32,128]{2,1,0:T(8,128)(2,1)} custom-call(bf16[6,160,128]{2,1,0:T(8,128)(2,1)} %get-tuple-element.34.refs_0_, bf16[16,432]{1,0:T(8,128)(2,1)} %reshape.34.refs_1_, f32[256,128]{1,0:T(8,128)} %get-tuple-element.35.refs_2_), custom_call_target="tpu_custom_call" | custom-call | flops 100000000 | bytes 4000000 | tf_op jit(solution)/shard_map/pallas_call | solution.py:55
  104.4 5.5 %all-to-all-done.2 = f32[64,4,128]{2,1,0:T(4,128)} async-done(((f32[64,4,128]{2,1,0:T(4,128)}), f32[64,4,128]{2,1,0:T(4,128)}, u32[]{:S(2)}, u32[]{:S(2)}) %all-to-all-start.2) | async-done | bytes 131104 | tf_op jit(solution)/shard_map/all_to_all | solution.py:631
  109.9 3.1 %shard_map.100 = (f32[16,432]{1,0:T(8,128)}, f32[432,432]{1,0:T(8,128)}, f32[16,16]{1,0:T(8,128)}) custom-call(f32[256,128]{1,0:T(8,128)} %bitcast.5.refs_0_), custom_call_target="tpu_custom_call" | custom-call | flops 1000000 | bytes 4000000 | tf_op jit(solution)/shard_map/pallas_call | solution.py:70
Async XLA Ops:
  2.5 10.7 %collective-permute-start = (bf16[44,16,128]{2,1,0:T(8,128)(2,1)}, bf16[44,16,128]{2,1,0:T(8,128)(2,1)}, u32[]{:S(2)}, u32[]{:S(2)}) collective-permute-start(bf16[44,16,128]{2,1,0:T(8,128)(2,1)} %get-tuple-element.23), channel_id=1, source_target_pairs={{0,1},{1,2},{2,3},{3,4},{4,5},{5,6},{6,7},{7,0},{8,9},{9,10},{10,1... | collective-permute-start | bytes 540680 | tf_op jit(solution)/shard_map/ppermute | solution.py:554
  9.8 10.1 %collective-permute-start.1 = (bf16[44,16,128]{2,1,0:T(8,128)(2,1)}, bf16[44,16,128]{2,1,0:T(8,128)(2,1)}, u32[]{:S(2)}, u32[]{:S(2)}) collective-permute-start(bf16[44,16,128]{2,1,0:T(8,128)(2,1)} %get-tuple-element.24), channel_id=1, source_target_pairs={{1,0},{2,1},{3,2},{4,3},{5,4},{6,5},{7,6},{0,7},{9,8},{10,9},{11,1... | collective-permute-start | bytes 540680 | tf_op jit(solution)/shard_map/ppermute | solution.py:554
  21.6 12.0 %collective-permute-start.2 = (bf16[53,16,128]{2,1,0:T(8,128)(2,1)}, bf16[53,16,128]{2,1,0:T(8,128)(2,1)}, u32[]{:S(2)}, u32[]{:S(2)}) collective-permute-start(bf16[53,16,128]{2,1,0:T(8,128)(2,1)} %get-tuple-element.26), channel_id=1, source_target_pairs={{0,8},{8,16},{16,24},{24,32},{32,40},{40,48},{48,56},{56,64},{64,7... | collective-permute-start | bytes 651272 | tf_op jit(solution)/shard_map/ppermute | solution.py:554
  24.7 9.5 %collective-permute-start.3 = (bf16[53,16,128]{2,1,0:T(8,128)(2,1)}, bf16[53,16,128]{2,1,0:T(8,128)(2,1)}, u32[]{:S(2)}, u32[]{:S(2)}) collective-permute-start(bf16[53,16,128]{2,1,0:T(8,128)(2,1)} %get-tuple-element.27), channel_id=1, source_target_pairs={{8,0},{16,8},{24,16},{32,24},{40,32},{48,40},{56,48},{64,56},{72,6... | collective-permute-start | bytes 651272 | tf_op jit(solution)/shard_map/ppermute | solution.py:554
  32.0 0.6 copy-start
  39.2 13.4 %collective-permute-start.4 = (f32[10,16,128]{2,1,0:T(8,128)}, f32[10,16,128]{2,1,0:T(8,128)}, u32[]{:S(2)}, u32[]{:S(2)}) collective-permute-start(f32[10,16,128]{2,1,0:T(8,128)} %get-tuple-element.28), channel_id=1, source_target_pairs={{0,8},{8,16},{16,24},{24,32},{32,40},{40,48},{48,56},{56,64},{64,7... | collective-permute-start | bytes 245768 | tf_op jit(solution)/shard_map/ppermute | solution.py:554
  41.1 11.5 %collective-permute-start.5 = (f32[10,16,128]{2,1,0:T(8,128)}, f32[10,16,128]{2,1,0:T(8,128)}, u32[]{:S(2)}, u32[]{:S(2)}) collective-permute-start(f32[10,16,128]{2,1,0:T(8,128)} %get-tuple-element.29), channel_id=1, source_target_pairs={{8,0},{16,8},{24,16},{32,24},{40,32},{48,40},{56,48},{64,56},{72,6... | collective-permute-start | bytes 245768 | tf_op jit(solution)/shard_map/ppermute | solution.py:554
  91.9 18.0 %all-to-all-start.2 = ((f32[64,4,128]{2,1,0:T(4,128)}), f32[64,4,128]{2,1,0:T(4,128)}, u32[]{:S(2)}, u32[]{:S(2)}) async-start(f32[64,4,128]{2,1,0:T(4,128)} %shard_map.99), calls=%async_computation.2 | async-start | bytes 262144 | tf_op jit(solution)/shard_map/all_to_all | solution.py:631

commit v10 on v9

--- a/solution.py
+++ b/solution.py
@@ -129,7 +129,7 @@
         to_prev[4 * NEXT + i] = tile
 
 
-def pack_z(own_feat, own_fields, before, after, to_up, to_down, up, down, moved, left):
+def pack_z(own_feat, own_fields, before, after, _, to_up, to_down, up, down, moved, left):
     copies = []
 
     def move(source, at, out, to, count):
@@ -573,12 +573,12 @@
     to_up, to_down = pl.pallas_call(
         pack_z,
         out_shape=[jax.ShapeDtypeStruct((n,) + tile, BF16) for n in along_z],
-        in_specs=[_HBM] * 4,
+        in_specs=[_HBM] * 5,
         out_specs=[_HBM] * 2,
         scratch_shapes=[pltpu.VMEM((n,) + tile, BF16) for n in along_z]
         + [pltpu.SemaphoreType.DMA((15,)), pltpu.SemaphoreType.DMA((2,))],
         compiler_params=pltpu.CompilerParams(vmem_limit_bytes=64 * 1024 * 1024),
-    )(own_feat, own_fields, before, after)
+    )(own_feat, own_fields, before, after, w_rows)
     below, above = neighbours(to_up, to_down, "gz")
     send_up, send_down, columns_own, coef, state = call(
         stage_one,

time: 114 us -> 114 us (level)
  transfers between devices with their start and end apart: 7 -> 7, of which waited for: 3 -> 4; matrix products, arithmetic and copies ran while one was open for 3% -> 3% of each run, Pallas kernels for 6% -> 6%
where the time goes in v10:
time: 114 us; the launch traced here: 113 us
  starting transfers between devices  37.9 us (33%)
  blocking collectives  34.6 us (30%)
  Pallas kernels  22.6 us (20%)
  waiting for transfers between devices  12.8 us (11%)
  local copies, waits for them, and re-layouts  4.34 us (4%)
    ppermute x6, starting transfers between devices, neighbours(): return (lax.ppermute(to_next, axis, up), lax.ppermute(to_prev, axis, down))  30.2 us
    all_to_all x1, blocking collectives, body(): parts = lax.all_to_all(parts, axes, 0, 0, axis_index_groups=line)  21.5 us
    pallas_call x5, Pallas kernels, call(): pl.pallas_call(run, out_shape=[jax.ShapeDtypeStruct(s, t) for s, t in out...  17 us
    all_to_all x1, blocking collectives, body(): parts = lax.all_to_all(parts, axes, 0, 0, axis_index_groups=plane)  13.2 us
    all_to_all x1, starting transfers between devices, body(): lax.all_to_all(parts, axes, 0, 0, axis_index_groups=line).reshape(256, 128)  7.72 us
    ppermute x6, waiting for transfers between devices, neighbours(): return (lax.ppermute(to_next, axis, up), lax.ppermute(to_prev, axis, down))  7.23 us
    all_to_all x1, waiting for transfers between devices, body(): lax.all_to_all(parts, axes, 0, 0, axis_index_groups=line).reshape(256, 128)  5.54 us
    pallas_call x3, Pallas kernels, call_small(): pl.pallas_call(kernel, out_shape=[jax.ShapeDtypeStruct(s, t) for s, t in...  3.89 us
  transfers between devices with their start and end apart: 7, of which 4 were waited for; matrix products, arithmetic and copies ran while one was open for 3% of the time, Pallas kernels for 6%

profile of v10, /device:TPU:1, one launch (start us, length us, event | category | flops | bytes accessed | tf_op | source)
XLA Modules:
  0.0 113.1 jit_solution(18156385397987991381)
XLA Ops:
  0.6 1.9 %shard_map.92 = (bf16[32,16,128]{2,1,0:T(8,128)(2,1)}, bf16[20,16,128]{2,1,0:T(8,128)(2,1)}, bf16[44,16,128]{2,1,0:T(8,128)(2,1)}, bf16[44,16,128]{2,1,0:T(8,128)(2,1)}) custom-call(bf16[16,32,128]{2,1,0:T(8,128)(2,1)} %bitcast.9, f32[4,8,128]{2,1,0:T(8,128)} %refs_5_.1, f32[3,4,8,128]{3,2,1,0:T(8,128)} %refs_6_.1, f32[4,8,128]{2,1,0:T(8,128)} %refs_7_.1), custom_call_target="tpu_custom_call" | custom-call | flops 1000000 | bytes 4000000 | tf_op jit(solution)/shard_map/pallas_call | solution.py:55
  2.5 7.2 %collective-permute-start = (bf16[44,16,128]{2,1,0:T(8,128)(2,1)}, bf16[44,16,128]{2,1,0:T(8,128)(2,1)}, u32[]{:S(2)}, u32[]{:S(2)}) collective-permute-start(bf16[44,16,128]{2,1,0:T(8,128)(2,1)} %get-tuple-element.23), channel_id=1, source_target_pairs={{0,1},{1,2},{2,3},{3,4},{4,5},{5,6},{6,7},{7,0},{8,9},{9,10},{10,1... | collective-permute-start | bytes 540680 | tf_op jit(solution)/shard_map/ppermute | solution.py:554
  9.8 3.5 %collective-permute-start.1 = (bf16[44,16,128]{2,1,0:T(8,128)(2,1)}, bf16[44,16,128]{2,1,0:T(8,128)(2,1)}, u32[]{:S(2)}, u32[]{:S(2)}) collective-permute-start(bf16[44,16,128]{2,1,0:T(8,128)(2,1)} %get-tuple-element.24), channel_id=1, source_target_pairs={{1,0},{2,1},{3,2},{4,3},{5,4},{6,5},{7,6},{0,7},{9,8},{10,9},{11,1... | collective-permute-start | bytes 540680 | tf_op jit(solution)/shard_map/ppermute | solution.py:554
  13.3 0.8 reshape.32
  14.1 0.0 copy-start
  14.1 0.6 copy-done
  14.7 0.2 copy.12
  14.9 0.8 reshape.33._.refs_8_
  15.7 0.0 collective-permute-done.before.refs_1_
  15.7 4.1 %collective-permute-done.1.after.refs_2_ = bf16[44,16,128]{2,1,0:T(8,128)(2,1)} collective-permute-done((bf16[44,16,128]{2,1,0:T(8,128)(2,1)}, bf16[44,16,128]{2,1,0:T(8,128)(2,1)}, u32[]{:S(2)}, u32[]{:S(2)}) %collective-permute-start.1) | collective-permute-done | bytes 180256 | tf_op jit(solution)/shard_map/ppermute | solution.py:554
  19.8 1.8 %shard_map.93 = (bf16[53,16,128]{2,1,0:T(8,128)(2,1)}, bf16[53,16,128]{2,1,0:T(8,128)(2,1)}) custom-call(bf16[32,16,128]{2,1,0:T(8,128)(2,1)} %get-tuple-element.22.own_feat.refs_0_, bf16[20,16,128]{2,1,0:T(8,128)(2,1)} %get-tuple-element.25.own_fields, bf16[44,16,128]{2,1,0:T(8,128)(2,1)} %collective-permute-done.before.refs_1_, ...), custom_call_target="tpu_custom_call" | custom-call | tf_op jit(solution)/shard_map/pallas_call | solution.py:573
  21.6 3.1 %collective-permute-start.2 = (bf16[53,16,128]{2,1,0:T(8,128)(2,1)}, bf16[53,16,128]{2,1,0:T(8,128)(2,1)}, u32[]{:S(2)}, u32[]{:S(2)}) collective-permute-start(bf16[53,16,128]{2,1,0:T(8,128)(2,1)} %get-tuple-element.26), channel_id=1, source_target_pairs={{0,8},{8,16},{16,24},{24,32},{32,40},{40,48},{48,56},{56,64},{64,7... | collective-permute-start | bytes 651272 | tf_op jit(solution)/shard_map/ppermute | solution.py:554
  24.7 6.4 %collective-permute-start.3 = (bf16[53,16,128]{2,1,0:T(8,128)(2,1)}, bf16[53,16,128]{2,1,0:T(8,128)(2,1)}, u32[]{:S(2)}, u32[]{:S(2)}) collective-permute-start(bf16[53,16,128]{2,1,0:T(8,128)(2,1)} %get-tuple-element.27), channel_id=1, source_target_pairs={{8,0},{16,8},{24,16},{32,24},{40,32},{48,40},{56,48},{64,56},{72,6... | collective-permute-start | bytes 651272 | tf_op jit(solution)/shard_map/ppermute | solution.py:554
  31.1 1.6 %collective-permute-done.2.refs_3_ = bf16[53,16,128]{2,1,0:T(8,128)(2,1)} collective-permute-done((bf16[53,16,128]{2,1,0:T(8,128)(2,1)}, bf16[53,16,128]{2,1,0:T(8,128)(2,1)}, u32[]{:S(2)}, u32[]{:S(2)}) %collective-permute-start.2) | collective-permute-done | bytes 217120 | tf_op jit(solution)/shard_map/ppermute | solution.py:554
  32.8 1.5 %collective-permute-done.3.refs_4_ = bf16[53,16,128]{2,1,0:T(8,128)(2,1)} collective-permute-done((bf16[53,16,128]{2,1,0:T(8,128)(2,1)}, bf16[53,16,128]{2,1,0:T(8,128)(2,1)}, u32[]{:S(2)}, u32[]{:S(2)}) %collective-permute-start.3) | collective-permute-done | bytes 217120 | tf_op jit(solution)/shard_map/ppermute | solution.py:554
  34.2 4.9 %shard_map.94 = (f32[10,16,128]{2,1,0:T(8,128)}, f32[10,16,128]{2,1,0:T(8,128)}, bf16[864,1024]{1,0:T(8,128)(2,1)}, f32[4,384,128]{2,1,0:T(8,128)}, f32[48,24,128]{2,1,0:T(8,128)}) custom-call(bf16[32,16,128]{2,1,0:T(8,128)(2,1)} %get-tuple-element.22.own_feat.refs_0_, bf16[44,16,128]{2,1,0:T(8,128)(2,1)} %collective-permute-done.before.refs_1_, ...), custom_call_target="tpu_custom_call" | custom-call | flops 1000000 | bytes 4000000 | tf_op jit(solution)/shard_map/pallas_call | solution.py:55
  39.2 1.9 %collective-permute-start.4 = (f32[10,16,128]{2,1,0:T(8,128)}, f32[10,16,128]{2,1,0:T(8,128)}, u32[]{:S(2)}, u32[]{:S(2)}) collective-permute-start(f32[10,16,128]{2,1,0:T(8,128)} %get-tuple-element.28), channel_id=1, source_target_pairs={{0,8},{8,16},{16,24},{24,32},{32,40},{40,48},{48,56},{56,64},{64,7... | collective-permute-start | bytes 245768 | tf_op jit(solution)/shard_map/ppermute | solution.py:554
  41.1 8.0 %collective-permute-start.5 = (f32[10,16,128]{2,1,0:T(8,128)}, f32[10,16,128]{2,1,0:T(8,128)}, u32[]{:S(2)}, u32[]{:S(2)}) collective-permute-start(f32[10,16,128]{2,1,0:T(8,128)} %get-tuple-element.29), channel_id=1, source_target_pairs={{8,0},{16,8},{24,16},{32,24},{40,32},{48,40},{56,48},{64,56},{72,6... | collective-permute-start | bytes 245768 | tf_op jit(solution)/shard_map/ppermute | solution.py:554
  49.1 3.4 %shard_map.95.refs_5_ = f32[192,128]{1,0:T(8,128)} custom-call(bf16[864,1024]{1,0:T(8,128)(2,1)} %get-tuple-element.32.refs_0_.refs_4_), custom_call_target="tpu_custom_call" | custom-call | flops 500000000 | bytes 4000000 | tf_op jit(solution)/shard_map/pallas_call | solution.py:55
  52.6 0.0 collective-permute-done.4.refs_0_
  52.6 0.0 collective-permute-done.5.refs_1_
  52.6 3.9 %shard_map.96 = (f32[256,128]{1,0:T(8,128)}, bf16[6,160,128]{2,1,0:T(8,128)(2,1)}, f32[4,8,128]{2,1,0:T(8,128)}) custom-call(f32[10,16,128]{2,1,0:T(8,128)} %collective-permute-done.4.refs_0_, f32[10,16,128]{2,1,0:T(8,128)} %collective-permute-done.5.refs_1_, f32[48,24,128]{2,1,0:T(8,128)} %get-tuple-element.30.refs_2_, ...), custom_call_target="tpu_custom_call" | custom-call | flops 1000000 | bytes 4000000 | tf_op jit(solution)/shard_map/pallas_call | solution.py:55
  56.5 21.5 %all_to_all.15.parts = f32[64,4,128]{2,1,0:T(4,128)S(1)} all-to-all(f32[64,4,128]{2,1,0:T(4,128)} %bitcast.8), channel_id=1, replica_groups={{0,1,2,3,4,5,6,7,8,9,10,11,12,13,14,15,16,17,18,19,20,21,22,23,24,25,26..., dimensions={0} | all-to-all | bytes 262144 | tf_op jit(solution)/shard_map/all_to_all | solution.py:627
  78.0 0.1 shard_map.98
  78.0 13.2 %all_to_all.16.parts = f32[8,4,128]{2,1,0:T(4,128)S(1)} all-to-all(f32[8,4,128]{2,1,0:T(4,128)S(1)} %shard_map.98), channel_id=1, replica_groups={{0,32,64,96,128,160,192,224},{1,33,65,97,129,161,193,225},{2,34,66,98,1..., dimensions={0} | all-to-all | bytes 32768 | tf_op jit(solution)/shard_map/all_to_all | solution.py:629
  91.2 0.7 shard_map.99
  91.9 7.7 %all-to-all-start.2 = ((f32[64,4,128]{2,1,0:T(4,128)}), f32[64,4,128]{2,1,0:T(4,128)}, u32[]{:S(2)}, u32[]{:S(2)}) async-start(f32[64,4,128]{2,1,0:T(4,128)} %shard_map.99), calls=%async_computation.2 | async-start | bytes 262144 | tf_op jit(solution)/shard_map/all_to_all | solution.py:631
  99.6 1.0 copy.13
  100.6 0.1 rev.3
  100.8 0.8 reshape.34.refs_1_
  101.5 2.8 %shard_map.97 = bf16[16,32,128]{2,1,0:T(8,128)(2,1)} custom-call(bf16[6,160,128]{2,1,0:T(8,128)(2,1)} %get-tuple-element.34.refs_0_, bf16[16,432]{1,0:T(8,128)(2,1)} %reshape.34.refs_1_, f32[256,128]{1,0:T(8,128)} %get-tuple-element.35.refs_2_), custom_call_target="tpu_custom_call" | custom-call | flops 100000000 | bytes 4000000 | tf_op jit(solution)/shard_map/pallas_call | solution.py:55
  104.4 5.5 %all-to-all-done.2 = f32[64,4,128]{2,1,0:T(4,128)} async-done(((f32[64,4,128]{2,1,0:T(4,128)}), f32[64,4,128]{2,1,0:T(4,128)}, u32[]{:S(2)}, u32[]{:S(2)}) %all-to-all-start.2) | async-done | bytes 131104 | tf_op jit(solution)/shard_map/all_to_all | solution.py:631
  109.9 3.1 %shard_map.100 = (f32[16,432]{1,0:T(8,128)}, f32[432,432]{1,0:T(8,128)}, f32[16,16]{1,0:T(8,128)}) custom-call(f32[256,128]{1,0:T(8,128)} %bitcast.5.refs_0_), custom_call_target="tpu_custom_call" | custom-call | flops 1000000 | bytes 4000000 | tf_op jit(solution)/shard_map/pallas_call | solution.py:70
Async XLA Ops:
  2.5 13.2 %collective-permute-start = (bf16[44,16,128]{2,1,0:T(8,128)(2,1)}, bf16[44,16,128]{2,1,0:T(8,128)(2,1)}, u32[]{:S(2)}, u32[]{:S(2)}) collective-permute-start(bf16[44,16,128]{2,1,0:T(8,128)(2,1)} %get-tuple-element.23), channel_id=1, source_target_pairs={{0,1},{1,2},{2,3},{3,4},{4,5},{5,6},{6,7},{7,0},{8,9},{9,10},{10,1... | collective-permute-start | bytes 540680 | tf_op jit(solution)/shard_map/ppermute | solution.py:554
  9.8 10.1 %collective-permute-start.1 = (bf16[44,16,128]{2,1,0:T(8,128)(2,1)}, bf16[44,16,128]{2,1,0:T(8,128)(2,1)}, u32[]{:S(2)}, u32[]{:S(2)}) collective-permute-start(bf16[44,16,128]{2,1,0:T(8,128)(2,1)} %get-tuple-element.24), channel_id=1, source_target_pairs={{1,0},{2,1},{3,2},{4,3},{5,4},{6,5},{7,6},{0,7},{9,8},{10,9},{11,1... | collective-permute-start | bytes 540680 | tf_op jit(solution)/shard_map/ppermute | solution.py:554
  14.1 0.6 copy-start
  21.6 11.2 %collective-permute-start.2 = (bf16[53,16,128]{2,1,0:T(8,128)(2,1)}, bf16[53,16,128]{2,1,0:T(8,128)(2,1)}, u32[]{:S(2)}, u32[]{:S(2)}) collective-permute-start(bf16[53,16,128]{2,1,0:T(8,128)(2,1)} %get-tuple-element.26), channel_id=1, source_target_pairs={{0,8},{8,16},{16,24},{24,32},{32,40},{40,48},{48,56},{56,64},{64,7... | collective-permute-start | bytes 651272 | tf_op jit(solution)/shard_map/ppermute | solution.py:554
  24.7 9.5 %collective-permute-start.3 = (bf16[53,16,128]{2,1,0:T(8,128)(2,1)}, bf16[53,16,128]{2,1,0:T(8,128)(2,1)}, u32[]{:S(2)}, u32[]{:S(2)}) collective-permute-start(bf16[53,16,128]{2,1,0:T(8,128)(2,1)} %get-tuple-element.27), channel_id=1, source_target_pairs={{8,0},{16,8},{24,16},{32,24},{40,32},{48,40},{56,48},{64,56},{72,6... | collective-permute-start | bytes 651272 | tf_op jit(solution)/shard_map/ppermute | solution.py:554
  39.2 13.4 %collective-permute-start.4 = (f32[10,16,128]{2,1,0:T(8,128)}, f32[10,16,128]{2,1,0:T(8,128)}, u32[]{:S(2)}, u32[]{:S(2)}) collective-permute-start(f32[10,16,128]{2,1,0:T(8,128)} %get-tuple-element.28), channel_id=1, source_target_pairs={{0,8},{8,16},{16,24},{24,32},{32,40},{40,48},{48,56},{56,64},{64,7... | collective-permute-start | bytes 245768 | tf_op jit(solution)/shard_map/ppermute | solution.py:554
  41.1 11.5 %collective-permute-start.5 = (f32[10,16,128]{2,1,0:T(8,128)}, f32[10,16,128]{2,1,0:T(8,128)}, u32[]{:S(2)}, u32[]{:S(2)}) collective-permute-start(f32[10,16,128]{2,1,0:T(8,128)} %get-tuple-element.29), channel_id=1, source_target_pairs={{8,0},{16,8},{24,16},{32,24},{40,32},{48,40},{56,48},{64,56},{72,6... | collective-permute-start | bytes 245768 | tf_op jit(solution)/shard_map/ppermute | solution.py:554
  91.9 18.0 %all-to-all-start.2 = ((f32[64,4,128]{2,1,0:T(4,128)}), f32[64,4,128]{2,1,0:T(4,128)}, u32[]{:S(2)}, u32[]{:S(2)}) async-start(f32[64,4,128]{2,1,0:T(4,128)} %shard_map.99), calls=%async_computation.2 | async-start | bytes 262144 | tf_op jit(solution)/shard_map/all_to_all | solution.py:631
